TPU v7x, 32 devices: a whole 2x2x4 slice. The times are simulated.
32 devices in a mesh: ctx: 8 (over y, x, core), inner: 4 (over z).
Axes of the slice: x: 2, y: 2, z: 4, core: 2. Of those that a mesh axis runs over, the one named last changes fastest.
Arguments:
- low_rank: bfloat16 [2048, 32], P(('ctx', 'inner')), may hold values from -6 to 6
- q_base: bfloat16 [2048, 4608], P(('ctx', 'inner')), may hold values from -6 to 6
- k_base: bfloat16 [2048, 4608], P(('ctx', 'inner')), may hold values from -6 to 6
- v_base: bfloat16 [2048, 4608], P(('ctx', 'inner')), may hold values from -6 to 6
- edit_up: bfloat16 [32, 13824], replicated, may hold values from -0.5 to 0.5
- log_decay: bfloat16 [2048, 36], P(('ctx', 'inner')), may hold values from -1 to 0
- lengths: int32 [8], P('ctx'), may hold values from 128 to 256, as said below
- norm_gain: float32 [4608], replicated, may hold values from 0.5 to 1.5
Outputs:
- attended: bfloat16 [2048, 4608], P(('ctx', 'inner'))
Inputs may be any that keep to these rules, and one draw needn't show every extreme that they name: `lengths`: every segment keeps at least half of its tokens, and some segment is full.
All inputs are finite; a program needn't handle non-finite values.
Results may differ from a plain program's by a relative error of at most 0.0072.
Values may be sent and summed in bfloat16 or wider, within the bound.
No kernel may reach another device: no remote copies, remote signals or barrier semaphores. Data moves between devices by JAX's collectives and lax.ppermute only.
A program may use at most 64 MiB of HBM per device.

v0:
```python
import math

import jax
import jax.numpy as jnp
from jax import lax
from jax.sharding import PartitionSpec as P


def carried_in(value, axis, join, neutral):
    count, mine = (lax.axis_size(axis), lax.axis_index(axis))
    pieces = jax.tree.map(lambda part: lax.all_gather(part, axis), value)
    so_far = jax.tree.map(
        lambda part, zero: jnp.full_like(part, 0) + jnp.asarray(zero, part.dtype), value, neutral
    )

    def hop(position, so_far):
        longer = join(so_far, jax.tree.map(lambda part: part[position], pieces))
        return jax.tree.map(lambda new, old: jnp.where(position < mine, new, old), longer, so_far)

    return lax.fori_loop(0, count - 1, hop, so_far)


def combine(earlier, later):
    return (earlier[0] * later[0], later[0][:, None, None] * earlier[1] + later[1])


def rows_to_heads(rows):
    return lax.all_to_all(rows, "inner", split_axis=1, concat_axis=0, tiled=True)


def shards(low_rank, q_base, k_base, v_base, edit_up, log_decay, lengths, norm_gain):
    row_count = q_base.shape[0]
    full_width = q_base.shape[1]
    head_count = log_decay.shape[1]
    groups = lax.axis_size("inner")
    local_heads = head_count // groups
    head_dim = full_width // head_count
    segment_rows = row_count * groups
    tile_count = math.gcd(groups, max(1, segment_rows // 512))
    block_rows = segment_rows // tile_count
    positions = lax.axis_index("inner") * row_count + jnp.arange(row_count, dtype=jnp.int32)
    live_rows = (positions < lengths[0])[:, None]

    def edit_part(column):
        factor = edit_up[:, column * full_width : (column + 1) * full_width]
        return jnp.dot(low_rank, factor, preferred_element_type=jnp.float32)

    queries = (q_base.astype(jnp.float32) + edit_part(0)).astype(jnp.bfloat16)
    keys_all = jnp.where(live_rows, k_base.astype(jnp.float32) + edit_part(1), 0.0).astype(
        jnp.bfloat16
    )
    values_all = jnp.where(live_rows, v_base.astype(jnp.float32) + edit_part(2), 0.0).astype(
        jnp.bfloat16
    )
    key_cols, decay_cols = (
        lax.all_to_all(keys_all, "inner", split_axis=1, concat_axis=0, tiled=True),
        lax.all_to_all(log_decay, "inner", split_axis=1, concat_axis=0, tiled=True),
    )
    query_cols = rows_to_heads(queries)
    value_cols = rows_to_heads(values_all)
    key_heads = key_cols.reshape(segment_rows, local_heads, head_dim)
    value_heads = value_cols.reshape(segment_rows, local_heads, head_dim)
    decay_sum = jnp.cumsum(decay_cols.astype(jnp.float32), axis=0)
    ending = decay_sum[-1]
    scaled = (
        key_heads.astype(jnp.float32) * jnp.exp(ending[None, :] - decay_sum)[:, :, None]
    ).astype(jnp.bfloat16)
    seg_state = jnp.einsum("shd,she->hde", scaled, value_heads, preferred_element_type=jnp.float32)
    query_heads = query_cols.reshape(segment_rows, local_heads, head_dim)
    sum_heads = decay_sum.T
    order_ids = jnp.arange(block_rows, dtype=jnp.int32)
    causal = (order_ids[:, None] >= order_ids[None, :])[None]
    identity = (
        jnp.ones((local_heads,), jnp.float32),
        jnp.zeros((local_heads, head_dim, head_dim), jnp.float32),
    )
    total_decay, former = carried_in((jnp.exp(ending), seg_state), "ctx", combine, identity)
    scores = jnp.einsum("thd,shd->hts", query_heads, key_heads, preferred_element_type=jnp.float32)
    gap_log = sum_heads[:, 0:block_rows, None] - sum_heads[:, None, 0:block_rows]
    weights = jnp.where(causal, scores * jnp.exp(jnp.where(causal, gap_log, 0.0)), 0.0).astype(
        jnp.bfloat16
    )
    total = jnp.einsum("hts,shd->thd", weights, value_heads, preferred_element_type=jnp.float32)
    inter_term = jnp.exp(decay_sum)[:, :, None] * jnp.einsum(
        "thd,hde->the", query_heads, former.astype(jnp.bfloat16), preferred_element_type=jnp.float32
    )
    mixed_out = (
        (total + inter_term).astype(jnp.bfloat16).reshape(segment_rows, local_heads * head_dim)
    )
    token_out = lax.all_to_all(mixed_out, "inner", split_axis=0, concat_axis=1, tiled=True)
    token_out = jnp.where(live_rows, token_out, jnp.zeros_like(token_out))
    flat_out = token_out.astype(jnp.float32)
    inv_rms = lax.rsqrt(jnp.mean(flat_out * flat_out, axis=-1, keepdims=True) + 1e-06)
    return (flat_out * inv_rms * norm_gain[None, :]).astype(jnp.bfloat16)


def solution(mesh):
    return jax.shard_map(
        shards,
        mesh=mesh,
        in_specs=(
            P(("ctx", "inner"), None),
            P(("ctx", "inner"), None),
            P(("ctx", "inner"), None),
            P(("ctx", "inner"), None),
            P(),
            P(("ctx", "inner"), None),
            P("ctx"),
            P(),
        ),
        out_specs=P(("ctx", "inner"), None),
        check_vma=False,
    )
```

profile of v0, /device:TPU:0, one launch (start us, length us, event | category | flops | bytes accessed | tf_op | source)
XLA Modules:
  0.0 142.3 jit_solution(2472708703401330446)
XLA Ops:
  7.9 6.3 %all-to-all-start.3 = ((bf16[4,2,288]{2,1,0:T(2,128)(2,1)}), bf16[4,2,288]{2,1,0:T(2,128)(2,1)S(1)}, u32[]{:S(2)}, u32[]{:S(2)}) async-start(bf16[4,2,288]{2,1,0:T(2,128)(2,1)} %reshape.111), calls=%async_computation.3 | async-start | bytes 12288 | tf_op jit(solution)/shard_map/all_to_all | solution.py:57
  14.9 1.5 %fusion.5 = bf16[64,4608]{1,0:T(8,128)(2,1)S(1)} fusion(bf16[64,32]{0,1:T(8,128)(2,1)S(1)} %copy-done, bf16[64,4608]{1,0:T(8,128)(2,1)} %param.12, pred[64]{0:T(512)(128)(4,1)S(1)} %add_compare_fusion, bf16[32,13824]{1,0:T(8,128)(2,1)} %param.14), kind=kOutput, calls=%fused_computation.10 | convolution fusion | flops 20054016 | bytes 1478720 | tf_op jit(solution)/shard_map/dot_general | solution.py:46
  17.3 2.5 %all-to-all-done.3 = bf16[4,2,288]{2,1,0:T(2,128)(2,1)S(1)} async-done(((bf16[4,2,288]{2,1,0:T(2,128)(2,1)}), bf16[4,2,288]{2,1,0:T(2,128)(2,1)S(1)}, u32[]{:S(2)}, u32[]{:S(2)}) %all-to-all-start.3) | async-done | bytes 4640 | tf_op jit(solution)/shard_map/all_to_all | solution.py:57
  19.9 3.5 %all-to-all-start.2 = ((bf16[64,4,1152]{2,0,1:T(8,128)(2,1)}), bf16[64,4,1152]{2,0,1:T(8,128)(2,1)S(1)}, u32[]{:S(2)}, u32[]{:S(2)}) async-start(bf16[64,4,1152]{2,0,1:T(8,128)(2,1)} %bitcast.60), calls=%async_computation.2 | async-start | bytes 1179648 | tf_op jit(solution)/shard_map/all_to_all | solution.py:56
  23.3 1.3 fusion.3
  25.6 12.4 %all-to-all-done.2 = bf16[64,4,1152]{2,0,1:T(8,128)(2,1)S(1)} async-done(((bf16[64,4,1152]{2,0,1:T(8,128)(2,1)}), bf16[64,4,1152]{2,0,1:T(8,128)(2,1)S(1)}, u32[]{:S(2)}, u32[]{:S(2)}) %all-to-all-start.2) | async-done | bytes 589856 | tf_op jit(solution)/shard_map/all_to_all | solution.py:56
  38.0 3.5 %all-to-all-start = ((bf16[64,4,1152]{2,0,1:T(8,128)(2,1)}), bf16[64,4,1152]{2,0,1:T(8,128)(2,1)S(1)}, u32[]{:S(2)}, u32[]{:S(2)}) async-start(bf16[64,4,1152]{2,0,1:T(8,128)(2,1)} %bitcast.62), calls=%async_computation | async-start | bytes 1179648 | tf_op jit(solution)/shard_map/all_to_all | solution.py:28
  43.3 13.5 %all-to-all-done = bf16[64,4,1152]{2,0,1:T(8,128)(2,1)S(1)} async-done(((bf16[64,4,1152]{2,0,1:T(8,128)(2,1)}), bf16[64,4,1152]{2,0,1:T(8,128)(2,1)S(1)}, u32[]{:S(2)}, u32[]{:S(2)}) %all-to-all-start) | async-done | bytes 589856 | tf_op jit(solution)/shard_map/all_to_all | solution.py:28
  57.9 1.3 fusion.13
  59.3 1.3 fusion.4
  61.5 3.5 %all-to-all-start.1 = ((bf16[64,4,1152]{2,0,1:T(8,128)(2,1)}), bf16[64,4,1152]{2,0,1:T(8,128)(2,1)S(1)}, u32[]{:S(2)}, u32[]{:S(2)}) async-start(bf16[64,4,1152]{2,0,1:T(8,128)(2,1)} %bitcast.61), calls=%async_computation.1 | async-start | bytes 1179648 | tf_op jit(solution)/shard_map/all_to_all | solution.py:28
  65.0 8.8 %all-gather.1 = f32[8,1,9]{2,1,0:T(1,128)S(1)} all-gather(f32[1,1,9]{2,1,0:T(1,128)S(1)} %bitcast.84), channel_id=1, replica_groups=mesh['ctx'=8,'inner'=4] {'ctx'}, dimensions={0}, use_global_device_ids=true | all-gather | bytes 324 | tf_op jit(solution)/shard_map/all_gather | solution.py:11
  73.8 6.5 %all-to-all-done.1 = bf16[64,4,1152]{2,0,1:T(8,128)(2,1)S(1)} async-done(((bf16[64,4,1152]{2,0,1:T(8,128)(2,1)}), bf16[64,4,1152]{2,0,1:T(8,128)(2,1)S(1)}, u32[]{:S(2)}, u32[]{:S(2)}) %all-to-all-start.1) | async-done | bytes 589856 | tf_op jit(solution)/shard_map/all_to_all | solution.py:28
  80.3 1.3 reshape.98
  81.6 15.8 %all-gather.4.cloned.1.call-done = f32[72,128,128]{2,1,0:T(8,128)} async-done(((f32[9,128,128]{2,1,0:T(8,128)}), f32[72,128,128]{2,1,0:T(8,128)}) %all-gather.4.cloned.1.call-update) | async-done | bytes 4718608 | tf_op jit(solution)/shard_map/all_gather | solution.py:11
  97.5 8.7 %while.14 = (s32[]{:T(128)}, f32[9,128,128]{2,1,0:T(8,128)S(1)}, s32[]{:T(128)}, f32[8,9]{1,0:T(8,128)S(1)}, f32[8,9,128,128]{3,2,1,0:T(8,128)}, /*index=5*/s32[]{:T(128)}, s32[]{:T(128)}) while((s32[]{:T(128)}, f32[9,128,128]{2,1,0:T(8,128)S(1)}, s32[]{:T(128)}, f32[8,9]{1,0:T(8,128)S(1)}, f32[8,9,128,128]{3,2,1,0:T(8,128)}, ...), condition=%wide.region_3.4_spmd.clone, body=%wide.region_2.3_spmd.clone.sunk | while | flops 589828 | bytes 1769685 | solution.py:20
  98.7 1.2 fusion.31
  100.0 1.2 fusion.31
  101.2 1.2 fusion.31
  102.4 1.2 fusion.31
  104.9 1.2 fusion.31
  106.1 2.6 %fusion.7 = f32[256,9,128]{0,2,1:T(8,128)} fusion(f32[256,9]{0,1:T(8,128)S(1)} %get-tuple-element.131, f32[9,128,128]{2,1,0:T(8,128)S(1)} %get-tuple-element.99, bf16[256,9,128]{2,1,0:T(8,128)(2,1)} %reshape.98), kind=kOutput, calls=%fused_computation.16 | convolution fusion | flops 75939840 | bytes 2368512 | tf_op jit(solution)/shard_map/thd,hde->the/dot_general | solution.py:84
  108.7 2.9 %fusion.8 = bf16[256,9,128]{0,2,1:T(8,128)(2,1)S(1)} fusion(f32[256,9,128]{0,2,1:T(8,128)} %fusion.7, f32[9,256]{1,0:T(8,128)S(1)} %bitcast.79, pred[256,256]{1,0:T(8,128)(4,1)S(1)} %iota_compare_fusion, bf16[256,9,128]{2,1,0:T(8,128)(2,1)S(1)} %reshape.99, bf16[256,9,128]{2,1,0:T(8,128)(2,1)S(1)} %reshape.97, bf16[256,9,128]{2,1,0:T(8,128)(2,1)} %reshape.98), kind=kOutput, calls=%fused_computation.17 | convolution fusion | flops 305528832 | bytes 3613696 | tf_op jit(solution)/shard_map/hts,shd->thd/dot_general | solution.py:83
  113.0 20.7 %all_to_all.80 = bf16[4,64,1152]{2,1,0:T(8,128)(2,1)S(1)} all-to-all(bf16[4,64,1152]{2,1,0:T(8,128)(2,1)S(1)} %copy.65), channel_id=1, replica_groups=mesh['ctx'=8,'inner'=4] {'inner'}, dimensions={0} | all-to-all | bytes 1179648 | tf_op jit(solution)/shard_map/all_to_all | solution.py:90
  (53 shorter events, 12.4 us)
Async XLA Ops:
  6.5 8.4 %copy-start = (bf16[64,32]{0,1:T(8,128)(2,1)S(1)}, bf16[64,32]{0,1:T(8,128)(2,1)}, u32[]{:S(2)}) copy-start(bf16[64,32]{0,1:T(8,128)(2,1)} %param.10) | copy-start | bytes 12292
  7.9 11.9 %all-to-all-start.3 = ((bf16[4,2,288]{2,1,0:T(2,128)(2,1)}), bf16[4,2,288]{2,1,0:T(2,128)(2,1)S(1)}, u32[]{:S(2)}, u32[]{:S(2)}) async-start(bf16[4,2,288]{2,1,0:T(2,128)(2,1)} %reshape.111), calls=%async_computation.3 | async-start | bytes 12288 | tf_op jit(solution)/shard_map/all_to_all | solution.py:57
  16.4 6.9 %copy-start.1 = (bf16[64,4608]{1,0:T(8,128)(2,1)S(1)}, bf16[64,4608]{1,0:T(8,128)(2,1)}, u32[]{:S(2)}) copy-start(bf16[64,4608]{1,0:T(8,128)(2,1)} %param.13) | copy-start | bytes 1769476
  19.9 18.2 %all-to-all-start.2 = ((bf16[64,4,1152]{2,0,1:T(8,128)(2,1)}), bf16[64,4,1152]{2,0,1:T(8,128)(2,1)S(1)}, u32[]{:S(2)}, u32[]{:S(2)}) async-start(bf16[64,4,1152]{2,0,1:T(8,128)(2,1)} %bitcast.60), calls=%async_computation.2 | async-start | bytes 1179648 | tf_op jit(solution)/shard_map/all_to_all | solution.py:56
  38.0 18.8 %all-to-all-start = ((bf16[64,4,1152]{2,0,1:T(8,128)(2,1)}), bf16[64,4,1152]{2,0,1:T(8,128)(2,1)S(1)}, u32[]{:S(2)}, u32[]{:S(2)}) async-start(bf16[64,4,1152]{2,0,1:T(8,128)(2,1)} %bitcast.62), calls=%async_computation | async-start | bytes 1179648 | tf_op jit(solution)/shard_map/all_to_all | solution.py:28
  41.5 55.9 %all-gather.4.cloned.1.call-start = ((), (), s32[]{:S(2)}) async-start(), calls=%async_computation.5 | async-start | bytes 5308416 | tf_op jit(solution)/shard_map/all_gather | solution.py:11
  57.9 1.4 copy-start.2
  61.5 18.8 %all-to-all-start.1 = ((bf16[64,4,1152]{2,0,1:T(8,128)(2,1)}), bf16[64,4,1152]{2,0,1:T(8,128)(2,1)S(1)}, u32[]{:S(2)}, u32[]{:S(2)}) async-start(bf16[64,4,1152]{2,0,1:T(8,128)(2,1)} %bitcast.61), calls=%async_computation.1 | async-start | bytes 1179648 | tf_op jit(solution)/shard_map/all_to_all | solution.py:28
  133.7 0.7 copy-start.3
Sparse Core Ops, SparseCore 0:
  59.4 38.0 all-gather.3
where the time goes:
time: 143 us; the launch traced here: 142 us
  waiting for transfers between devices  50.9 us (36%)
  blocking collectives  29.5 us (21%)
  starting transfers between devices  16.8 us (12%)
  between operations  14.3 us (10%)
  other arithmetic  11.3 us (8%)
  matrix products  11 us (8%)
  local copies, waits for them, and re-layouts  8.41 us (6%)
    all_to_all x1, blocking collectives, shards(): lax.all_to_all(mixed_out, 'inner', split_axis=0, concat_axis=1, tiled=True)  20.7 us
    all_to_all x2, waiting for transfers between devices, rows_to_heads(): lax.all_to_all(rows, 'inner', split_axis=1, concat_axis=0, tiled=True)  20.1 us
    all_gather x1, waiting for transfers between devices, carried_in(): pieces = jax.tree.map(lambda part: lax.all_gather(part, axis), value)  15.8 us
    all_to_all x1, waiting for transfers between devices, shards(): lax.all_to_all(keys_all, 'inner', split_axis=1, concat_axis=0, tiled=True)  12.4 us
    all_gather x1, blocking collectives, carried_in(): pieces = jax.tree.map(lambda part: lax.all_gather(part, axis), value)  8.77 us
    select_n x7, other arithmetic, hop(): jnp.where(position < mine, new, old)  8.41 us
    all_to_all x2, starting transfers between devices, rows_to_heads(): lax.all_to_all(rows, 'inner', split_axis=1, concat_axis=0, tiled=True)  6.95 us
    all_to_all x1, starting transfers between devices, shards(): lax.all_to_all(log_decay, 'inner', split_axis=1, concat_axis=0, tiled=True)  6.32 us
  transfers between devices with their start and end apart: 5, of which 5 were waited for; matrix products, arithmetic and copies ran while one was open for 7% of the time, Pallas kernels for 0%

commit v1 on v0

v1 whole, which is shorter than its diff:
```python
import jax
import jax.numpy as jnp
from jax import lax
from jax.experimental import pallas as pl
from jax.experimental.pallas import tpu as pltpu
from jax.sharding import PartitionSpec as P

F32, BF16 = jnp.float32, jnp.bfloat16
LANES = 128
PAD = 16
PARTS = 2
PARAMS = pltpu.CompilerParams(vmem_limit_bytes=48 * 1024 * 1024)
SMEM = pl.BlockSpec(memory_space=pltpu.SMEM)


def dot(a, b, dims):
    return lax.dot_general(a, b, ((dims[:1], dims[1:]), ((), ())), preferred_element_type=F32)


def call(kernel, shapes, args, specs=None, scratch=()):
    whole = [pl.BlockSpec(memory_space=pltpu.VMEM)] * len(args) if specs is None else specs
    return pl.pallas_call(
        kernel,
        grid=(1,),
        out_shape=[jax.ShapeDtypeStruct(*shape) for shape in shapes],
        in_specs=whole,
        out_specs=[pl.BlockSpec(memory_space=pltpu.VMEM)] * len(shapes),
        scratch_shapes=list(scratch),
        compiler_params=PARAMS,
    )(*args)


def live_mask(len_ref, rows):
    at = lax.axis_index("inner") * rows + lax.broadcasted_iota(jnp.int32, (rows, 1), 0)
    return at < len_ref[0]


class Sizes:
    def __init__(self, q_base, log_decay):
        self.n = lax.axis_size("inner")
        self.rows, self.width = q_base.shape
        self.heads = log_decay.shape[1]
        self.local = self.heads // self.n
        self.dh = self.width // self.heads
        self.seg = self.rows * self.n
        self.steps = (lax.axis_size("ctx") - 1).bit_length()
        first = -(-self.local // PARTS)
        self.parts = []
        at = 0
        while at < self.local:
            self.parts.append((at, min(first, self.local - at)))
            at += first


def project(z, names, part, lengths, low_rank, bases, edit_up, columns, log_decay=None):
    h0, count = part
    n, rows, dh = z.n, z.rows, z.dh
    kinds = len(bases)
    height = kinds * count * rows + (PAD if log_decay is not None else 0)

    def kernel(len_ref, lr_ref, *refs):
        base_refs, up_refs = refs[:kinds], refs[kinds : 2 * kinds]
        ld_ref = refs[2 * kinds] if log_decay is not None else None
        outs = refs[-n:]
        me = lax.axis_index("inner")
        live = live_mask(len_ref, rows)
        low = lr_ref[...]
        for k in range(n):
            group = lax.rem(me + k, n)
            at = pl.multiple_of((group * z.local + h0) * dh, LANES)
            cols = pl.ds(at, count * dh)
            for kind in range(kinds):
                term = dot(low, up_refs[kind][:, cols], (1, 0))
                edited = base_refs[kind][:, cols].astype(F32) + term
                if names[kind] != "q":
                    edited = jnp.where(live, edited, 0.0)
                edited = edited.astype(BF16)
                for h in range(count):
                    top = (kind * count + h) * rows
                    outs[k][top : top + rows, :] = edited[:, h * dh : (h + 1) * dh]
            if ld_ref is not None:
                row = lax.broadcasted_iota(jnp.int32, (PAD, z.heads), 0)
                col = lax.broadcasted_iota(jnp.int32, (PAD, z.heads), 1)
                pick = jnp.where((row < z.local) & (col == row + group * z.local), 1.0, 0.0).astype(BF16)
                wide = jnp.concatenate(
                    [dot(pick, ld_ref[...], (1, 1)), jnp.zeros((PAD, LANES - rows), F32)], axis=1
                )
                outs[k][height - PAD : height, :] = wide.astype(BF16)

    vm = pl.BlockSpec(memory_space=pltpu.VMEM)
    args = [lengths, low_rank, *bases, *([edit_up] * kinds)]
    specs = [SMEM, vm, *([vm] * kinds)]
    specs += [pl.BlockSpec((edit_up.shape[0], z.width), lambda _, c=c: (0, c)) for c in columns]
    if log_decay is not None:
        args.append(log_decay)
        specs.append(vm)
    return call(kernel, [((height, dh), BF16)] * n, args, specs)


def scatter_heads(z, refs, held, first, count):
    me = lax.axis_index("inner")
    for k in range(z.n):
        chunk = lax.rem(me + (z.n - k), z.n)
        at = pl.ds(pl.multiple_of(chunk * z.rows, z.rows), z.rows)
        for h in range(count):
            top = (first + h) * z.rows
            held[h, at, :] = refs[k][top : top + z.rows, :]


def segment_states(z, part, blocks, decays=None):
    h0, count = part
    n, rows, dh, seg = z.n, z.rows, z.dh, z.seg
    first = decays is None

    def kernel(*refs):
        kv = refs[:n]
        if first:
            state, send, col_ref, row_ref, ks, vs, lds = refs[n:]
        else:
            col_ref, row_ref, state, send, ks, vs = refs[n:]
        scatter_heads(z, kv, ks, 0, count)
        scatter_heads(z, kv, vs, count, count)
        if first:
            me = lax.axis_index("inner")
            for k in range(n):
                lds[lax.rem(me + (n - k), n)] = kv[k][2 * count * rows :, :]
            t = lax.broadcasted_iota(jnp.int32, (rows, LANES), 0)
            s = lax.broadcasted_iota(jnp.int32, (rows, LANES), 1)
            tri = jnp.where(s <= t, 1.0, 0.0).astype(BF16)
            so_far = jnp.zeros((1, PAD), F32)
            for j in range(n):
                cum = dot(tri, lds[j], (1, 1)) + so_far
                so_far = cum[rows - 1 : rows, :]
                wide = jnp.concatenate([cum, jnp.zeros((rows, LANES - PAD), F32)], axis=1)
                col_ref[j * rows : (j + 1) * rows, :] = wide
            row_ref[...] = col_ref[...].T[:PAD, :]
        col = col_ref[...]
        scale = jnp.exp(col[seg - 1 : seg, :] - col)
        for h in range(count):
            scaled = (ks[h].astype(F32) * scale[:, h0 + h : h0 + h + 1]).astype(BF16)
            value = dot(scaled, vs[h], (0, 0))
            state[h * dh : (h + 1) * dh, :] = value
            send[h * dh : (h + 1) * dh, :] = value.astype(BF16)
        put_sums(send, count * dh, jnp.broadcast_to(row_ref[:, seg - 1 : seg], (PAD, LANES)))

    shapes = [((count * dh, dh), F32), ((count * dh + 2 * PAD, dh), BF16)]
    scratch = [pltpu.VMEM((count, seg, dh), BF16)] * 2
    if first:
        shapes += [((seg, LANES), F32), ((PAD, seg), F32)]
        scratch.append(pltpu.VMEM((n, PAD, LANES), BF16))
    return call(kernel, shapes, [*blocks, *(decays or ())], scratch=scratch)


def put_sums(send, at, sums):
    high = sums.astype(BF16)
    send[at : at + PAD, :] = high
    send[at + PAD : at + 2 * PAD, :] = (sums - high.astype(F32)).astype(BF16)


def get_sums(got, at):
    return got[at : at + PAD, :].astype(F32) + got[at + PAD : at + 2 * PAD, :].astype(F32)


def is_later(step):
    return lax.rem(lax.axis_index("ctx") // (1 << step), 2) == 1


def join(z, step, part, total, got, sums, carried=None):
    h0, count = part
    dh = z.dh

    def kernel(*refs):
        total_ref, got_ref, sums_ref = refs[:3]
        carried_ref = refs[3] if carried is not None else None
        new_total, new_carried, send, new_sums = refs[-4:]
        later = is_later(step)
        own = sums_ref[...] if carried is None else sums_ref[:PAD, :]
        if carried is None:
            own = jnp.broadcast_to(own[:, z.seg - 1 : z.seg], (PAD, LANES))
            before = jnp.zeros((PAD, LANES), F32)
        else:
            before = sums_ref[PAD:, :]
        other = get_sums(got_ref, count * dh)
        keep = jnp.where(later, 1.0, jnp.exp(other))
        take = jnp.where(later, jnp.exp(own), 1.0)
        carry = jnp.where(later, jnp.exp(before), 0.0)
        for h in range(count):
            at = slice(h * dh, (h + 1) * dh)
            row = slice(h0 + h, h0 + h + 1)
            theirs = got_ref[at, :].astype(F32)
            value = total_ref[at, :] * keep[row, :] + theirs * take[row, :]
            new_total[at, :] = value
            send[at, :] = value.astype(BF16)
            moved = theirs * carry[row, :]
            new_carried[at, :] = moved if carried is None else carried_ref[at, :] + moved
        put_sums(send, count * dh, own + other)
        new_sums[:PAD, :] = own + other
        new_sums[PAD:, :] = before + jnp.where(later, other, 0.0)

    shapes = [((count * dh, dh), F32)] * 2 + [((count * dh + 2 * PAD, dh), BF16), ((2 * PAD, LANES), F32)]
    args = [total, got, sums] + ([] if carried is None else [carried])
    return call(kernel, shapes, args)


def attend(z, part, kv, qs_in, col, row, carried, got, sums):
    h0, count = part
    n, rows, dh, seg = z.n, z.rows, z.dh, z.seg

    def kernel(*refs):
        kv_refs, q_refs = refs[:n], refs[n : 2 * n]
        col_ref, row_ref, carried_ref, got_ref, sums_ref = refs[2 * n : 2 * n + 5]
        outs = refs[2 * n + 5 : 3 * n + 5]
        ks, vs, qs, mixed = refs[3 * n + 5 :]
        scatter_heads(z, kv_refs, ks, 0, count)
        scatter_heads(z, kv_refs, vs, count, count)
        scatter_heads(z, q_refs, qs, 0, count)
        later = is_later(z.steps - 1)
        carry = jnp.where(later, jnp.exp(sums_ref[PAD:, :]), 0.0)
        t = lax.broadcasted_iota(jnp.int32, (seg, seg), 0)
        s = lax.broadcasted_iota(jnp.int32, (seg, seg), 1)
        causal = s <= t
        for h in range(count):
            at = slice(h * dh, (h + 1) * dh)
            former = carried_ref[at, :] + got_ref[at, :].astype(F32) * carry[h0 + h : h0 + h + 1, :]
            q = qs[h]
            d_col = col_ref[:, h0 + h : h0 + h + 1]
            scores = dot(q, ks[h], (1, 1))
            gap = jnp.where(causal, d_col - row_ref[h0 + h : h0 + h + 1, :], 0.0)
            weights = jnp.where(causal, scores * jnp.exp(gap), 0.0).astype(BF16)
            out = dot(weights, vs[h], (1, 0)) + jnp.exp(d_col) * dot(q, former.astype(BF16), (1, 0))
            mixed[:, at] = out.astype(BF16)
        me = lax.axis_index("inner")
        for k in range(n):
            chunk = lax.rem(me + k, n)
            outs[k][...] = mixed[pl.ds(pl.multiple_of(chunk * rows, rows), rows), :]

    scratch = [pltpu.VMEM((count, seg, dh), BF16)] * 3 + [pltpu.VMEM((seg, count * dh), BF16)]
    args = [*kv, *qs_in, col, row, carried, got, sums]
    return call(kernel, [((rows, count * dh), BF16)] * n, args, scratch=scratch)


def normalize(z, lengths, gain, blocks):
    n, rows, dh = z.n, z.rows, z.dh

    def kernel(len_ref, gain_ref, *refs):
        out = refs[-1]
        me = lax.axis_index("inner")
        live = live_mask(len_ref, rows)
        total = jnp.zeros((rows, 1), F32)
        for ref in refs[:-1]:
            flat = ref[...].astype(F32)
            total = total + jnp.sum(flat * flat, axis=1, keepdims=True)
        inv = lax.rsqrt(total / z.width + 1e-06)
        for p, (h0, count) in enumerate(z.parts):
            for k in range(n):
                group = lax.rem(me + (n - k), n)
                cols = pl.ds(pl.multiple_of((group * z.local + h0) * dh, LANES), count * dh)
                scaled = refs[p * n + k][...].astype(F32) * inv * gain_ref[:, cols]
                out[:, cols] = jnp.where(live, scaled, 0.0).astype(BF16)

    flat_blocks = [block for part in blocks for block in part]
    args = [lengths, gain, *flat_blocks]
    specs = [SMEM] + [pl.BlockSpec(memory_space=pltpu.VMEM)] * (len(args) - 1)
    return call(kernel, [((rows, z.width), BF16)], args, specs)[0]


def shift_blocks(z, blocks):
    n = z.n
    return [blocks[0]] + [
        lax.ppermute(blocks[k], "inner", [(i, (i + k) % n) for i in range(n)]) for k in range(1, n)
    ]


def shards(low_rank, q_base, k_base, v_base, edit_up, log_decay, lengths, norm_gain):
    z = Sizes(q_base, log_decay)
    ctx = lax.axis_size("ctx")
    kv, qs, outs = [], [], []
    for p, part in enumerate(z.parts):
        blocks = project(
            z, "kv", part, lengths, low_rank, (k_base, v_base), edit_up, (1, 2), log_decay if p == 0 else None
        )
        kv.append(shift_blocks(z, blocks))
    for part in z.parts:
        qs.append(shift_blocks(z, project(z, "q", part, lengths, low_rank, (q_base,), edit_up, (0,))))
    decays = None
    for p, part in enumerate(z.parts):
        total, send, *made = segment_states(z, part, kv[p], decays)
        decays = decays or made
        carried, sums = None, decays[1]
        for step in range(z.steps):
            hop = 1 << step
            last = step == z.steps - 1
            pairs = [(i, i ^ hop) for i in range(ctx) if not (last and i & hop)]
            got = lax.ppermute(send, "ctx", pairs)
            if not last:
                total, carried, send, sums = join(z, step, part, total, got, sums, carried)
        outs.append(shift_blocks(z, attend(z, part, kv[p], qs[p], *decays, carried, got, sums)))
    return normalize(z, lengths, norm_gain[None, :], outs)


def solution(mesh):
    rows = P(("ctx", "inner"), None)
    return jax.shard_map(
        shards,
        mesh=mesh,
        in_specs=(rows, rows, rows, rows, P(), rows, P("ctx"), P()),
        out_specs=rows,
        check_vma=False,
    )
```

time: 143 us -> 85.1 us (0.60)
  blocking collectives: 29.5 us -> 0 us
  starting transfers between devices: 16.8 us -> 35.3 us
  waiting for transfers between devices: 50.9 us -> 37.3 us
  between operations: 14.3 us -> 0.85 us
  other arithmetic: 11.3 us -> 0 us
  matrix products: 11 us -> 0 us
  Pallas kernels: 0 us -> 7.09 us
  local copies, waits for them, and re-layouts: 8.41 us -> 4.22 us
    ppermute x0 -> x24, waiting for transfers between devices: none -> 37.3 us  [the longest x18 30.4 us: shift_blocks(): lax.ppermute(blocks[k], 'inner', [(i, (i + k) % n) for i in range(n)])]
    ppermute x0 -> x24, starting transfers between devices: none -> 35.3 us  [the longest x18 27.6 us: shift_blocks(): lax.ppermute(blocks[k], 'inner', [(i, (i + k) % n) for i in range(n)])]
    all_to_all x4 -> x0, waiting for transfers between devices: 35 us -> none  [the longest x2 20.1 us: rows_to_heads(): lax.all_to_all(rows, 'inner', split_axis=1, concat_axis=0, tiled=True)]
    all_to_all x1 -> x0, blocking collectives: 20.7 us -> none  [shards(): lax.all_to_all(mixed_out, 'inner', split_axis=0, concat_axis=1, tiled=True)]
    all_to_all x4 -> x0, starting transfers between devices: 16.7 us -> none  [the longest x2 6.95 us: rows_to_heads(): lax.all_to_all(rows, 'inner', split_axis=1, concat_axis=0, tiled=True)]
    all_gather x1 -> x0, waiting for transfers between devices: 15.8 us -> none  [carried_in(): pieces = jax.tree.map(lambda part: lax.all_gather(part, axis), value)]
    dot_general x6 -> x0, matrix products: 11 us -> none  [the longest x3 4.09 us: edit_part(): return jnp.dot(low_rank, factor, preferred_element_type=jnp.float32)]
    all_gather x1 -> x0, blocking collectives: 8.77 us -> none  [carried_in(): pieces = jax.tree.map(lambda part: lax.all_gather(part, axis), value)]
  transfers between devices with their start and end apart: 5 -> 24, of which waited for: 5 -> 11; matrix products, arithmetic and copies ran while one was open for 7% -> 0% of each run, Pallas kernels for 0% -> 7%
where the time goes in v1:
time: 85.1 us; the launch traced here: 84.8 us
  waiting for transfers between devices  37.3 us (44%)
  starting transfers between devices  35.3 us (41%)
  Pallas kernels  7.09 us (8%)
  local copies, waits for them, and re-layouts  4.22 us (5%)
    ppermute x18, waiting for transfers between devices, shift_blocks(): lax.ppermute(blocks[k], 'inner', [(i, (i + k) % n) for i in range(n)])  30.4 us
    ppermute x18, starting transfers between devices, shift_blocks(): lax.ppermute(blocks[k], 'inner', [(i, (i + k) % n) for i in range(n)])  27.6 us
    ppermute x6, starting transfers between devices, shards(): got = lax.ppermute(send, 'ctx', pairs)  7.73 us
    pallas_call x13, Pallas kernels, call(): pl.pallas_call(kernel, grid=(1,), out_shape=[jax.ShapeDtypeStruct(*shape)...  7.09 us
    ppermute x6, waiting for transfers between devices, shards(): got = lax.ppermute(send, 'ctx', pairs)  6.95 us
    unnamed x16, local copies, waits for them, and re-layouts  4.21 us
  transfers between devices with their start and end apart: 24, of which 11 were waited for; matrix products, arithmetic and copies ran while one was open for 0% of the time, Pallas kernels for 7%

profile of v1, /device:TPU:0, one launch (start us, length us, event | category | flops | bytes accessed | tf_op | source)
XLA Modules:
  0.0 84.8 jit_solution(4567789899076458868)
XLA Ops:
  5.2 3.1 %collective-permute-start = (bf16[656,128]{1,0:T(8,128)(2,1)S(1)}, bf16[656,128]{1,0:T(8,128)(2,1)S(1)}, u32[]{:S(2)}, u32[]{:S(2)}) collective-permute-start(bf16[656,128]{1,0:T(8,128)(2,1)S(1)} %get-tuple-element.50), channel_id=1, source_target_pairs={{0,1},{1,2},{2,3},{3,0},{4,5},{5,6},{6,7},{7,4},{8,9},{9,10},{10,1... | collective-permute-start | bytes 503816 | tf_op jit(solution)/shard_map/ppermute | solution.py:270
  8.3 2.6 %collective-permute-start.1 = (bf16[656,128]{1,0:T(8,128)(2,1)S(1)}, bf16[656,128]{1,0:T(8,128)(2,1)S(1)}, u32[]{:S(2)}, u32[]{:S(2)}) collective-permute-start(bf16[656,128]{1,0:T(8,128)(2,1)S(1)} %get-tuple-element.51), channel_id=1, source_target_pairs={{0,2},{1,3},{2,0},{3,1},{4,6},{5,7},{6,4},{7,5},{8,10},{9,11},{10,... | collective-permute-start | bytes 503816 | tf_op jit(solution)/shard_map/ppermute | solution.py:270
  10.9 1.3 %collective-permute-start.2 = (bf16[656,128]{1,0:T(8,128)(2,1)S(1)}, bf16[656,128]{1,0:T(8,128)(2,1)S(1)}, u32[]{:S(2)}, u32[]{:S(2)}) collective-permute-start(bf16[656,128]{1,0:T(8,128)(2,1)S(1)} %get-tuple-element.52), channel_id=1, source_target_pairs={{0,3},{1,0},{2,1},{3,2},{4,7},{5,4},{6,5},{7,6},{8,11},{9,8},{10,9... | collective-permute-start | bytes 503816 | tf_op jit(solution)/shard_map/ppermute | solution.py:270
  13.6 1.9 %collective-permute-done.refs_1_ = bf16[656,128]{1,0:T(8,128)(2,1)S(1)} collective-permute-done((bf16[656,128]{1,0:T(8,128)(2,1)S(1)}, bf16[656,128]{1,0:T(8,128)(2,1)S(1)}, u32[]{:S(2)}, u32[]{:S(2)}) %collective-permute-start) | collective-permute-done | bytes 167968 | tf_op jit(solution)/shard_map/ppermute | solution.py:270
  15.6 2.5 %collective-permute-start.14 = (bf16[512,128]{1,0:T(8,128)(2,1)S(1)}, bf16[512,128]{1,0:T(8,128)(2,1)S(1)}, u32[]{:S(2)}, u32[]{:S(2)}) collective-permute-start(bf16[512,128]{1,0:T(8,128)(2,1)S(1)} %get-tuple-element.75), channel_id=1, source_target_pairs={{0,3},{1,0},{2,1},{3,2},{4,7},{5,4},{6,5},{7,6},{8,11},{9,8},{10,9... | collective-permute-start | bytes 393224 | tf_op jit(solution)/shard_map/ppermute | solution.py:270
  18.1 4.7 %collective-permute-done.1.refs_2_ = bf16[656,128]{1,0:T(8,128)(2,1)S(1)} collective-permute-done((bf16[656,128]{1,0:T(8,128)(2,1)S(1)}, bf16[656,128]{1,0:T(8,128)(2,1)S(1)}, u32[]{:S(2)}, u32[]{:S(2)}) %collective-permute-start.1) | collective-permute-done | bytes 167968 | tf_op jit(solution)/shard_map/ppermute | solution.py:270
  22.8 1.4 %collective-permute-done.2.refs_3_ = bf16[656,128]{1,0:T(8,128)(2,1)S(1)} collective-permute-done((bf16[656,128]{1,0:T(8,128)(2,1)S(1)}, bf16[656,128]{1,0:T(8,128)(2,1)S(1)}, u32[]{:S(2)}, u32[]{:S(2)}) %collective-permute-start.2) | collective-permute-done | bytes 167968 | tf_op jit(solution)/shard_map/ppermute | solution.py:270
  25.6 8.4 %collective-permute-done.13.refs_2_ = bf16[512,128]{1,0:T(8,128)(2,1)S(1)} collective-permute-done((bf16[512,128]{1,0:T(8,128)(2,1)S(1)}, bf16[512,128]{1,0:T(8,128)(2,1)S(1)}, u32[]{:S(2)}, u32[]{:S(2)}) %collective-permute-start.13) | collective-permute-done | bytes 131104 | tf_op jit(solution)/shard_map/ppermute | solution.py:270
  34.7 1.5 %collective-permute-start.7 = (bf16[672,128]{1,0:T(8,128)(2,1)S(1)}, bf16[672,128]{1,0:T(8,128)(2,1)S(1)}, u32[]{:S(2)}, u32[]{:S(2)}) collective-permute-start(bf16[672,128]{1,0:T(8,128)(2,1)S(1)} %get-tuple-element.62), channel_id=1, source_target_pairs={{0,8},{4,12},{8,0},{12,4},{16,24},{20,28},{24,16},{28,20},{1,9},{5... | collective-permute-start | bytes 516104 | tf_op jit(solution)/shard_map/ppermute | solution.py:294
  36.4 1.2 %collective-permute-start.19 = (bf16[544,128]{1,0:T(8,128)(2,1)S(1)}, bf16[544,128]{1,0:T(8,128)(2,1)S(1)}, u32[]{:S(2)}, u32[]{:S(2)}) collective-permute-start(bf16[544,128]{1,0:T(8,128)(2,1)S(1)} %get-tuple-element.83), channel_id=1, source_target_pairs={{0,8},{4,12},{8,0},{12,4},{16,24},{20,28},{24,16},{28,20},{1,9},{5... | collective-permute-start | bytes 417800 | tf_op jit(solution)/shard_map/ppermute | solution.py:294
  37.6 6.9 %collective-permute-done.19.refs_1_ = bf16[544,128]{1,0:T(8,128)(2,1)S(1)} collective-permute-done((bf16[544,128]{1,0:T(8,128)(2,1)S(1)}, bf16[544,128]{1,0:T(8,128)(2,1)S(1)}, u32[]{:S(2)}, u32[]{:S(2)}) %collective-permute-start.19) | collective-permute-done | bytes 139296 | tf_op jit(solution)/shard_map/ppermute | solution.py:294
  45.3 3.5 %collective-permute-start.20 = (bf16[544,128]{1,0:T(8,128)(2,1)S(1)}, bf16[544,128]{1,0:T(8,128)(2,1)S(1)}, u32[]{:S(2)}, u32[]{:S(2)}) collective-permute-start(bf16[544,128]{1,0:T(8,128)(2,1)S(1)} %get-tuple-element.87), channel_id=1, source_target_pairs={{0,16},{4,20},{8,24},{12,28},{1,17},{5,21},{9,25},{13,29},{2,18},{... | collective-permute-start | bytes 417800 | tf_op jit(solution)/shard_map/ppermute | solution.py:294
  49.7 1.3 %collective-permute-start.8 = (bf16[672,128]{1,0:T(8,128)(2,1)S(1)}, bf16[672,128]{1,0:T(8,128)(2,1)S(1)}, u32[]{:S(2)}, u32[]{:S(2)}) collective-permute-start(bf16[672,128]{1,0:T(8,128)(2,1)S(1)} %get-tuple-element.66), channel_id=1, source_target_pairs={{0,16},{4,20},{8,24},{12,28},{1,17},{5,21},{9,25},{13,29},{2,18},{... | collective-permute-start | bytes 516104 | tf_op jit(solution)/shard_map/ppermute | solution.py:294
  51.2 3.3 %collective-permute-start.15 = (bf16[256,128]{1,0:T(8,128)(2,1)S(1)}, bf16[256,128]{1,0:T(8,128)(2,1)S(1)}, u32[]{:S(2)}, u32[]{:S(2)}) collective-permute-start(bf16[256,128]{1,0:T(8,128)(2,1)S(1)} %get-tuple-element.77), channel_id=1, source_target_pairs={{0,1},{1,2},{2,3},{3,0},{4,5},{5,6},{6,7},{7,4},{8,9},{9,10},{10,1... | collective-permute-start | bytes 196616 | tf_op jit(solution)/shard_map/ppermute | solution.py:270
  54.6 1.6 %collective-permute-start.16 = (bf16[256,128]{1,0:T(8,128)(2,1)S(1)}, bf16[256,128]{1,0:T(8,128)(2,1)S(1)}, u32[]{:S(2)}, u32[]{:S(2)}) collective-permute-start(bf16[256,128]{1,0:T(8,128)(2,1)S(1)} %get-tuple-element.78), channel_id=1, source_target_pairs={{0,2},{1,3},{2,0},{3,1},{4,6},{5,7},{6,4},{7,5},{8,10},{9,11},{10,... | collective-permute-start | bytes 196616 | tf_op jit(solution)/shard_map/ppermute | solution.py:270
  57.3 1.3 %collective-permute-done.15.refs_5_ = bf16[256,128]{1,0:T(8,128)(2,1)S(1)} collective-permute-done((bf16[256,128]{1,0:T(8,128)(2,1)S(1)}, bf16[256,128]{1,0:T(8,128)(2,1)S(1)}, u32[]{:S(2)}, u32[]{:S(2)}) %collective-permute-start.15) | collective-permute-done | bytes 65568 | tf_op jit(solution)/shard_map/ppermute | solution.py:270
  59.5 1.6 %collective-permute-done.16.refs_6_ = bf16[256,128]{1,0:T(8,128)(2,1)S(1)} collective-permute-done((bf16[256,128]{1,0:T(8,128)(2,1)S(1)}, bf16[256,128]{1,0:T(8,128)(2,1)S(1)}, u32[]{:S(2)}, u32[]{:S(2)}) %collective-permute-start.16) | collective-permute-done | bytes 65568 | tf_op jit(solution)/shard_map/ppermute | solution.py:270
  62.1 2.0 %collective-permute-start.5 = (bf16[320,128]{1,0:T(8,128)(2,1)S(1)}, bf16[320,128]{1,0:T(8,128)(2,1)S(1)}, u32[]{:S(2)}, u32[]{:S(2)}) collective-permute-start(bf16[320,128]{1,0:T(8,128)(2,1)S(1)} %get-tuple-element.56), channel_id=1, source_target_pairs={{0,3},{1,0},{2,1},{3,2},{4,7},{5,4},{6,5},{7,6},{8,11},{9,8},{10,9... | collective-permute-start | bytes 245768 | tf_op jit(solution)/shard_map/ppermute | solution.py:270
  65.1 3.5 %collective-permute-done.4.refs_6_ = bf16[320,128]{1,0:T(8,128)(2,1)S(1)} collective-permute-done((bf16[320,128]{1,0:T(8,128)(2,1)S(1)}, bf16[320,128]{1,0:T(8,128)(2,1)S(1)}, u32[]{:S(2)}, u32[]{:S(2)}) %collective-permute-start.4) | collective-permute-done | bytes 81952 | tf_op jit(solution)/shard_map/ppermute | solution.py:270
  69.6 1.5 %collective-permute-start.9 = (bf16[64,640]{1,0:T(8,128)(2,1)S(1)}, bf16[64,640]{1,0:T(8,128)(2,1)S(1)}, u32[]{:S(2)}, u32[]{:S(2)}) collective-permute-start(bf16[64,640]{1,0:T(8,128)(2,1)S(1)} %get-tuple-element.69), channel_id=1, source_target_pairs={{0,1},{1,2},{2,3},{3,0},{4,5},{5,6},{6,7},{7,4},{8,9},{9,10},{10,1... | collective-permute-start | bytes 245768 | tf_op jit(solution)/shard_map/ppermute | solution.py:270
  72.3 1.3 %collective-permute-start.11 = (bf16[64,640]{1,0:T(8,128)(2,1)S(1)}, bf16[64,640]{1,0:T(8,128)(2,1)S(1)}, u32[]{:S(2)}, u32[]{:S(2)}) collective-permute-start(bf16[64,640]{1,0:T(8,128)(2,1)S(1)} %get-tuple-element.71), channel_id=1, source_target_pairs={{0,3},{1,0},{2,1},{3,2},{4,7},{5,4},{6,5},{7,6},{8,11},{9,8},{10,9... | collective-permute-start | bytes 245768 | tf_op jit(solution)/shard_map/ppermute | solution.py:270
  73.6 2.0 %collective-permute-start.22 = (bf16[64,512]{1,0:T(8,128)(2,1)S(1)}, bf16[64,512]{1,0:T(8,128)(2,1)S(1)}, u32[]{:S(2)}, u32[]{:S(2)}) collective-permute-start(bf16[64,512]{1,0:T(8,128)(2,1)S(1)} %get-tuple-element.91), channel_id=1, source_target_pairs={{0,2},{1,3},{2,0},{3,1},{4,6},{5,7},{6,4},{7,5},{8,10},{9,11},{10,... | collective-permute-start | bytes 196616 | tf_op jit(solution)/shard_map/ppermute | solution.py:270
  76.7 6.9 %collective-permute-done.22.refs_6_ = bf16[64,512]{1,0:T(8,128)(2,1)S(1)} collective-permute-done((bf16[64,512]{1,0:T(8,128)(2,1)S(1)}, bf16[64,512]{1,0:T(8,128)(2,1)S(1)}, u32[]{:S(2)}, u32[]{:S(2)}) %collective-permute-start.22) | collective-permute-done | bytes 65568 | tf_op jit(solution)/shard_map/ppermute | solution.py:270
  83.6 1.2 %shard_map.94 = bf16[64,4608]{1,0:T(8,128)(2,1)} custom-call(s32[1]{0:T(128)S(6)} %copy.14.len_ref, f32[1,4608]{1,0:T(1,128)S(1)} %broadcast_in_dim.3.gain_ref, bf16[64,640]{1,0:T(8,128)(2,1)S(1)} %get-tuple-element.68.refs_0_, bf16[64,640]{1,0:T(8,128)(2,1)S(1)} %collective-permute-done.9.refs_1_, bf16[64,640]{1,0:T(8,128)(2,1)S(1)} %collective-permute-done.10.refs_2_, ...), custom_call_target="tpu_custom_call" | custom-call | tf_op jit(solution)/shard_map/pallas_call | solution.py:22
  (54 shorter events, 17.2 us)
Async XLA Ops:
  5.2 10.3 %collective-permute-start = (bf16[656,128]{1,0:T(8,128)(2,1)S(1)}, bf16[656,128]{1,0:T(8,128)(2,1)S(1)}, u32[]{:S(2)}, u32[]{:S(2)}) collective-permute-start(bf16[656,128]{1,0:T(8,128)(2,1)S(1)} %get-tuple-element.50), channel_id=1, source_target_pairs={{0,1},{1,2},{2,3},{3,0},{4,5},{5,6},{6,7},{7,4},{8,9},{9,10},{10,1... | collective-permute-start | bytes 503816 | tf_op jit(solution)/shard_map/ppermute | solution.py:270
  8.3 14.5 %collective-permute-start.1 = (bf16[656,128]{1,0:T(8,128)(2,1)S(1)}, bf16[656,128]{1,0:T(8,128)(2,1)S(1)}, u32[]{:S(2)}, u32[]{:S(2)}) collective-permute-start(bf16[656,128]{1,0:T(8,128)(2,1)S(1)} %get-tuple-element.51), channel_id=1, source_target_pairs={{0,2},{1,3},{2,0},{3,1},{4,6},{5,7},{6,4},{7,5},{8,10},{9,11},{10,... | collective-permute-start | bytes 503816 | tf_op jit(solution)/shard_map/ppermute | solution.py:270
  10.9 13.3 %collective-permute-start.2 = (bf16[656,128]{1,0:T(8,128)(2,1)S(1)}, bf16[656,128]{1,0:T(8,128)(2,1)S(1)}, u32[]{:S(2)}, u32[]{:S(2)}) collective-permute-start(bf16[656,128]{1,0:T(8,128)(2,1)S(1)} %get-tuple-element.52), channel_id=1, source_target_pairs={{0,3},{1,0},{2,1},{3,2},{4,7},{5,4},{6,5},{7,6},{8,11},{9,8},{10,9... | collective-permute-start | bytes 503816 | tf_op jit(solution)/shard_map/ppermute | solution.py:270
  12.6 13.0 %collective-permute-start.12 = (bf16[512,128]{1,0:T(8,128)(2,1)S(1)}, bf16[512,128]{1,0:T(8,128)(2,1)S(1)}, u32[]{:S(2)}, u32[]{:S(2)}) collective-permute-start(bf16[512,128]{1,0:T(8,128)(2,1)S(1)} %get-tuple-element.73), channel_id=1, source_target_pairs={{0,1},{1,2},{2,3},{3,0},{4,5},{5,6},{6,7},{7,4},{8,9},{9,10},{10,1... | collective-permute-start | bytes 393224 | tf_op jit(solution)/shard_map/ppermute | solution.py:270
  13.3 20.7 %collective-permute-start.13 = (bf16[512,128]{1,0:T(8,128)(2,1)S(1)}, bf16[512,128]{1,0:T(8,128)(2,1)S(1)}, u32[]{:S(2)}, u32[]{:S(2)}) collective-permute-start(bf16[512,128]{1,0:T(8,128)(2,1)S(1)} %get-tuple-element.74), channel_id=1, source_target_pairs={{0,2},{1,3},{2,0},{3,1},{4,6},{5,7},{6,4},{7,5},{8,10},{9,11},{10,... | collective-permute-start | bytes 393224 | tf_op jit(solution)/shard_map/ppermute | solution.py:270
  15.6 18.4 %collective-permute-start.14 = (bf16[512,128]{1,0:T(8,128)(2,1)S(1)}, bf16[512,128]{1,0:T(8,128)(2,1)S(1)}, u32[]{:S(2)}, u32[]{:S(2)}) collective-permute-start(bf16[512,128]{1,0:T(8,128)(2,1)S(1)} %get-tuple-element.75), channel_id=1, source_target_pairs={{0,3},{1,0},{2,1},{3,2},{4,7},{5,4},{6,5},{7,6},{8,11},{9,8},{10,9... | collective-permute-start | bytes 393224 | tf_op jit(solution)/shard_map/ppermute | solution.py:270
  25.0 9.6 %collective-permute-start.6 = (bf16[672,128]{1,0:T(8,128)(2,1)S(1)}, bf16[672,128]{1,0:T(8,128)(2,1)S(1)}, u32[]{:S(2)}, u32[]{:S(2)}) collective-permute-start(bf16[672,128]{1,0:T(8,128)(2,1)S(1)} %get-tuple-element.60), channel_id=1, source_target_pairs={{0,4},{4,0},{8,12},{12,8},{16,20},{20,16},{24,28},{28,24},{1,5},{5... | collective-permute-start | bytes 516104 | tf_op jit(solution)/shard_map/ppermute | solution.py:294
  34.5 1.8 %collective-permute-start.18 = (bf16[544,128]{1,0:T(8,128)(2,1)S(1)}, bf16[544,128]{1,0:T(8,128)(2,1)S(1)}, u32[]{:S(2)}, u32[]{:S(2)}) collective-permute-start(bf16[544,128]{1,0:T(8,128)(2,1)S(1)} %get-tuple-element.81), channel_id=1, source_target_pairs={{0,4},{4,0},{8,12},{12,8},{16,20},{20,16},{24,28},{28,24},{1,5},{5... | collective-permute-start | bytes 417800 | tf_op jit(solution)/shard_map/ppermute | solution.py:294
  34.7 14.1 %collective-permute-start.7 = (bf16[672,128]{1,0:T(8,128)(2,1)S(1)}, bf16[672,128]{1,0:T(8,128)(2,1)S(1)}, u32[]{:S(2)}, u32[]{:S(2)}) collective-permute-start(bf16[672,128]{1,0:T(8,128)(2,1)S(1)} %get-tuple-element.62), channel_id=1, source_target_pairs={{0,8},{4,12},{8,0},{12,4},{16,24},{20,28},{24,16},{28,20},{1,9},{5... | collective-permute-start | bytes 516104 | tf_op jit(solution)/shard_map/ppermute | solution.py:294
  36.4 8.1 %collective-permute-start.19 = (bf16[544,128]{1,0:T(8,128)(2,1)S(1)}, bf16[544,128]{1,0:T(8,128)(2,1)S(1)}, u32[]{:S(2)}, u32[]{:S(2)}) collective-permute-start(bf16[544,128]{1,0:T(8,128)(2,1)S(1)} %get-tuple-element.83), channel_id=1, source_target_pairs={{0,8},{4,12},{8,0},{12,4},{16,24},{20,28},{24,16},{28,20},{1,9},{5... | collective-permute-start | bytes 417800 | tf_op jit(solution)/shard_map/ppermute | solution.py:294
  45.3 18.8 %collective-permute-start.20 = (bf16[544,128]{1,0:T(8,128)(2,1)S(1)}, bf16[544,128]{1,0:T(8,128)(2,1)S(1)}, u32[]{:S(2)}, u32[]{:S(2)}) collective-permute-start(bf16[544,128]{1,0:T(8,128)(2,1)S(1)} %get-tuple-element.87), channel_id=1, source_target_pairs={{0,16},{4,20},{8,24},{12,28},{1,17},{5,21},{9,25},{13,29},{2,18},{... | collective-permute-start | bytes 417800 | tf_op jit(solution)/shard_map/ppermute | solution.py:294
  49.7 19.1 %collective-permute-start.8 = (bf16[672,128]{1,0:T(8,128)(2,1)S(1)}, bf16[672,128]{1,0:T(8,128)(2,1)S(1)}, u32[]{:S(2)}, u32[]{:S(2)}) collective-permute-start(bf16[672,128]{1,0:T(8,128)(2,1)S(1)} %get-tuple-element.66), channel_id=1, source_target_pairs={{0,16},{4,20},{8,24},{12,28},{1,17},{5,21},{9,25},{13,29},{2,18},{... | collective-permute-start | bytes 516104 | tf_op jit(solution)/shard_map/ppermute | solution.py:294
  51.2 7.3 %collective-permute-start.15 = (bf16[256,128]{1,0:T(8,128)(2,1)S(1)}, bf16[256,128]{1,0:T(8,128)(2,1)S(1)}, u32[]{:S(2)}, u32[]{:S(2)}) collective-permute-start(bf16[256,128]{1,0:T(8,128)(2,1)S(1)} %get-tuple-element.77), channel_id=1, source_target_pairs={{0,1},{1,2},{2,3},{3,0},{4,5},{5,6},{6,7},{7,4},{8,9},{9,10},{10,1... | collective-permute-start | bytes 196616 | tf_op jit(solution)/shard_map/ppermute | solution.py:270
  54.6 6.6 %collective-permute-start.16 = (bf16[256,128]{1,0:T(8,128)(2,1)S(1)}, bf16[256,128]{1,0:T(8,128)(2,1)S(1)}, u32[]{:S(2)}, u32[]{:S(2)}) collective-permute-start(bf16[256,128]{1,0:T(8,128)(2,1)S(1)} %get-tuple-element.78), channel_id=1, source_target_pairs={{0,2},{1,3},{2,0},{3,1},{4,6},{5,7},{6,4},{7,5},{8,10},{9,11},{10,... | collective-permute-start | bytes 196616 | tf_op jit(solution)/shard_map/ppermute | solution.py:270
  56.1 5.9 %collective-permute-start.17 = (bf16[256,128]{1,0:T(8,128)(2,1)S(1)}, bf16[256,128]{1,0:T(8,128)(2,1)S(1)}, u32[]{:S(2)}, u32[]{:S(2)}) collective-permute-start(bf16[256,128]{1,0:T(8,128)(2,1)S(1)} %get-tuple-element.79), channel_id=1, source_target_pairs={{0,3},{1,0},{2,1},{3,2},{4,7},{5,4},{6,5},{7,6},{8,11},{9,8},{10,9... | collective-permute-start | bytes 196616 | tf_op jit(solution)/shard_map/ppermute | solution.py:270
  58.5 6.6 %collective-permute-start.3 = (bf16[320,128]{1,0:T(8,128)(2,1)S(1)}, bf16[320,128]{1,0:T(8,128)(2,1)S(1)}, u32[]{:S(2)}, u32[]{:S(2)}) collective-permute-start(bf16[320,128]{1,0:T(8,128)(2,1)S(1)} %get-tuple-element.54), channel_id=1, source_target_pairs={{0,1},{1,2},{2,3},{3,0},{4,5},{5,6},{6,7},{7,4},{8,9},{9,10},{10,1... | collective-permute-start | bytes 245768 | tf_op jit(solution)/shard_map/ppermute | solution.py:270
  61.1 7.5 %collective-permute-start.4 = (bf16[320,128]{1,0:T(8,128)(2,1)S(1)}, bf16[320,128]{1,0:T(8,128)(2,1)S(1)}, u32[]{:S(2)}, u32[]{:S(2)}) collective-permute-start(bf16[320,128]{1,0:T(8,128)(2,1)S(1)} %get-tuple-element.55), channel_id=1, source_target_pairs={{0,2},{1,3},{2,0},{3,1},{4,6},{5,7},{6,4},{7,5},{8,10},{9,11},{10,... | collective-permute-start | bytes 245768 | tf_op jit(solution)/shard_map/ppermute | solution.py:270
  62.1 6.7 %collective-permute-start.5 = (bf16[320,128]{1,0:T(8,128)(2,1)S(1)}, bf16[320,128]{1,0:T(8,128)(2,1)S(1)}, u32[]{:S(2)}, u32[]{:S(2)}) collective-permute-start(bf16[320,128]{1,0:T(8,128)(2,1)S(1)} %get-tuple-element.56), channel_id=1, source_target_pairs={{0,3},{1,0},{2,1},{3,2},{4,7},{5,4},{6,5},{7,6},{8,11},{9,8},{10,9... | collective-permute-start | bytes 245768 | tf_op jit(solution)/shard_map/ppermute | solution.py:270
  64.9 10.7 %collective-permute-start.21 = (bf16[64,512]{1,0:T(8,128)(2,1)S(1)}, bf16[64,512]{1,0:T(8,128)(2,1)S(1)}, u32[]{:S(2)}, u32[]{:S(2)}) collective-permute-start(bf16[64,512]{1,0:T(8,128)(2,1)S(1)} %get-tuple-element.90), channel_id=1, source_target_pairs={{0,1},{1,2},{2,3},{3,0},{4,5},{5,6},{6,7},{7,4},{8,9},{9,10},{10,1... | collective-permute-start | bytes 196616 | tf_op jit(solution)/shard_map/ppermute | solution.py:270
  69.6 13.9 %collective-permute-start.9 = (bf16[64,640]{1,0:T(8,128)(2,1)S(1)}, bf16[64,640]{1,0:T(8,128)(2,1)S(1)}, u32[]{:S(2)}, u32[]{:S(2)}) collective-permute-start(bf16[64,640]{1,0:T(8,128)(2,1)S(1)} %get-tuple-element.69), channel_id=1, source_target_pairs={{0,1},{1,2},{2,3},{3,0},{4,5},{5,6},{6,7},{7,4},{8,9},{9,10},{10,1... | collective-permute-start | bytes 245768 | tf_op jit(solution)/shard_map/ppermute | solution.py:270
  71.1 12.4 %collective-permute-start.10 = (bf16[64,640]{1,0:T(8,128)(2,1)S(1)}, bf16[64,640]{1,0:T(8,128)(2,1)S(1)}, u32[]{:S(2)}, u32[]{:S(2)}) collective-permute-start(bf16[64,640]{1,0:T(8,128)(2,1)S(1)} %get-tuple-element.70), channel_id=1, source_target_pairs={{0,2},{1,3},{2,0},{3,1},{4,6},{5,7},{6,4},{7,5},{8,10},{9,11},{10,... | collective-permute-start | bytes 245768 | tf_op jit(solution)/shard_map/ppermute | solution.py:270
  72.3 11.3 %collective-permute-start.11 = (bf16[64,640]{1,0:T(8,128)(2,1)S(1)}, bf16[64,640]{1,0:T(8,128)(2,1)S(1)}, u32[]{:S(2)}, u32[]{:S(2)}) collective-permute-start(bf16[64,640]{1,0:T(8,128)(2,1)S(1)} %get-tuple-element.71), channel_id=1, source_target_pairs={{0,3},{1,0},{2,1},{3,2},{4,7},{5,4},{6,5},{7,6},{8,11},{9,8},{10,9... | collective-permute-start | bytes 245768 | tf_op jit(solution)/shard_map/ppermute | solution.py:270
  73.6 10.0 %collective-permute-start.22 = (bf16[64,512]{1,0:T(8,128)(2,1)S(1)}, bf16[64,512]{1,0:T(8,128)(2,1)S(1)}, u32[]{:S(2)}, u32[]{:S(2)}) collective-permute-start(bf16[64,512]{1,0:T(8,128)(2,1)S(1)} %get-tuple-element.91), channel_id=1, source_target_pairs={{0,2},{1,3},{2,0},{3,1},{4,6},{5,7},{6,4},{7,5},{8,10},{9,11},{10,... | collective-permute-start | bytes 196616 | tf_op jit(solution)/shard_map/ppermute | solution.py:270
  75.6 8.0 %collective-permute-start.23 = (bf16[64,512]{1,0:T(8,128)(2,1)S(1)}, bf16[64,512]{1,0:T(8,128)(2,1)S(1)}, u32[]{:S(2)}, u32[]{:S(2)}) collective-permute-start(bf16[64,512]{1,0:T(8,128)(2,1)S(1)} %get-tuple-element.92), channel_id=1, source_target_pairs={{0,3},{1,0},{2,1},{3,2},{4,7},{5,4},{6,5},{7,6},{8,11},{9,8},{10,9... | collective-permute-start | bytes 196616 | tf_op jit(solution)/shard_map/ppermute | solution.py:270
  (7 other events, 32.4 us)

commit v2 on v1

v2 whole, which is shorter than its diff:
```python
import jax
import jax.numpy as jnp
from jax import lax
from jax.experimental import pallas as pl
from jax.experimental.pallas import tpu as pltpu
from jax.sharding import PartitionSpec as P

F32, BF16 = jnp.float32, jnp.bfloat16
LANES = 128
PAD = 16
PARTS = 2
PARAMS = pltpu.CompilerParams(vmem_limit_bytes=48 * 1024 * 1024)
COST = pl.CostEstimate(flops=1_000_000_000, bytes_accessed=1, transcendentals=0)
SMEM = pl.BlockSpec(memory_space=pltpu.SMEM)


def dot(a, b, dims):
    return lax.dot_general(a, b, ((dims[:1], dims[1:]), ((), ())), preferred_element_type=F32)


def call(kernel, shapes, args, specs=None, scratch=(), after=()):
    whole = [pl.BlockSpec(memory_space=pltpu.VMEM)] * len(args) if specs is None else specs
    if after:
        inner, used = kernel, len(args)

        def kernel(*refs):
            inner(*refs[:used], *refs[used + len(after) :])

        args = [*args, *after]
        whole = [*whole, *([pl.BlockSpec(memory_space=pl.ANY)] * len(after))]
    return pl.pallas_call(
        kernel,
        out_shape=[jax.ShapeDtypeStruct(*shape) for shape in shapes],
        in_specs=whole,
        out_specs=[pl.BlockSpec(memory_space=pltpu.VMEM)] * len(shapes),
        scratch_shapes=list(scratch),
        compiler_params=PARAMS,
        cost_estimate=COST,
    )(*args)


def gate(arrays, after):
    every = pl.BlockSpec(memory_space=pl.ANY)
    return pl.pallas_call(
        lambda *refs: None,
        out_shape=[jax.ShapeDtypeStruct(a.shape, a.dtype) for a in arrays],
        in_specs=[every] * (len(arrays) + len(after)),
        out_specs=[every] * len(arrays),
        input_output_aliases={i: i for i in range(len(arrays))},
        compiler_params=PARAMS,
    )(*arrays, *after)


def live_mask(len_ref, rows):
    at = lax.axis_index("inner") * rows + lax.broadcasted_iota(jnp.int32, (rows, 1), 0)
    return at < len_ref[0]


class Sizes:
    def __init__(self, q_base, log_decay):
        self.n = lax.axis_size("inner")
        self.rows, self.width = q_base.shape
        self.heads = log_decay.shape[1]
        self.local = self.heads // self.n
        self.dh = self.width // self.heads
        self.seg = self.rows * self.n
        bits = (lax.axis_size("ctx") - 1).bit_length()
        self.steps = [(at, 1) for at in range(bits)]
        first = -(-self.local // PARTS)
        self.parts = []
        at = 0
        while at < self.local:
            self.parts.append((at, min(first, self.local - at)))
            at += first


def project(z, names, part, lengths, low_rank, bases, edit_up, columns, log_decay, decays, after=()):
    h0, count = part
    n, rows, dh = z.n, z.rows, z.dh
    kinds = len(bases)
    rank = edit_up.shape[0]
    height = kinds * count * rows + (PAD if decays else 0)

    def kernel(len_ref, lr_ref, *refs):
        base_refs, up_ref, ld_from = refs[:kinds], refs[kinds], refs[kinds + 1]
        outs = refs[-n - 5 : -5]
        base_buf, up_buf, low_buf, ld_ref, sems = refs[-5:]
        me = lax.axis_index("inner")

        def copies(k):
            at = (lax.rem(me + k, n) * z.local + h0) * dh
            for kind in range(kinds):
                cols = pl.ds(pl.multiple_of(at, LANES), count * dh)
                up_cols = pl.ds(pl.multiple_of(at + columns[kind] * z.width, LANES), count * dh)
                slot = k * kinds + kind
                yield pltpu.make_async_copy(base_refs[kind].at[:, cols], base_buf.at[slot], sems.at[0, slot])
                yield pltpu.make_async_copy(up_ref.at[:, up_cols], up_buf.at[slot], sems.at[1, slot])

        small = [
            pltpu.make_async_copy(lr_ref, low_buf, sems.at[0, n * kinds]),
            pltpu.make_async_copy(ld_from, ld_ref, sems.at[1, n * kinds]),
        ]
        order = [*range(1, n), 0]
        for copy in small:
            copy.start()
        for k in order:
            for copy in copies(k):
                copy.start()
        live = live_mask(len_ref, rows)
        for copy in small:
            copy.wait()
        low = low_buf[...].T
        for k in order:
            for copy in copies(k):
                copy.wait()
            for kind in range(kinds):
                slot = k * kinds + kind
                edited = base_buf[slot].astype(F32) + dot(low, up_buf[slot], (1, 0))
                if names[kind] != "q":
                    edited = jnp.where(live, edited, 0.0)
                edited = edited.astype(BF16)
                for h in range(count):
                    top = (kind * count + h) * rows
                    outs[k][top : top + rows, :] = edited[:, h * dh : (h + 1) * dh]
            if decays:
                row = lax.broadcasted_iota(jnp.int32, (PAD, z.heads), 0)
                col = lax.broadcasted_iota(jnp.int32, (PAD, z.heads), 1)
                group = lax.rem(me + k, n)
                pick = jnp.where((row < z.local) & (col == row + group * z.local), 1.0, 0.0).astype(BF16)
                wide = jnp.concatenate(
                    [dot(pick, ld_ref[...], (1, 0)), jnp.zeros((PAD, LANES - rows), F32)], axis=1
                )
                outs[k][height - PAD : height, :] = wide.astype(BF16)

    args = [lengths, *(pltpu.with_memory_space_constraint(a, pltpu.HBM) for a in (low_rank, *bases, edit_up, log_decay))]
    specs = [SMEM, *([pl.BlockSpec(memory_space=pltpu.HBM)] * (kinds + 3))]
    scratch = [
        pltpu.VMEM((n * kinds, rows, count * dh), BF16),
        pltpu.VMEM((n * kinds, rank, count * dh), BF16),
        pltpu.VMEM(low_rank.shape, BF16),
        pltpu.VMEM(log_decay.shape, BF16),
        pltpu.SemaphoreType.DMA((2, n * kinds + 1)),
    ]
    return call(kernel, [((height, dh), BF16)] * n, args, specs, scratch, after)


def scatter_heads(z, refs, held, first, count):
    me = lax.axis_index("inner")
    for k in range(z.n):
        chunk = lax.rem(me + (z.n - k), z.n)
        at = pl.ds(pl.multiple_of(chunk * z.rows, z.rows), z.rows)
        for h in range(count):
            top = (first + h) * z.rows
            held[h, at, :] = refs[k][top : top + z.rows, :]


def segment_states(z, kv):
    n, rows, dh, seg, heads = z.n, z.rows, z.dh, z.seg, z.local

    def kernel(*refs):
        kv_refs = refs[:n]
        col_ref, row_ref = refs[n : n + 2]
        results = refs[n + 2 : n + 2 + 2 * len(z.parts)]
        ks, vs, lds = refs[-3:]
        me = lax.axis_index("inner")
        for k in range(n):
            lds[lax.rem(me + (n - k), n)] = kv_refs[k][2 * heads * rows :, :]
        t = lax.broadcasted_iota(jnp.int32, (rows, LANES), 0)
        s = lax.broadcasted_iota(jnp.int32, (rows, LANES), 1)
        tri = jnp.where(s <= t, 1.0, 0.0).astype(BF16)
        so_far = jnp.zeros((1, PAD), F32)
        for j in range(n):
            cum = dot(tri, lds[j], (1, 1)) + so_far
            so_far = cum[rows - 1 : rows, :]
            wide = jnp.concatenate([cum, jnp.zeros((rows, LANES - PAD), F32)], axis=1)
            col_ref[j * rows : (j + 1) * rows, :] = wide
        row_ref[...] = col_ref[...].T[:PAD, :]
        scatter_heads(z, kv_refs, ks, 0, heads)
        scatter_heads(z, kv_refs, vs, heads, heads)
        col = col_ref[...]
        scale = jnp.exp(col[seg - 1 : seg, :] - col)
        ending = jnp.broadcast_to(row_ref[:, seg - 1 : seg], (PAD, LANES))
        for p, (h0, count) in enumerate(z.parts):
            state, send = results[2 * p : 2 * p + 2]
            for h in range(count):
                scaled = (ks[h0 + h].astype(F32) * scale[:, h0 + h : h0 + h + 1]).astype(BF16)
                value = dot(scaled, vs[h0 + h], (0, 0))
                state[h * dh : (h + 1) * dh, :] = value
                send[h * dh : (h + 1) * dh, :] = value.astype(BF16)
            put_sums(send, count * dh, ending)

    shapes = [((seg, LANES), F32), ((PAD, seg), F32)]
    for _, count in z.parts:
        shapes += [((count * dh, dh), F32), ((count * dh + 2 * PAD, dh), BF16)]
    scratch = [pltpu.VMEM((heads, seg, dh), BF16)] * 2 + [pltpu.VMEM((n, PAD, LANES), BF16)]
    return call(kernel, shapes, kv, scratch=scratch)


def put_sums(send, at, sums):
    high = sums.astype(BF16)
    send[at : at + PAD, :] = high
    send[at + PAD : at + 2 * PAD, :] = (sums - high.astype(F32)).astype(BF16)


def get_sums(got, at):
    return got[at : at + PAD, :].astype(F32) + got[at + PAD : at + 2 * PAD, :].astype(F32)


def digit_of(step):
    shift, width = step
    return lax.rem(lax.axis_index("ctx") // (1 << shift), 1 << width)


def exchange(step, last, send):
    shift, width = step
    size, mask = lax.axis_size("ctx"), (1 << width) - 1

    def needed(source, m):
        mine = (source >> shift) & mask
        return not last or mine < mine ^ m

    return [
        lax.ppermute(send, "ctx", [(i, i ^ (m << shift)) for i in range(size) if needed(i, m)])
        for m in range(1, mask + 1)
    ]


def weights_of(step, others):
    mine = digit_of(step)
    at = [mine ^ (m + 1) for m in range(len(others))]
    zero = jnp.zeros_like(others[0])
    before = []
    for a in at:
        between = zero
        for b, other in zip(at, others):
            between = between + jnp.where((a < b) & (b < mine), other, 0.0)
        before.append(jnp.where(a < mine, jnp.exp(between), 0.0))
    return mine, at, before


def join(z, step, part, total, got, sums, carried=None):
    h0, count = part
    dh, parts = z.dh, len(got)

    def kernel(*refs):
        total_ref, sums_ref = refs[:2]
        got_refs = refs[2 : 2 + parts]
        carried_ref = refs[2 + parts] if carried is not None else None
        new_total, new_carried, send, new_sums = refs[-4:]
        if carried is None:
            own = jnp.broadcast_to(sums_ref[:, z.seg - 1 : z.seg], (PAD, LANES))
            ahead = jnp.zeros((PAD, LANES), F32)
        else:
            own, ahead = sums_ref[:PAD, :], sums_ref[PAD:, :]
        others = [get_sums(ref, count * dh) for ref in got_refs]
        mine, at, before = weights_of(step, others)
        whole, passed = own, jnp.zeros((PAD, LANES), F32)
        keep = jnp.zeros((PAD, LANES), F32)
        takes = []
        for a, other in zip(at, others):
            whole = whole + other
            passed = passed + jnp.where(a < mine, other, 0.0)
            keep = keep + jnp.where(a > mine, other, 0.0)
            behind = jnp.where(mine > a, own, 0.0)
            for b, third in zip(at, others):
                behind = behind + jnp.where(b > a, third, 0.0)
            takes.append(jnp.exp(behind))
        keep, lead = jnp.exp(keep), jnp.exp(ahead)
        for h in range(count):
            rows = slice(h * dh, (h + 1) * dh)
            row = slice(h0 + h, h0 + h + 1)
            value = total_ref[rows, :] * keep[row, :]
            moved = jnp.zeros((dh, dh), F32)
            for ref, take, weight in zip(got_refs, takes, before):
                theirs = ref[rows, :].astype(F32)
                value = value + theirs * take[row, :]
                moved = moved + theirs * (weight * lead)[row, :]
            new_total[rows, :] = value
            send[rows, :] = value.astype(BF16)
            new_carried[rows, :] = moved if carried is None else carried_ref[rows, :] + moved
        put_sums(send, count * dh, whole)
        new_sums[:PAD, :] = whole
        new_sums[PAD:, :] = ahead + passed

    shapes = [((count * dh, dh), F32)] * 2 + [((count * dh + 2 * PAD, dh), BF16), ((2 * PAD, LANES), F32)]
    args = [total, sums, *got] + ([] if carried is None else [carried])
    return call(kernel, shapes, args)


def attend(z, part, kv, qs_in, col, row, carried, got, sums):
    h0, count = part
    n, rows, dh, seg = z.n, z.rows, z.dh, z.seg

    def kernel(*refs):
        kv_refs, q_refs = refs[:n], refs[n : 2 * n]
        col_ref, row_ref, carried_ref, sums_ref = refs[2 * n : 2 * n + 4]
        got_refs = refs[2 * n + 4 : 2 * n + 4 + len(got)]
        outs = refs[-n - 4 : -4]
        ks, vs, qs, mixed = refs[-4:]
        scatter_heads(z, kv_refs, ks, h0, count)
        scatter_heads(z, kv_refs, vs, z.local + h0, count)
        scatter_heads(z, q_refs, qs, h0, count)
        before = weights_of(z.steps[-1], [get_sums(ref, count * dh) for ref in got_refs])[2]
        lead = jnp.exp(sums_ref[PAD:, :])
        before = [weight * lead for weight in before]
        t = lax.broadcasted_iota(jnp.int32, (seg, seg), 0)
        s = lax.broadcasted_iota(jnp.int32, (seg, seg), 1)
        causal = s <= t
        for h in range(count):
            at = slice(h * dh, (h + 1) * dh)
            former = carried_ref[at, :]
            for ref, weight in zip(got_refs, before):
                former = former + ref[at, :].astype(F32) * weight[h0 + h : h0 + h + 1, :]
            q = qs[h]
            d_col = col_ref[:, h0 + h : h0 + h + 1]
            scores = dot(q, ks[h], (1, 1))
            gap = jnp.where(causal, d_col - row_ref[h0 + h : h0 + h + 1, :], 0.0)
            weights = jnp.where(causal, scores * jnp.exp(gap), 0.0).astype(BF16)
            out = dot(weights, vs[h], (1, 0)) + jnp.exp(d_col) * dot(q, former.astype(BF16), (1, 0))
            mixed[:, at] = out.astype(BF16)
        me = lax.axis_index("inner")
        for k in range(n):
            chunk = lax.rem(me + k, n)
            outs[k][...] = mixed[pl.ds(pl.multiple_of(chunk * rows, rows), rows), :]

    scratch = [pltpu.VMEM((count, seg, dh), BF16)] * 3 + [pltpu.VMEM((seg, count * dh), BF16)]
    args = [*kv, *qs_in, col, row, carried, sums, *got]
    return call(kernel, [((rows, count * dh), BF16)] * n, args, scratch=scratch)


def normalize(z, lengths, gain, blocks):
    n, rows, dh = z.n, z.rows, z.dh

    def kernel(len_ref, gain_ref, *refs):
        out = refs[-1]
        me = lax.axis_index("inner")
        live = live_mask(len_ref, rows)
        total = jnp.zeros((rows, 1), F32)
        for ref in refs[:-1]:
            flat = ref[...].astype(F32)
            total = total + jnp.sum(flat * flat, axis=1, keepdims=True)
        inv = lax.rsqrt(total / z.width + 1e-06)
        for p, (h0, count) in enumerate(z.parts):
            for k in range(n):
                group = lax.rem(me + (n - k), n)
                cols = pl.ds(pl.multiple_of((group * z.local + h0) * dh, LANES), count * dh)
                scaled = refs[p * n + k][...].astype(F32) * inv * gain_ref[:, cols]
                out[:, cols] = jnp.where(live, scaled, 0.0).astype(BF16)

    flat_blocks = [block for part in blocks for block in part]
    args = [lengths, gain, *flat_blocks]
    specs = [SMEM] + [pl.BlockSpec(memory_space=pltpu.VMEM)] * (len(args) - 1)
    return call(kernel, [((rows, z.width), BF16)], args, specs)[0]


def shift_blocks(z, blocks):
    n = z.n
    return [blocks[0]] + [
        lax.ppermute(blocks[k], "inner", [(i, (i + k) % n) for i in range(n)]) for k in range(1, n)
    ]


def shards(low_rank, q_base, k_base, v_base, edit_up, log_decay, lengths, norm_gain):
    z = Sizes(q_base, log_decay)
    every = (0, z.local)
    low_rank, log_decay = low_rank.T, log_decay.T
    kv = project(z, "kv", every, lengths, low_rank, (k_base, v_base), edit_up, (1, 2), log_decay, True)
    kv = shift_blocks(z, kv)
    qs = project(z, "q", every, lengths, low_rank, (q_base,), edit_up, (0,), log_decay, False)
    qs = shift_blocks(z, [qs[0], *gate(qs[1:], (kv[1],))])
    col, row, *states = segment_states(z, kv)
    outs = []
    for p, part in enumerate(z.parts):
        total, send = states[2 * p : 2 * p + 2]
        carried, sums = None, row
        for step in z.steps[:-1]:
            got = exchange(step, False, send)
            total, carried, send, sums = join(z, step, part, total, got, sums, carried)
        got = exchange(z.steps[-1], True, send)
        outs.append(shift_blocks(z, attend(z, part, kv, qs, col, row, carried, got, sums)))
    return normalize(z, lengths, norm_gain[None, :], outs)


def solution(mesh):
    rows = P(("ctx", "inner"), None)
    return jax.shard_map(
        shards,
        mesh=mesh,
        in_specs=(rows, rows, rows, rows, P(), rows, P("ctx"), P()),
        out_specs=rows,
        check_vma=False,
    )
```

time: 85.1 us -> 72.8 us (0.86)
  waiting for transfers between devices: 37.3 us -> 28 us
  local copies, waits for them, and re-layouts: 4.22 us -> 0.02 us
  Pallas kernels: 7.09 us -> 9.83 us
  starting transfers between devices: 35.3 us -> 33.8 us
    ppermute x6, waiting for transfers between devices: 6.95 us -> 0.86 us  [exchange(): lax.ppermute(send, 'ctx', [(i, i ^ m << shift) for i in range(size) if ne...]
    unnamed x16 -> x2, local copies, waits for them, and re-layouts: 4.21 us -> 0.01 us
    ppermute x18 -> x12, waiting for transfers between devices: 30.4 us -> 27.2 us  [shift_blocks(): lax.ppermute(blocks[k], 'inner', [(i, (i + k) % n) for i in range(n)])]
    pallas_call x13 -> x11, Pallas kernels: 7.09 us -> 9.83 us  [the longest x10 9.83 us: call(): pl.pallas_call(kernel, out_shape=[jax.ShapeDtypeStruct(*shape) for shape...]
    ppermute x18 -> x12, starting transfers between devices: 27.6 us -> 26.4 us  [shift_blocks(): lax.ppermute(blocks[k], 'inner', [(i, (i + k) % n) for i in range(n)])]
  transfers between devices with their start and end apart: 24 -> 18, of which waited for: 11 -> 5; matrix products, arithmetic and copies ran while one was open for 0% -> 0% of each run, Pallas kernels for 7% -> 7%
where the time goes in v2:
time: 72.8 us; the launch traced here: 72.4 us
  starting transfers between devices  33.8 us (46%)
  waiting for transfers between devices  28 us (38%)
  Pallas kernels  9.83 us (14%)
  between operations  0.78 us (1%)
    ppermute x12, waiting for transfers between devices, shift_blocks(): lax.ppermute(blocks[k], 'inner', [(i, (i + k) % n) for i in range(n)])  27.2 us
    ppermute x12, starting transfers between devices, shift_blocks(): lax.ppermute(blocks[k], 'inner', [(i, (i + k) % n) for i in range(n)])  26.4 us
    pallas_call x10, Pallas kernels, call(): pl.pallas_call(kernel, out_shape=[jax.ShapeDtypeStruct(*shape) for shape...  9.83 us
    ppermute x6, starting transfers between devices, exchange(): lax.ppermute(send, 'ctx', [(i, i ^ m << shift) for i in range(size) if ne...  7.42 us
  transfers between devices with their start and end apart: 18, of which 5 were waited for; matrix products, arithmetic and copies ran while one was open for 0% of the time, Pallas kernels for 7%

profile of v2, /device:TPU:0, one launch (start us, length us, event | category | flops | bytes accessed | tf_op | source)
XLA Modules:
  0.0 72.4 jit_solution(4830755968933883808)
XLA Ops:
  0.7 2.1 %shard_map.82 = (bf16[1168,128]{1,0:T(8,128)(2,1)S(1)}, bf16[1168,128]{1,0:T(8,128)(2,1)S(1)}, bf16[1168,128]{1,0:T(8,128)(2,1)S(1)}, bf16[1168,128]{1,0:T(8,128)(2,1)S(1)}) custom-call(s32[1]{0:T(128)S(6)} %copy.15.len_ref, bf16[32,64]{1,0:T(8,128)(2,1)} %bitcast.4, bf16[64,4608]{1,0:T(8,128)(2,1)} %refs_0_.2, bf16[64,4608]{1,0:T(8,128)(2,1)} %refs_1_.2, ...), custom_call_target="tpu_custom_call" | custom-call | flops 1000000000 | bytes 1 | tf_op jit(solution)/shard_map/pallas_call | solution.py:31
  2.8 3.1 %collective-permute-start = (bf16[1168,128]{1,0:T(8,128)(2,1)S(1)}, bf16[1168,128]{1,0:T(8,128)(2,1)S(1)}, u32[]{:S(2)}, u32[]{:S(2)}) collective-permute-start(bf16[1168,128]{1,0:T(8,128)(2,1)S(1)} %get-tuple-element.45), channel_id=1, source_target_pairs={{0,1},{1,2},{2,3},{3,0},{4,5},{5,6},{6,7},{7,4},{8,9},{9,10},{10,1... | collective-permute-start | bytes 897032 | tf_op jit(solution)/shard_map/ppermute | solution.py:359
  5.9 2.6 %collective-permute-start.1 = (bf16[1168,128]{1,0:T(8,128)(2,1)S(1)}, bf16[1168,128]{1,0:T(8,128)(2,1)S(1)}, u32[]{:S(2)}, u32[]{:S(2)}) collective-permute-start(bf16[1168,128]{1,0:T(8,128)(2,1)S(1)} %get-tuple-element.46), channel_id=1, source_target_pairs={{0,2},{1,3},{2,0},{3,1},{4,6},{5,7},{6,4},{7,5},{8,10},{9,11},{10,... | collective-permute-start | bytes 897032 | tf_op jit(solution)/shard_map/ppermute | solution.py:359
  8.5 1.4 %collective-permute-start.2 = (bf16[1168,128]{1,0:T(8,128)(2,1)S(1)}, bf16[1168,128]{1,0:T(8,128)(2,1)S(1)}, u32[]{:S(2)}, u32[]{:S(2)}) collective-permute-start(bf16[1168,128]{1,0:T(8,128)(2,1)S(1)} %get-tuple-element.47), channel_id=1, source_target_pairs={{0,3},{1,0},{2,1},{3,2},{4,7},{5,4},{6,5},{7,6},{8,11},{9,8},{10,9... | collective-permute-start | bytes 897032 | tf_op jit(solution)/shard_map/ppermute | solution.py:359
  9.8 6.2 %collective-permute-done.refs_3_.refs_1_ = bf16[1168,128]{1,0:T(8,128)(2,1)S(1)} collective-permute-done((bf16[1168,128]{1,0:T(8,128)(2,1)S(1)}, bf16[1168,128]{1,0:T(8,128)(2,1)S(1)}, u32[]{:S(2)}, u32[]{:S(2)}) %collective-permute-start) | collective-permute-done | bytes 299040 | tf_op jit(solution)/shard_map/ppermute | solution.py:359
  16.0 12.0 %collective-permute-done.1.refs_2_ = bf16[1168,128]{1,0:T(8,128)(2,1)S(1)} collective-permute-done((bf16[1168,128]{1,0:T(8,128)(2,1)S(1)}, bf16[1168,128]{1,0:T(8,128)(2,1)S(1)}, u32[]{:S(2)}, u32[]{:S(2)}) %collective-permute-start.1) | collective-permute-done | bytes 299040 | tf_op jit(solution)/shard_map/ppermute | solution.py:359
  28.0 1.2 %shard_map.85 = (f32[256,128]{1,0:T(8,128)S(1)}, f32[16,256]{1,0:T(8,128)S(1)}, f32[640,128]{1,0:T(8,128)S(1)}, bf16[672,128]{1,0:T(8,128)(2,1)S(1)}, f32[512,12...) custom-call(bf16[1168,128]{1,0:T(8,128)(2,1)S(1)} %get-tuple-element.44.refs_0_, ...), custom_call_target="tpu_custom_call" | custom-call | flops 1000000000 | bytes 1 | tf_op jit(solution)/shard_map/pallas_call | solution.py:31
  30.7 1.5 %collective-permute-start.13 = (bf16[544,128]{1,0:T(8,128)(2,1)S(1)}, bf16[544,128]{1,0:T(8,128)(2,1)S(1)}, u32[]{:S(2)}, u32[]{:S(2)}) collective-permute-start(bf16[544,128]{1,0:T(8,128)(2,1)S(1)} %get-tuple-element.74), channel_id=1, source_target_pairs={{0,8},{4,12},{8,0},{12,4},{16,24},{20,28},{24,16},{28,20},{1,9},{5... | collective-permute-start | bytes 417800 | tf_op jit(solution)/shard_map/ppermute | solution.py:223
  33.0 1.8 %shard_map.83 = (bf16[576,128]{1,0:T(8,128)(2,1)S(1)}, bf16[576,128]{1,0:T(8,128)(2,1)S(1)}, bf16[576,128]{1,0:T(8,128)(2,1)S(1)}, bf16[576,128]{1,0:T(8,128)(2,1)S(1)}) custom-call(s32[1]{0:T(128)S(6)} %copy.15.len_ref, bf16[32,64]{1,0:T(8,128)(2,1)} %bitcast.5, bf16[64,4608]{1,0:T(8,128)(2,1)} %refs_0_.3, bf16[32,13824]{1,0:T(8,128)(2,1)} %refs_1_.3, ...), custom_call_target="tpu_custom_call" | custom-call | flops 1000000000 | bytes 1 | tf_op jit(solution)/shard_map/pallas_call | solution.py:31
  34.8 6.9 %collective-permute-start.3 = (bf16[576,128]{1,0:T(8,128)(2,1)S(1)}, bf16[576,128]{1,0:T(8,128)(2,1)S(1)}, u32[]{:S(2)}, u32[]{:S(2)}) collective-permute-start(bf16[576,128]{1,0:T(8,128)(2,1)S(1)} %get-tuple-element.52), channel_id=1, source_target_pairs={{0,1},{1,2},{2,3},{3,0},{4,5},{5,6},{6,7},{7,4},{8,9},{9,10},{10,1... | collective-permute-start | bytes 442376 | tf_op jit(solution)/shard_map/ppermute | solution.py:359
  41.7 1.6 %collective-permute-start.4 = (bf16[576,128]{1,0:T(8,128)(2,1)S(1)}, bf16[576,128]{1,0:T(8,128)(2,1)S(1)}, u32[]{:S(2)}, u32[]{:S(2)}) collective-permute-start(bf16[576,128]{1,0:T(8,128)(2,1)S(1)} %get-tuple-element.53), channel_id=1, source_target_pairs={{0,2},{1,3},{2,0},{3,1},{4,6},{5,7},{6,4},{7,5},{8,10},{9,11},{10,... | collective-permute-start | bytes 442376 | tf_op jit(solution)/shard_map/ppermute | solution.py:359
  43.3 0.9 %collective-permute-start.5 = (bf16[576,128]{1,0:T(8,128)(2,1)S(1)}, bf16[576,128]{1,0:T(8,128)(2,1)S(1)}, u32[]{:S(2)}, u32[]{:S(2)}) collective-permute-start(bf16[576,128]{1,0:T(8,128)(2,1)S(1)} %get-tuple-element.54), channel_id=1, source_target_pairs={{0,3},{1,0},{2,1},{3,2},{4,7},{5,4},{6,5},{7,6},{8,11},{9,8},{10,9... | collective-permute-start | bytes 442376 | tf_op jit(solution)/shard_map/ppermute | solution.py:359
  45.0 3.4 %collective-permute-start.14 = (bf16[544,128]{1,0:T(8,128)(2,1)S(1)}, bf16[544,128]{1,0:T(8,128)(2,1)S(1)}, u32[]{:S(2)}, u32[]{:S(2)}) collective-permute-start(bf16[544,128]{1,0:T(8,128)(2,1)S(1)} %get-tuple-element.78), channel_id=1, source_target_pairs={{0,16},{4,20},{8,24},{12,28},{1,17},{5,21},{9,25},{13,29},{2,18},{... | collective-permute-start | bytes 417800 | tf_op jit(solution)/shard_map/ppermute | solution.py:223
  49.2 1.3 %collective-permute-start.8 = (bf16[672,128]{1,0:T(8,128)(2,1)S(1)}, bf16[672,128]{1,0:T(8,128)(2,1)S(1)}, u32[]{:S(2)}, u32[]{:S(2)}) collective-permute-start(bf16[672,128]{1,0:T(8,128)(2,1)S(1)} %get-tuple-element.65), channel_id=1, source_target_pairs={{0,16},{4,20},{8,24},{12,28},{1,17},{5,21},{9,25},{13,29},{2,18},{... | collective-permute-start | bytes 516104 | tf_op jit(solution)/shard_map/ppermute | solution.py:223
  50.5 2.3 %collective-permute-done.4.refs_6_ = bf16[576,128]{1,0:T(8,128)(2,1)S(1)} collective-permute-done((bf16[576,128]{1,0:T(8,128)(2,1)S(1)}, bf16[576,128]{1,0:T(8,128)(2,1)S(1)}, u32[]{:S(2)}, u32[]{:S(2)}) %collective-permute-start.4) | collective-permute-done | bytes 147488 | tf_op jit(solution)/shard_map/ppermute | solution.py:359
  53.6 3.7 %collective-permute-start.15 = (bf16[64,512]{1,0:T(8,128)(2,1)S(1)}, bf16[64,512]{1,0:T(8,128)(2,1)S(1)}, u32[]{:S(2)}, u32[]{:S(2)}) collective-permute-start(bf16[64,512]{1,0:T(8,128)(2,1)S(1)} %get-tuple-element.80), channel_id=1, source_target_pairs={{0,1},{1,2},{2,3},{3,0},{4,5},{5,6},{6,7},{7,4},{8,9},{9,10},{10,1... | collective-permute-start | bytes 196616 | tf_op jit(solution)/shard_map/ppermute | solution.py:359
  57.3 0.9 %shard_map.88 = (bf16[64,640]{1,0:T(8,128)(2,1)S(1)}, bf16[64,640]{1,0:T(8,128)(2,1)S(1)}, bf16[64,640]{1,0:T(8,128)(2,1)S(1)}, bf16[64,640]{1,0:T(8,128)(2,1)S(1)}) custom-call(bf16[1168,128]{1,0:T(8,128)(2,1)S(1)} %get-tuple-element.44.refs_0_, bf16[1168,128]{1,0:T(8,128)(2,1)S(1)} %collective-permute-done.refs_3_.refs_1_, ...), custom_call_target="tpu_custom_call" | custom-call | flops 1000000000 | bytes 1 | tf_op jit(solution)/shard_map/pallas_call | solution.py:31
  58.2 1.4 %collective-permute-start.10 = (bf16[64,640]{1,0:T(8,128)(2,1)S(1)}, bf16[64,640]{1,0:T(8,128)(2,1)S(1)}, u32[]{:S(2)}, u32[]{:S(2)}) collective-permute-start(bf16[64,640]{1,0:T(8,128)(2,1)S(1)} %get-tuple-element.68), channel_id=1, source_target_pairs={{0,2},{1,3},{2,0},{3,1},{4,6},{5,7},{6,4},{7,5},{8,10},{9,11},{10,... | collective-permute-start | bytes 245768 | tf_op jit(solution)/shard_map/ppermute | solution.py:359
  59.6 1.1 %collective-permute-start.11 = (bf16[64,640]{1,0:T(8,128)(2,1)S(1)}, bf16[64,640]{1,0:T(8,128)(2,1)S(1)}, u32[]{:S(2)}, u32[]{:S(2)}) collective-permute-start(bf16[64,640]{1,0:T(8,128)(2,1)S(1)} %get-tuple-element.69), channel_id=1, source_target_pairs={{0,3},{1,0},{2,1},{3,2},{4,7},{5,4},{6,5},{7,6},{8,11},{9,8},{10,9... | collective-permute-start | bytes 245768 | tf_op jit(solution)/shard_map/ppermute | solution.py:359
  60.6 1.0 %collective-permute-start.9 = (bf16[64,640]{1,0:T(8,128)(2,1)S(1)}, bf16[64,640]{1,0:T(8,128)(2,1)S(1)}, u32[]{:S(2)}, u32[]{:S(2)}) collective-permute-start(bf16[64,640]{1,0:T(8,128)(2,1)S(1)} %get-tuple-element.67), channel_id=1, source_target_pairs={{0,1},{1,2},{2,3},{3,0},{4,5},{5,6},{6,7},{7,4},{8,9},{9,10},{10,1... | collective-permute-start | bytes 245768 | tf_op jit(solution)/shard_map/ppermute | solution.py:359
  61.6 1.6 %collective-permute-start.16 = (bf16[64,512]{1,0:T(8,128)(2,1)S(1)}, bf16[64,512]{1,0:T(8,128)(2,1)S(1)}, u32[]{:S(2)}, u32[]{:S(2)}) collective-permute-start(bf16[64,512]{1,0:T(8,128)(2,1)S(1)} %get-tuple-element.81), channel_id=1, source_target_pairs={{0,2},{1,3},{2,0},{3,1},{4,6},{5,7},{6,4},{7,5},{8,10},{9,11},{10,... | collective-permute-start | bytes 196616 | tf_op jit(solution)/shard_map/ppermute | solution.py:359
  63.2 1.3 %collective-permute-start.17 = (bf16[64,512]{1,0:T(8,128)(2,1)S(1)}, bf16[64,512]{1,0:T(8,128)(2,1)S(1)}, u32[]{:S(2)}, u32[]{:S(2)}) collective-permute-start(bf16[64,512]{1,0:T(8,128)(2,1)S(1)} %get-tuple-element.82), channel_id=1, source_target_pairs={{0,3},{1,0},{2,1},{3,2},{4,7},{5,4},{6,5},{7,6},{8,11},{9,8},{10,9... | collective-permute-start | bytes 196616 | tf_op jit(solution)/shard_map/ppermute | solution.py:359
  64.5 6.7 %collective-permute-done.16.refs_6_ = bf16[64,512]{1,0:T(8,128)(2,1)S(1)} collective-permute-done((bf16[64,512]{1,0:T(8,128)(2,1)S(1)}, bf16[64,512]{1,0:T(8,128)(2,1)S(1)}, u32[]{:S(2)}, u32[]{:S(2)}) %collective-permute-start.16) | collective-permute-done | bytes 65568 | tf_op jit(solution)/shard_map/ppermute | solution.py:359
  71.2 1.2 %shard_map.92 = bf16[64,4608]{1,0:T(8,128)(2,1)} custom-call(s32[1]{0:T(128)S(6)} %copy.15.len_ref, f32[1,4608]{1,0:T(1,128)S(1)} %broadcast_in_dim.3.gain_ref, bf16[64,640]{1,0:T(8,128)(2,1)S(1)} %get-tuple-element.66.refs_0_, bf16[64,640]{1,0:T(8,128)(2,1)S(1)} %collective-permute-done.9.refs_1_, bf16[64,640]{1,0:T(8,128)(2,1)S(1)} %collective-permute-done.10.refs_2_, ...), custom_call_target="tpu_custom_call" | custom-call | flops 1000000000 | bytes 1 | tf_op jit(solution)/shard_map/pallas_call | solution.py:31
  (26 shorter events, 4.7 us)
Async XLA Ops:
  2.8 13.2 %collective-permute-start = (bf16[1168,128]{1,0:T(8,128)(2,1)S(1)}, bf16[1168,128]{1,0:T(8,128)(2,1)S(1)}, u32[]{:S(2)}, u32[]{:S(2)}) collective-permute-start(bf16[1168,128]{1,0:T(8,128)(2,1)S(1)} %get-tuple-element.45), channel_id=1, source_target_pairs={{0,1},{1,2},{2,3},{3,0},{4,5},{5,6},{6,7},{7,4},{8,9},{9,10},{10,1... | collective-permute-start | bytes 897032 | tf_op jit(solution)/shard_map/ppermute | solution.py:359
  5.9 22.1 %collective-permute-start.1 = (bf16[1168,128]{1,0:T(8,128)(2,1)S(1)}, bf16[1168,128]{1,0:T(8,128)(2,1)S(1)}, u32[]{:S(2)}, u32[]{:S(2)}) collective-permute-start(bf16[1168,128]{1,0:T(8,128)(2,1)S(1)} %get-tuple-element.46), channel_id=1, source_target_pairs={{0,2},{1,3},{2,0},{3,1},{4,6},{5,7},{6,4},{7,5},{8,10},{9,11},{10,... | collective-permute-start | bytes 897032 | tf_op jit(solution)/shard_map/ppermute | solution.py:359
  8.5 19.5 %collective-permute-start.2 = (bf16[1168,128]{1,0:T(8,128)(2,1)S(1)}, bf16[1168,128]{1,0:T(8,128)(2,1)S(1)}, u32[]{:S(2)}, u32[]{:S(2)}) collective-permute-start(bf16[1168,128]{1,0:T(8,128)(2,1)S(1)} %get-tuple-element.47), channel_id=1, source_target_pairs={{0,3},{1,0},{2,1},{3,2},{4,7},{5,4},{6,5},{7,6},{8,11},{9,8},{10,9... | collective-permute-start | bytes 897032 | tf_op jit(solution)/shard_map/ppermute | solution.py:359
  29.2 1.4 %collective-permute-start.12 = (bf16[544,128]{1,0:T(8,128)(2,1)S(1)}, bf16[544,128]{1,0:T(8,128)(2,1)S(1)}, u32[]{:S(2)}, u32[]{:S(2)}) collective-permute-start(bf16[544,128]{1,0:T(8,128)(2,1)S(1)} %get-tuple-element.71), channel_id=1, source_target_pairs={{0,4},{4,0},{8,12},{12,8},{16,20},{20,16},{24,28},{28,24},{1,5},{5... | collective-permute-start | bytes 417800 | tf_op jit(solution)/shard_map/ppermute | solution.py:223
  29.3 3.0 %collective-permute-start.6 = (bf16[672,128]{1,0:T(8,128)(2,1)S(1)}, bf16[672,128]{1,0:T(8,128)(2,1)S(1)}, u32[]{:S(2)}, u32[]{:S(2)}) collective-permute-start(bf16[672,128]{1,0:T(8,128)(2,1)S(1)} %get-tuple-element.58), channel_id=1, source_target_pairs={{0,4},{4,0},{8,12},{12,8},{16,20},{20,16},{24,28},{28,24},{1,5},{5... | collective-permute-start | bytes 516104 | tf_op jit(solution)/shard_map/ppermute | solution.py:223
  30.7 13.5 %collective-permute-start.13 = (bf16[544,128]{1,0:T(8,128)(2,1)S(1)}, bf16[544,128]{1,0:T(8,128)(2,1)S(1)}, u32[]{:S(2)}, u32[]{:S(2)}) collective-permute-start(bf16[544,128]{1,0:T(8,128)(2,1)S(1)} %get-tuple-element.74), channel_id=1, source_target_pairs={{0,8},{4,12},{8,0},{12,4},{16,24},{20,28},{24,16},{28,20},{1,9},{5... | collective-permute-start | bytes 417800 | tf_op jit(solution)/shard_map/ppermute | solution.py:223
  32.4 16.0 %collective-permute-start.7 = (bf16[672,128]{1,0:T(8,128)(2,1)S(1)}, bf16[672,128]{1,0:T(8,128)(2,1)S(1)}, u32[]{:S(2)}, u32[]{:S(2)}) collective-permute-start(bf16[672,128]{1,0:T(8,128)(2,1)S(1)} %get-tuple-element.61), channel_id=1, source_target_pairs={{0,8},{4,12},{8,0},{12,4},{16,24},{20,28},{24,16},{28,20},{1,9},{5... | collective-permute-start | bytes 516104 | tf_op jit(solution)/shard_map/ppermute | solution.py:223
  34.8 15.7 %collective-permute-start.3 = (bf16[576,128]{1,0:T(8,128)(2,1)S(1)}, bf16[576,128]{1,0:T(8,128)(2,1)S(1)}, u32[]{:S(2)}, u32[]{:S(2)}) collective-permute-start(bf16[576,128]{1,0:T(8,128)(2,1)S(1)} %get-tuple-element.52), channel_id=1, source_target_pairs={{0,1},{1,2},{2,3},{3,0},{4,5},{5,6},{6,7},{7,4},{8,9},{9,10},{10,1... | collective-permute-start | bytes 442376 | tf_op jit(solution)/shard_map/ppermute | solution.py:359
  41.7 11.0 %collective-permute-start.4 = (bf16[576,128]{1,0:T(8,128)(2,1)S(1)}, bf16[576,128]{1,0:T(8,128)(2,1)S(1)}, u32[]{:S(2)}, u32[]{:S(2)}) collective-permute-start(bf16[576,128]{1,0:T(8,128)(2,1)S(1)} %get-tuple-element.53), channel_id=1, source_target_pairs={{0,2},{1,3},{2,0},{3,1},{4,6},{5,7},{6,4},{7,5},{8,10},{9,11},{10,... | collective-permute-start | bytes 442376 | tf_op jit(solution)/shard_map/ppermute | solution.py:359
  43.3 9.5 %collective-permute-start.5 = (bf16[576,128]{1,0:T(8,128)(2,1)S(1)}, bf16[576,128]{1,0:T(8,128)(2,1)S(1)}, u32[]{:S(2)}, u32[]{:S(2)}) collective-permute-start(bf16[576,128]{1,0:T(8,128)(2,1)S(1)} %get-tuple-element.54), channel_id=1, source_target_pairs={{0,3},{1,0},{2,1},{3,2},{4,7},{5,4},{6,5},{7,6},{8,11},{9,8},{10,9... | collective-permute-start | bytes 442376 | tf_op jit(solution)/shard_map/ppermute | solution.py:359
  45.0 7.8 %collective-permute-start.14 = (bf16[544,128]{1,0:T(8,128)(2,1)S(1)}, bf16[544,128]{1,0:T(8,128)(2,1)S(1)}, u32[]{:S(2)}, u32[]{:S(2)}) collective-permute-start(bf16[544,128]{1,0:T(8,128)(2,1)S(1)} %get-tuple-element.78), channel_id=1, source_target_pairs={{0,16},{4,20},{8,24},{12,28},{1,17},{5,21},{9,25},{13,29},{2,18},{... | collective-permute-start | bytes 417800 | tf_op jit(solution)/shard_map/ppermute | solution.py:223
  49.2 8.1 %collective-permute-start.8 = (bf16[672,128]{1,0:T(8,128)(2,1)S(1)}, bf16[672,128]{1,0:T(8,128)(2,1)S(1)}, u32[]{:S(2)}, u32[]{:S(2)}) collective-permute-start(bf16[672,128]{1,0:T(8,128)(2,1)S(1)} %get-tuple-element.65), channel_id=1, source_target_pairs={{0,16},{4,20},{8,24},{12,28},{1,17},{5,21},{9,25},{13,29},{2,18},{... | collective-permute-start | bytes 516104 | tf_op jit(solution)/shard_map/ppermute | solution.py:223
  53.6 9.6 %collective-permute-start.15 = (bf16[64,512]{1,0:T(8,128)(2,1)S(1)}, bf16[64,512]{1,0:T(8,128)(2,1)S(1)}, u32[]{:S(2)}, u32[]{:S(2)}) collective-permute-start(bf16[64,512]{1,0:T(8,128)(2,1)S(1)} %get-tuple-element.80), channel_id=1, source_target_pairs={{0,1},{1,2},{2,3},{3,0},{4,5},{5,6},{6,7},{7,4},{8,9},{9,10},{10,1... | collective-permute-start | bytes 196616 | tf_op jit(solution)/shard_map/ppermute | solution.py:359
  57.3 7.2 %copy-start = (f32[4608]{0:T(1024)S(1)}, f32[4608]{0:T(1024)}, u32[]{:S(2)}) copy-start(f32[4608]{0:T(1024)} %param.15) | copy-start | bytes 55300
  58.2 13.1 %collective-permute-start.10 = (bf16[64,640]{1,0:T(8,128)(2,1)S(1)}, bf16[64,640]{1,0:T(8,128)(2,1)S(1)}, u32[]{:S(2)}, u32[]{:S(2)}) collective-permute-start(bf16[64,640]{1,0:T(8,128)(2,1)S(1)} %get-tuple-element.68), channel_id=1, source_target_pairs={{0,2},{1,3},{2,0},{3,1},{4,6},{5,7},{6,4},{7,5},{8,10},{9,11},{10,... | collective-permute-start | bytes 245768 | tf_op jit(solution)/shard_map/ppermute | solution.py:359
  59.6 11.6 %collective-permute-start.11 = (bf16[64,640]{1,0:T(8,128)(2,1)S(1)}, bf16[64,640]{1,0:T(8,128)(2,1)S(1)}, u32[]{:S(2)}, u32[]{:S(2)}) collective-permute-start(bf16[64,640]{1,0:T(8,128)(2,1)S(1)} %get-tuple-element.69), channel_id=1, source_target_pairs={{0,3},{1,0},{2,1},{3,2},{4,7},{5,4},{6,5},{7,6},{8,11},{9,8},{10,9... | collective-permute-start | bytes 245768 | tf_op jit(solution)/shard_map/ppermute | solution.py:359
  60.6 10.6 %collective-permute-start.9 = (bf16[64,640]{1,0:T(8,128)(2,1)S(1)}, bf16[64,640]{1,0:T(8,128)(2,1)S(1)}, u32[]{:S(2)}, u32[]{:S(2)}) collective-permute-start(bf16[64,640]{1,0:T(8,128)(2,1)S(1)} %get-tuple-element.67), channel_id=1, source_target_pairs={{0,1},{1,2},{2,3},{3,0},{4,5},{5,6},{6,7},{7,4},{8,9},{9,10},{10,1... | collective-permute-start | bytes 245768 | tf_op jit(solution)/shard_map/ppermute | solution.py:359
  61.6 9.6 %collective-permute-start.16 = (bf16[64,512]{1,0:T(8,128)(2,1)S(1)}, bf16[64,512]{1,0:T(8,128)(2,1)S(1)}, u32[]{:S(2)}, u32[]{:S(2)}) collective-permute-start(bf16[64,512]{1,0:T(8,128)(2,1)S(1)} %get-tuple-element.81), channel_id=1, source_target_pairs={{0,2},{1,3},{2,0},{3,1},{4,6},{5,7},{6,4},{7,5},{8,10},{9,11},{10,... | collective-permute-start | bytes 196616 | tf_op jit(solution)/shard_map/ppermute | solution.py:359
  63.2 8.0 %collective-permute-start.17 = (bf16[64,512]{1,0:T(8,128)(2,1)S(1)}, bf16[64,512]{1,0:T(8,128)(2,1)S(1)}, u32[]{:S(2)}, u32[]{:S(2)}) collective-permute-start(bf16[64,512]{1,0:T(8,128)(2,1)S(1)} %get-tuple-element.82), channel_id=1, source_target_pairs={{0,3},{1,0},{2,1},{3,2},{4,7},{5,4},{6,5},{7,6},{8,11},{9,8},{10,9... | collective-permute-start | bytes 196616 | tf_op jit(solution)/shard_map/ppermute | solution.py:359

commit v3 on v2

--- a/solution.py
+++ b/solution.py
@@ -10,7 +10,7 @@
 PAD = 16
 PARTS = 2
 PARAMS = pltpu.CompilerParams(vmem_limit_bytes=48 * 1024 * 1024)
-COST = pl.CostEstimate(flops=1_000_000_000, bytes_accessed=1, transcendentals=0)
+COST = pl.CostEstimate(flops=1000000000, bytes_accessed=1, transcendentals=0)
 SMEM = pl.BlockSpec(memory_space=pltpu.SMEM)
 
 
@@ -74,25 +74,29 @@
             at += first
 
 
-def project(z, names, part, lengths, low_rank, bases, edit_up, columns, log_decay, decays, after=()):
+def project(z, names, part, lengths, low_rank, bases, edit_up, columns, log_decay, decays, after=(), whole=False, places=None):
     h0, count = part
     n, rows, dh = z.n, z.rows, z.dh
     kinds = len(bases)
     rank = edit_up.shape[0]
+    places = places or (*range(1, n), 0)
     height = kinds * count * rows + (PAD if decays else 0)
 
     def kernel(len_ref, lr_ref, *refs):
         base_refs, up_ref, ld_from = refs[:kinds], refs[kinds], refs[kinds + 1]
-        outs = refs[-n - 5 : -5]
+        me = lax.axis_index("inner")
+        if whole:
+            outs = [refs[-6].at[lax.rem(me + k, n)] for k in places]
+        else:
+            outs = refs[-len(places) - 5 : -5]
         base_buf, up_buf, low_buf, ld_ref, sems = refs[-5:]
-        me = lax.axis_index("inner")
-
-        def copies(k):
-            at = (lax.rem(me + k, n) * z.local + h0) * dh
+
+        def copies(i):
+            at = (lax.rem(me + places[i], n) * z.local + h0) * dh
             for kind in range(kinds):
                 cols = pl.ds(pl.multiple_of(at, LANES), count * dh)
                 up_cols = pl.ds(pl.multiple_of(at + columns[kind] * z.width, LANES), count * dh)
-                slot = k * kinds + kind
+                slot = i * kinds + kind
                 yield pltpu.make_async_copy(base_refs[kind].at[:, cols], base_buf.at[slot], sems.at[0, slot])
                 yield pltpu.make_async_copy(up_ref.at[:, up_cols], up_buf.at[slot], sems.at[1, slot])
 
@@ -100,28 +104,27 @@
             pltpu.make_async_copy(lr_ref, low_buf, sems.at[0, n * kinds]),
             pltpu.make_async_copy(ld_from, ld_ref, sems.at[1, n * kinds]),
         ]
-        order = [*range(1, n), 0]
         for copy in small:
             copy.start()
-        for k in order:
-            for copy in copies(k):
+        for i in range(len(places)):
+            for copy in copies(i):
                 copy.start()
         live = live_mask(len_ref, rows)
         for copy in small:
             copy.wait()
         low = low_buf[...].T
-        for k in order:
-            for copy in copies(k):
+        for i, k in enumerate(places):
+            for copy in copies(i):
                 copy.wait()
             for kind in range(kinds):
-                slot = k * kinds + kind
+                slot = i * kinds + kind
                 edited = base_buf[slot].astype(F32) + dot(low, up_buf[slot], (1, 0))
                 if names[kind] != "q":
                     edited = jnp.where(live, edited, 0.0)
                 edited = edited.astype(BF16)
                 for h in range(count):
                     top = (kind * count + h) * rows
-                    outs[k][top : top + rows, :] = edited[:, h * dh : (h + 1) * dh]
+                    outs[i][top : top + rows, :] = edited[:, h * dh : (h + 1) * dh]
             if decays:
                 row = lax.broadcasted_iota(jnp.int32, (PAD, z.heads), 0)
                 col = lax.broadcasted_iota(jnp.int32, (PAD, z.heads), 1)
@@ -130,7 +133,7 @@
                 wide = jnp.concatenate(
                     [dot(pick, ld_ref[...], (1, 0)), jnp.zeros((PAD, LANES - rows), F32)], axis=1
                 )
-                outs[k][height - PAD : height, :] = wide.astype(BF16)
+                outs[i][height - PAD : height, :] = wide.astype(BF16)
 
     args = [lengths, *(pltpu.with_memory_space_constraint(a, pltpu.HBM) for a in (low_rank, *bases, edit_up, log_decay))]
     specs = [SMEM, *([pl.BlockSpec(memory_space=pltpu.HBM)] * (kinds + 3))]
@@ -141,7 +144,8 @@
         pltpu.VMEM(log_decay.shape, BF16),
         pltpu.SemaphoreType.DMA((2, n * kinds + 1)),
     ]
-    return call(kernel, [((height, dh), BF16)] * n, args, specs, scratch, after)
+    shapes = [((n, height, dh), BF16)] if whole else [((height, dh), BF16)] * len(places)
+    return call(kernel, shapes, args, specs, scratch, after)
 
 
 def scatter_heads(z, refs, held, first, count):
@@ -154,46 +158,48 @@
             held[h, at, :] = refs[k][top : top + z.rows, :]
 
 
-def segment_states(z, kv):
-    n, rows, dh, seg, heads = z.n, z.rows, z.dh, z.seg, z.local
+def segment_states(z, part, kv, decays=None, after=()):
+    h0, count = part
+    n, rows, dh, seg = z.n, z.rows, z.dh, z.seg
+    first = decays is None
 
     def kernel(*refs):
-        kv_refs = refs[:n]
-        col_ref, row_ref = refs[n : n + 2]
-        results = refs[n + 2 : n + 2 + 2 * len(z.parts)]
-        ks, vs, lds = refs[-3:]
-        me = lax.axis_index("inner")
-        for k in range(n):
-            lds[lax.rem(me + (n - k), n)] = kv_refs[k][2 * heads * rows :, :]
-        t = lax.broadcasted_iota(jnp.int32, (rows, LANES), 0)
-        s = lax.broadcasted_iota(jnp.int32, (rows, LANES), 1)
-        tri = jnp.where(s <= t, 1.0, 0.0).astype(BF16)
-        so_far = jnp.zeros((1, PAD), F32)
-        for j in range(n):
-            cum = dot(tri, lds[j], (1, 1)) + so_far
-            so_far = cum[rows - 1 : rows, :]
-            wide = jnp.concatenate([cum, jnp.zeros((rows, LANES - PAD), F32)], axis=1)
-            col_ref[j * rows : (j + 1) * rows, :] = wide
-        row_ref[...] = col_ref[...].T[:PAD, :]
-        scatter_heads(z, kv_refs, ks, 0, heads)
-        scatter_heads(z, kv_refs, vs, heads, heads)
+        kv_refs, refs = refs[:n], refs[n:]
+        if first:
+            state, send, col_ref, row_ref, ks, vs, lds = refs
+        else:
+            col_ref, row_ref, state, send, ks, vs = refs
+        if first:
+            me = lax.axis_index("inner")
+            for k in range(n):
+                lds[lax.rem(me + (n - k), n)] = kv_refs[k][2 * z.local * rows :, :]
+            t = lax.broadcasted_iota(jnp.int32, (rows, LANES), 0)
+            s = lax.broadcasted_iota(jnp.int32, (rows, LANES), 1)
+            tri = jnp.where(s <= t, 1.0, 0.0).astype(BF16)
+            so_far = jnp.zeros((1, PAD), F32)
+            for j in range(n):
+                cum = dot(tri, lds[j], (1, 1)) + so_far
+                so_far = cum[rows - 1 : rows, :]
+                wide = jnp.concatenate([cum, jnp.zeros((rows, LANES - PAD), F32)], axis=1)
+                col_ref[j * rows : (j + 1) * rows, :] = wide
+            row_ref[...] = col_ref[...].T[:PAD, :]
+        scatter_heads(z, kv_refs, ks, h0, count)
+        scatter_heads(z, kv_refs, vs, z.local + h0, count)
         col = col_ref[...]
         scale = jnp.exp(col[seg - 1 : seg, :] - col)
-        ending = jnp.broadcast_to(row_ref[:, seg - 1 : seg], (PAD, LANES))
-        for p, (h0, count) in enumerate(z.parts):
-            state, send = results[2 * p : 2 * p + 2]
-            for h in range(count):
-                scaled = (ks[h0 + h].astype(F32) * scale[:, h0 + h : h0 + h + 1]).astype(BF16)
-                value = dot(scaled, vs[h0 + h], (0, 0))
-                state[h * dh : (h + 1) * dh, :] = value
-                send[h * dh : (h + 1) * dh, :] = value.astype(BF16)
-            put_sums(send, count * dh, ending)
-
-    shapes = [((seg, LANES), F32), ((PAD, seg), F32)]
-    for _, count in z.parts:
-        shapes += [((count * dh, dh), F32), ((count * dh + 2 * PAD, dh), BF16)]
-    scratch = [pltpu.VMEM((heads, seg, dh), BF16)] * 2 + [pltpu.VMEM((n, PAD, LANES), BF16)]
-    return call(kernel, shapes, kv, scratch=scratch)
+        for h in range(count):
+            scaled = (ks[h].astype(F32) * scale[:, h0 + h : h0 + h + 1]).astype(BF16)
+            value = dot(scaled, vs[h], (0, 0))
+            state[h * dh : (h + 1) * dh, :] = value
+            send[h * dh : (h + 1) * dh, :] = value.astype(BF16)
+        put_sums(send, count * dh, jnp.broadcast_to(row_ref[:, seg - 1 : seg], (PAD, LANES)))
+
+    shapes = [((count * dh, dh), F32), ((count * dh + 2 * PAD, dh), BF16)]
+    scratch = [pltpu.VMEM((count, seg, dh), BF16)] * 2
+    if first:
+        shapes += [((seg, LANES), F32), ((PAD, seg), F32)]
+        scratch.append(pltpu.VMEM((n, PAD, LANES), BF16))
+    return call(kernel, shapes, [*kv, *(decays or ())], scratch=scratch, after=after)
 
 
 def put_sums(send, at, sums):
@@ -238,7 +244,7 @@
     return mine, at, before
 
 
-def join(z, step, part, total, got, sums, carried=None):
+def join(z, step, part, total, got, sums, carried=None, final=False):
     h0, count = part
     dh, parts = z.dh, len(got)
 
@@ -246,7 +252,8 @@
         total_ref, sums_ref = refs[:2]
         got_refs = refs[2 : 2 + parts]
         carried_ref = refs[2 + parts] if carried is not None else None
-        new_total, new_carried, send, new_sums = refs[-4:]
+        new_carried, send, new_sums = refs[-3:]
+        new_total = None if final else refs[-4]
         if carried is None:
             own = jnp.broadcast_to(sums_ref[:, z.seg - 1 : z.seg], (PAD, LANES))
             ahead = jnp.zeros((PAD, LANES), F32)
@@ -275,14 +282,16 @@
                 theirs = ref[rows, :].astype(F32)
                 value = value + theirs * take[row, :]
                 moved = moved + theirs * (weight * lead)[row, :]
-            new_total[rows, :] = value
+            if not final:
+                new_total[rows, :] = value
             send[rows, :] = value.astype(BF16)
             new_carried[rows, :] = moved if carried is None else carried_ref[rows, :] + moved
         put_sums(send, count * dh, whole)
         new_sums[:PAD, :] = whole
         new_sums[PAD:, :] = ahead + passed
 
-    shapes = [((count * dh, dh), F32)] * 2 + [((count * dh + 2 * PAD, dh), BF16), ((2 * PAD, LANES), F32)]
+    shapes = [((count * dh, dh), F32)] * (1 if final else 2)
+    shapes += [((count * dh + 2 * PAD, dh), BF16), ((2 * PAD, LANES), F32)]
     args = [total, sums, *got] + ([] if carried is None else [carried])
     return call(kernel, shapes, args)
 
@@ -292,14 +301,17 @@
     n, rows, dh, seg = z.n, z.rows, z.dh, z.seg
 
     def kernel(*refs):
-        kv_refs, q_refs = refs[:n], refs[n : 2 * n]
-        col_ref, row_ref, carried_ref, sums_ref = refs[2 * n : 2 * n + 4]
-        got_refs = refs[2 * n + 4 : 2 * n + 4 + len(got)]
+        kv_refs, q_refs = refs[:n], refs[n : n + 1]
+        col_ref, row_ref, carried_ref, sums_ref = refs[n + 1 : n + 5]
+        got_refs = refs[n + 5 : n + 5 + len(got)]
         outs = refs[-n - 4 : -4]
         ks, vs, qs, mixed = refs[-4:]
         scatter_heads(z, kv_refs, ks, h0, count)
         scatter_heads(z, kv_refs, vs, z.local + h0, count)
-        scatter_heads(z, q_refs, qs, h0, count)
+        for chunk in range(n):
+            for h in range(count):
+                rows_of = slice((h0 + h) * rows, (h0 + h + 1) * rows)
+                qs[h, chunk * rows : (chunk + 1) * rows, :] = q_refs[0][chunk, rows_of, :]
         before = weights_of(z.steps[-1], [get_sums(ref, count * dh) for ref in got_refs])[2]
         lead = jnp.exp(sums_ref[PAD:, :])
         before = [weight * lead for weight in before]
@@ -364,20 +376,31 @@
     z = Sizes(q_base, log_decay)
     every = (0, z.local)
     low_rank, log_decay = low_rank.T, log_decay.T
-    kv = project(z, "kv", every, lengths, low_rank, (k_base, v_base), edit_up, (1, 2), log_decay, True)
+    kv = [None] * z.n
+    first = z.n // 2
+    for ks in ((first,), tuple(k for k in range(1, z.n) if k != first) + (0,)):
+        made = project(
+            z, "kv", every, lengths, low_rank, (k_base, v_base), edit_up, (1, 2), log_decay, True, places=ks
+        )
+        for k, block in zip(ks, made):
+            kv[k] = block
     kv = shift_blocks(z, kv)
-    qs = project(z, "q", every, lengths, low_rank, (q_base,), edit_up, (0,), log_decay, False)
-    qs = shift_blocks(z, [qs[0], *gate(qs[1:], (kv[1],))])
-    col, row, *states = segment_states(z, kv)
+    qs = project(z, "q", every, lengths, low_rank, (q_base,), edit_up, (0,), log_decay, False, whole=True)
+    qs = gate(qs, (kv[2],))
+    qs = [lax.all_to_all(qs[0], "inner", split_axis=0, concat_axis=0, tiled=True)]
     outs = []
+    decays = None
     for p, part in enumerate(z.parts):
-        total, send = states[2 * p : 2 * p + 2]
-        carried, sums = None, row
+        total, send, *made = segment_states(z, part, kv, decays)
+        decays = decays or made
+        carried, sums = None, decays[1]
         for step in z.steps[:-1]:
+            final = step is z.steps[-2]
             got = exchange(step, False, send)
-            total, carried, send, sums = join(z, step, part, total, got, sums, carried)
+            *total, carried, send, sums = join(z, step, part, total, got, sums, carried, final)
+            total = total[0] if total else None
         got = exchange(z.steps[-1], True, send)
-        outs.append(shift_blocks(z, attend(z, part, kv, qs, col, row, carried, got, sums)))
+        outs.append(shift_blocks(z, attend(z, part, kv, qs, *decays, carried, got, sums)))
     return normalize(z, lengths, norm_gain[None, :], outs)
 
 

time: 72.8 us -> 69.2 us (0.951)
  waiting for transfers between devices: 28 us -> 22.8 us
  Pallas kernels: 9.83 us -> 10.6 us
    ppermute x12 -> x9, waiting for transfers between devices: 27.2 us -> 17.6 us  [shift_blocks(): lax.ppermute(blocks[k], 'inner', [(i, (i + k) % n) for i in range(n)])]
    ppermute x12 -> x9, starting transfers between devices: 26.4 us -> 21.8 us  [shift_blocks(): lax.ppermute(blocks[k], 'inner', [(i, (i + k) % n) for i in range(n)])]
    ppermute x6, waiting for transfers between devices: 0.86 us -> 5.15 us  [exchange(): lax.ppermute(send, 'ctx', [(i, i ^ m << shift) for i in range(size) if ne...]
    all_to_all x0 -> x1, starting transfers between devices: none -> 3.48 us  [shards(): lax.all_to_all(qs[0], 'inner', split_axis=0, concat_axis=0, tiled=True)]
    ppermute x6, starting transfers between devices: 7.42 us -> 9.29 us  [exchange(): lax.ppermute(send, 'ctx', [(i, i ^ m << shift) for i in range(size) if ne...]
    pallas_call x10 -> x12, Pallas kernels: 9.83 us -> 10.6 us  [call(): pl.pallas_call(kernel, out_shape=[jax.ShapeDtypeStruct(*shape) for shape...]
  transfers between devices with their start and end apart: 18 -> 16, of which waited for: 5 -> 4; matrix products, arithmetic and copies ran while one was open for 0% -> 0% of each run, Pallas kernels for 7% -> 12%
where the time goes in v3:
time: 69.2 us; the launch traced here: 68.8 us
  starting transfers between devices  34.5 us (50%)
  waiting for transfers between devices  22.8 us (33%)
  Pallas kernels  10.6 us (15%)
  between operations  0.83 us (1%)
    ppermute x9, starting transfers between devices, shift_blocks(): lax.ppermute(blocks[k], 'inner', [(i, (i + k) % n) for i in range(n)])  21.8 us
    ppermute x9, waiting for transfers between devices, shift_blocks(): lax.ppermute(blocks[k], 'inner', [(i, (i + k) % n) for i in range(n)])  17.6 us
    pallas_call x12, Pallas kernels, call(): pl.pallas_call(kernel, out_shape=[jax.ShapeDtypeStruct(*shape) for shape...  10.6 us
    ppermute x6, starting transfers between devices, exchange(): lax.ppermute(send, 'ctx', [(i, i ^ m << shift) for i in range(size) if ne...  9.29 us
    ppermute x6, waiting for transfers between devices, exchange(): lax.ppermute(send, 'ctx', [(i, i ^ m << shift) for i in range(size) if ne...  5.15 us
    all_to_all x1, starting transfers between devices, shards(): lax.all_to_all(qs[0], 'inner', split_axis=0, concat_axis=0, tiled=True)  3.48 us
  transfers between devices with their start and end apart: 16, of which 4 were waited for; matrix products, arithmetic and copies ran while one was open for 0% of the time, Pallas kernels for 12%

profile of v3, /device:TPU:0, one launch (start us, length us, event | category | flops | bytes accessed | tf_op | source)
XLA Modules:
  0.0 68.8 jit_solution(5677740375741639749)
XLA Ops:
  0.7 1.5 %shard_map.83 = bf16[1168,128]{1,0:T(8,128)(2,1)S(1)} custom-call(s32[1]{0:T(128)S(6)} %copy.11.len_ref, bf16[32,64]{1,0:T(8,128)(2,1)} %bitcast.5, bf16[64,4608]{1,0:T(8,128)(2,1)} %refs_0_.4, bf16[64,4608]{1,0:T(8,128)(2,1)} %refs_1_.4, bf16[32,13824]{1,0:T(8,128)(2,1)} %refs_1_.5, bf16[36,64]{1,0:T(8,128)(2,1)} %bitcast.2), custom_call_target="tpu_custom_call" | custom-call | flops 1000000000 | bytes 1 | tf_op jit(solution)/shard_map/pallas_call | solution.py:31
  2.1 4.1 %collective-permute-start.1 = (bf16[1168,128]{1,0:T(8,128)(2,1)S(1)}, bf16[1168,128]{1,0:T(8,128)(2,1)S(1)}, u32[]{:S(2)}, u32[]{:S(2)}) collective-permute-start(bf16[1168,128]{1,0:T(8,128)(2,1)S(1)} %shard_map.83), channel_id=1, source_target_pairs={{0,2},{1,3},{2,0},{3,1},{4,6},{5,7},{6,4},{7,5},{8,10},{9,11},{10,... | collective-permute-start | bytes 897032 | tf_op jit(solution)/shard_map/ppermute | solution.py:371
  6.2 1.9 %shard_map.82 = (bf16[1168,128]{1,0:T(8,128)(2,1)S(1)}, bf16[1168,128]{1,0:T(8,128)(2,1)S(1)}, bf16[1168,128]{1,0:T(8,128)(2,1)S(1)}) custom-call(s32[1]{0:T(128)S(6)} %copy.11.len_ref, bf16[32,64]{1,0:T(8,128)(2,1)} %bitcast.6, bf16[64,4608]{1,0:T(8,128)(2,1)} %refs_0_.4, bf16[64,4608]{1,0:T(8,128)(2,1)} %refs_1_.4, bf16[32,13824]{1,0:T(8,128)(2,1)} %refs_1_.5, ...), custom_call_target="tpu_custom_call" | custom-call | flops 1000000000 | bytes 1 | tf_op jit(solution)/shard_map/pallas_call | solution.py:31
  8.2 1.6 %collective-permute-start = (bf16[1168,128]{1,0:T(8,128)(2,1)S(1)}, bf16[1168,128]{1,0:T(8,128)(2,1)S(1)}, u32[]{:S(2)}, u32[]{:S(2)}) collective-permute-start(bf16[1168,128]{1,0:T(8,128)(2,1)S(1)} %get-tuple-element.37), channel_id=1, source_target_pairs={{0,1},{1,2},{2,3},{3,0},{4,5},{5,6},{6,7},{7,4},{8,9},{9,10},{10,1... | collective-permute-start | bytes 897032 | tf_op jit(solution)/shard_map/ppermute | solution.py:371
  9.8 2.2 %collective-permute-start.2 = (bf16[1168,128]{1,0:T(8,128)(2,1)S(1)}, bf16[1168,128]{1,0:T(8,128)(2,1)S(1)}, u32[]{:S(2)}, u32[]{:S(2)}) collective-permute-start(bf16[1168,128]{1,0:T(8,128)(2,1)S(1)} %get-tuple-element.38), channel_id=1, source_target_pairs={{0,3},{1,0},{2,1},{3,2},{4,7},{5,4},{6,5},{7,6},{8,11},{9,8},{10,9... | collective-permute-start | bytes 897032 | tf_op jit(solution)/shard_map/ppermute | solution.py:371
  12.0 2.6 %shard_map.84.refs_0_ = bf16[4,576,128]{2,1,0:T(8,128)(2,1)} custom-call(s32[1]{0:T(128)S(6)} %copy.11.len_ref, bf16[32,64]{1,0:T(8,128)(2,1)} %bitcast.7, bf16[64,4608]{1,0:T(8,128)(2,1)} %refs_0_.5, bf16[32,13824]{1,0:T(8,128)(2,1)} %refs_1_.5, bf16[36,64]{1,0:T(8,128)(2,1)} %bitcast.4), custom_call_target="tpu_custom_call" | custom-call | flops 1000000000 | bytes 1 | tf_op jit(solution)/shard_map/pallas_call | solution.py:31
  14.6 12.4 %collective-permute-done.1.refs_1_.refs_2_ = bf16[1168,128]{1,0:T(8,128)(2,1)S(1)} collective-permute-done((bf16[1168,128]{1,0:T(8,128)(2,1)S(1)}, bf16[1168,128]{1,0:T(8,128)(2,1)S(1)}, u32[]{:S(2)}, u32[]{:S(2)}) %collective-permute-start.1) | collective-permute-done | bytes 299040 | tf_op jit(solution)/shard_map/ppermute | solution.py:371
  27.0 3.5 %all-to-all-start = ((bf16[4,576,128]{2,1,0:T(8,128)(2,1)}), bf16[4,576,128]{2,1,0:T(8,128)(2,1)S(1)}, u32[]{:S(2)}, u32[]{:S(2)}) async-start(bf16[4,576,128]{2,1,0:T(8,128)(2,1)} %shard_map.85), calls=%async_computation | async-start | bytes 1179648 | tf_op jit(solution)/shard_map/all_to_all | solution.py:390
  30.5 0.8 %shard_map.86 = (f32[640,128]{1,0:T(8,128)S(1)}, bf16[672,128]{1,0:T(8,128)(2,1)S(1)}, f32[256,128]{1,0:T(8,128)S(1)}, f32[16,256]{1,0:T(8,128)S(1)}) custom-call(bf16[1168,128]{1,0:T(8,128)(2,1)S(1)} %get-tuple-element.36.refs_0_, bf16[1168,128]{1,0:T(8,128)(2,1)S(1)} %collective-permute-done.refs_1_, ...), custom_call_target="tpu_custom_call" | custom-call | flops 1000000000 | bytes 1 | tf_op jit(solution)/shard_map/pallas_call | solution.py:31
  31.3 0.5 shard_map.90
  32.5 0.8 %collective-permute-done.9.refs_2_ = bf16[544,128]{1,0:T(8,128)(2,1)S(1)} collective-permute-done((bf16[544,128]{1,0:T(8,128)(2,1)S(1)}, bf16[544,128]{1,0:T(8,128)(2,1)S(1)}, u32[]{:S(2)}, u32[]{:S(2)}) %collective-permute-start.9) | collective-permute-done | bytes 139296 | tf_op jit(solution)/shard_map/ppermute | solution.py:229
  33.4 1.9 %collective-permute-start.10 = (bf16[544,128]{1,0:T(8,128)(2,1)S(1)}, bf16[544,128]{1,0:T(8,128)(2,1)S(1)}, u32[]{:S(2)}, u32[]{:S(2)}) collective-permute-start(bf16[544,128]{1,0:T(8,128)(2,1)S(1)} %get-tuple-element.58), channel_id=1, source_target_pairs={{0,8},{4,12},{8,0},{12,4},{16,24},{20,28},{24,16},{28,20},{1,9},{5... | collective-permute-start | bytes 417800 | tf_op jit(solution)/shard_map/ppermute | solution.py:229
  35.7 4.3 %collective-permute-done.10.refs_2_ = bf16[544,128]{1,0:T(8,128)(2,1)S(1)} collective-permute-done((bf16[544,128]{1,0:T(8,128)(2,1)S(1)}, bf16[544,128]{1,0:T(8,128)(2,1)S(1)}, u32[]{:S(2)}, u32[]{:S(2)}) %collective-permute-start.10) | collective-permute-done | bytes 139296 | tf_op jit(solution)/shard_map/ppermute | solution.py:229
  40.1 3.8 %collective-permute-start.11 = (bf16[544,128]{1,0:T(8,128)(2,1)S(1)}, bf16[544,128]{1,0:T(8,128)(2,1)S(1)}, u32[]{:S(2)}, u32[]{:S(2)}) collective-permute-start(bf16[544,128]{1,0:T(8,128)(2,1)S(1)} %get-tuple-element.62), channel_id=1, source_target_pairs={{0,16},{4,20},{8,24},{12,28},{1,17},{5,21},{9,25},{13,29},{2,18},{... | collective-permute-start | bytes 417800 | tf_op jit(solution)/shard_map/ppermute | solution.py:229
  44.0 2.8 %collective-permute-start.5 = (bf16[672,128]{1,0:T(8,128)(2,1)S(1)}, bf16[672,128]{1,0:T(8,128)(2,1)S(1)}, u32[]{:S(2)}, u32[]{:S(2)}) collective-permute-start(bf16[672,128]{1,0:T(8,128)(2,1)S(1)} %get-tuple-element.49), channel_id=1, source_target_pairs={{0,16},{4,20},{8,24},{12,28},{1,17},{5,21},{9,25},{13,29},{2,18},{... | collective-permute-start | bytes 516104 | tf_op jit(solution)/shard_map/ppermute | solution.py:229
  46.8 0.8 %shard_map.93 = (bf16[64,512]{1,0:T(8,128)(2,1)S(1)}, bf16[64,512]{1,0:T(8,128)(2,1)S(1)}, bf16[64,512]{1,0:T(8,128)(2,1)S(1)}, bf16[64,512]{1,0:T(8,128)(2,1)S(1)}) custom-call(bf16[1168,128]{1,0:T(8,128)(2,1)S(1)} %get-tuple-element.36.refs_0_, bf16[1168,128]{1,0:T(8,128)(2,1)S(1)} %collective-permute-done.refs_1_, ...), custom_call_target="tpu_custom_call" | custom-call | flops 1000000000 | bytes 1 | tf_op jit(solution)/shard_map/pallas_call | solution.py:31
  47.6 4.6 %collective-permute-start.12 = (bf16[64,512]{1,0:T(8,128)(2,1)S(1)}, bf16[64,512]{1,0:T(8,128)(2,1)S(1)}, u32[]{:S(2)}, u32[]{:S(2)}) collective-permute-start(bf16[64,512]{1,0:T(8,128)(2,1)S(1)} %get-tuple-element.64), channel_id=1, source_target_pairs={{0,1},{1,2},{2,3},{3,0},{4,5},{5,6},{6,7},{7,4},{8,9},{9,10},{10,1... | collective-permute-start | bytes 196616 | tf_op jit(solution)/shard_map/ppermute | solution.py:371
  52.2 0.9 %shard_map.89 = (bf16[64,640]{1,0:T(8,128)(2,1)S(1)}, bf16[64,640]{1,0:T(8,128)(2,1)S(1)}, bf16[64,640]{1,0:T(8,128)(2,1)S(1)}, bf16[64,640]{1,0:T(8,128)(2,1)S(1)}) custom-call(bf16[1168,128]{1,0:T(8,128)(2,1)S(1)} %get-tuple-element.36.refs_0_, bf16[1168,128]{1,0:T(8,128)(2,1)S(1)} %collective-permute-done.refs_1_, ...), custom_call_target="tpu_custom_call" | custom-call | flops 1000000000 | bytes 1 | tf_op jit(solution)/shard_map/pallas_call | solution.py:31
  53.1 2.9 %collective-permute-start.6 = (bf16[64,640]{1,0:T(8,128)(2,1)S(1)}, bf16[64,640]{1,0:T(8,128)(2,1)S(1)}, u32[]{:S(2)}, u32[]{:S(2)}) collective-permute-start(bf16[64,640]{1,0:T(8,128)(2,1)S(1)} %get-tuple-element.51), channel_id=1, source_target_pairs={{0,1},{1,2},{2,3},{3,0},{4,5},{5,6},{6,7},{7,4},{8,9},{9,10},{10,1... | collective-permute-start | bytes 245768 | tf_op jit(solution)/shard_map/ppermute | solution.py:371
  55.9 2.0 %collective-permute-start.7 = (bf16[64,640]{1,0:T(8,128)(2,1)S(1)}, bf16[64,640]{1,0:T(8,128)(2,1)S(1)}, u32[]{:S(2)}, u32[]{:S(2)}) collective-permute-start(bf16[64,640]{1,0:T(8,128)(2,1)S(1)} %get-tuple-element.52), channel_id=1, source_target_pairs={{0,2},{1,3},{2,0},{3,1},{4,6},{5,7},{6,4},{7,5},{8,10},{9,11},{10,... | collective-permute-start | bytes 245768 | tf_op jit(solution)/shard_map/ppermute | solution.py:371
  57.9 2.8 %collective-permute-start.8 = (bf16[64,640]{1,0:T(8,128)(2,1)S(1)}, bf16[64,640]{1,0:T(8,128)(2,1)S(1)}, u32[]{:S(2)}, u32[]{:S(2)}) collective-permute-start(bf16[64,640]{1,0:T(8,128)(2,1)S(1)} %get-tuple-element.53), channel_id=1, source_target_pairs={{0,3},{1,0},{2,1},{3,2},{4,7},{5,4},{6,5},{7,6},{8,11},{9,8},{10,9... | collective-permute-start | bytes 245768 | tf_op jit(solution)/shard_map/ppermute | solution.py:371
  60.8 1.5 %collective-permute-start.14 = (bf16[64,512]{1,0:T(8,128)(2,1)S(1)}, bf16[64,512]{1,0:T(8,128)(2,1)S(1)}, u32[]{:S(2)}, u32[]{:S(2)}) collective-permute-start(bf16[64,512]{1,0:T(8,128)(2,1)S(1)} %get-tuple-element.66), channel_id=1, source_target_pairs={{0,3},{1,0},{2,1},{3,2},{4,7},{5,4},{6,5},{7,6},{8,11},{9,8},{10,9... | collective-permute-start | bytes 196616 | tf_op jit(solution)/shard_map/ppermute | solution.py:371
  62.3 5.2 %collective-permute-done.13.refs_6_ = bf16[64,512]{1,0:T(8,128)(2,1)S(1)} collective-permute-done((bf16[64,512]{1,0:T(8,128)(2,1)S(1)}, bf16[64,512]{1,0:T(8,128)(2,1)S(1)}, u32[]{:S(2)}, u32[]{:S(2)}) %collective-permute-start.13) | collective-permute-done | bytes 65568 | tf_op jit(solution)/shard_map/ppermute | solution.py:371
  67.6 1.2 %shard_map.94 = bf16[64,4608]{1,0:T(8,128)(2,1)} custom-call(s32[1]{0:T(128)S(6)} %copy.11.len_ref, f32[1,4608]{1,0:T(1,128)S(1)} %broadcast_in_dim.3.gain_ref, bf16[64,640]{1,0:T(8,128)(2,1)S(1)} %get-tuple-element.50.refs_0_, bf16[64,640]{1,0:T(8,128)(2,1)S(1)} %collective-permute-done.6.refs_1_, bf16[64,640]{1,0:T(8,128)(2,1)S(1)} %collective-permute-done.7.refs_2_, ...), custom_call_target="tpu_custom_call" | custom-call | flops 1000000000 | bytes 1 | tf_op jit(solution)/shard_map/pallas_call | solution.py:31
  (24 shorter events, 1.3 us)
Async XLA Ops:
  2.1 24.9 %collective-permute-start.1 = (bf16[1168,128]{1,0:T(8,128)(2,1)S(1)}, bf16[1168,128]{1,0:T(8,128)(2,1)S(1)}, u32[]{:S(2)}, u32[]{:S(2)}) collective-permute-start(bf16[1168,128]{1,0:T(8,128)(2,1)S(1)} %shard_map.83), channel_id=1, source_target_pairs={{0,2},{1,3},{2,0},{3,1},{4,6},{5,7},{6,4},{7,5},{8,10},{9,11},{10,... | collective-permute-start | bytes 897032 | tf_op jit(solution)/shard_map/ppermute | solution.py:371
  8.2 22.4 %collective-permute-start = (bf16[1168,128]{1,0:T(8,128)(2,1)S(1)}, bf16[1168,128]{1,0:T(8,128)(2,1)S(1)}, u32[]{:S(2)}, u32[]{:S(2)}) collective-permute-start(bf16[1168,128]{1,0:T(8,128)(2,1)S(1)} %get-tuple-element.37), channel_id=1, source_target_pairs={{0,1},{1,2},{2,3},{3,0},{4,5},{5,6},{6,7},{7,4},{8,9},{9,10},{10,1... | collective-permute-start | bytes 897032 | tf_op jit(solution)/shard_map/ppermute | solution.py:371
  9.8 20.7 %collective-permute-start.2 = (bf16[1168,128]{1,0:T(8,128)(2,1)S(1)}, bf16[1168,128]{1,0:T(8,128)(2,1)S(1)}, u32[]{:S(2)}, u32[]{:S(2)}) collective-permute-start(bf16[1168,128]{1,0:T(8,128)(2,1)S(1)} %get-tuple-element.38), channel_id=1, source_target_pairs={{0,3},{1,0},{2,1},{3,2},{4,7},{5,4},{6,5},{7,6},{8,11},{9,8},{10,9... | collective-permute-start | bytes 897032 | tf_op jit(solution)/shard_map/ppermute | solution.py:371
  27.0 19.8 %all-to-all-start = ((bf16[4,576,128]{2,1,0:T(8,128)(2,1)}), bf16[4,576,128]{2,1,0:T(8,128)(2,1)S(1)}, u32[]{:S(2)}, u32[]{:S(2)}) async-start(bf16[4,576,128]{2,1,0:T(8,128)(2,1)} %shard_map.85), calls=%async_computation | async-start | bytes 1179648 | tf_op jit(solution)/shard_map/all_to_all | solution.py:390
  31.9 1.4 %collective-permute-start.9 = (bf16[544,128]{1,0:T(8,128)(2,1)S(1)}, bf16[544,128]{1,0:T(8,128)(2,1)S(1)}, u32[]{:S(2)}, u32[]{:S(2)}) collective-permute-start(bf16[544,128]{1,0:T(8,128)(2,1)S(1)} %get-tuple-element.55), channel_id=1, source_target_pairs={{0,4},{4,0},{8,12},{12,8},{16,20},{20,16},{24,28},{28,24},{1,5},{5... | collective-permute-start | bytes 417800 | tf_op jit(solution)/shard_map/ppermute | solution.py:229
  32.0 3.4 %collective-permute-start.3 = (bf16[672,128]{1,0:T(8,128)(2,1)S(1)}, bf16[672,128]{1,0:T(8,128)(2,1)S(1)}, u32[]{:S(2)}, u32[]{:S(2)}) collective-permute-start(bf16[672,128]{1,0:T(8,128)(2,1)S(1)} %get-tuple-element.42), channel_id=1, source_target_pairs={{0,4},{4,0},{8,12},{12,8},{16,20},{20,16},{24,28},{28,24},{1,5},{5... | collective-permute-start | bytes 516104 | tf_op jit(solution)/shard_map/ppermute | solution.py:229
  33.4 6.6 %collective-permute-start.10 = (bf16[544,128]{1,0:T(8,128)(2,1)S(1)}, bf16[544,128]{1,0:T(8,128)(2,1)S(1)}, u32[]{:S(2)}, u32[]{:S(2)}) collective-permute-start(bf16[544,128]{1,0:T(8,128)(2,1)S(1)} %get-tuple-element.58), channel_id=1, source_target_pairs={{0,8},{4,12},{8,0},{12,4},{16,24},{20,28},{24,16},{28,20},{1,9},{5... | collective-permute-start | bytes 417800 | tf_op jit(solution)/shard_map/ppermute | solution.py:229
  35.5 8.4 %collective-permute-start.4 = (bf16[672,128]{1,0:T(8,128)(2,1)S(1)}, bf16[672,128]{1,0:T(8,128)(2,1)S(1)}, u32[]{:S(2)}, u32[]{:S(2)}) collective-permute-start(bf16[672,128]{1,0:T(8,128)(2,1)S(1)} %get-tuple-element.45), channel_id=1, source_target_pairs={{0,8},{4,12},{8,0},{12,4},{16,24},{20,28},{24,16},{28,20},{1,9},{5... | collective-permute-start | bytes 516104 | tf_op jit(solution)/shard_map/ppermute | solution.py:229
  40.1 6.7 %collective-permute-start.11 = (bf16[544,128]{1,0:T(8,128)(2,1)S(1)}, bf16[544,128]{1,0:T(8,128)(2,1)S(1)}, u32[]{:S(2)}, u32[]{:S(2)}) collective-permute-start(bf16[544,128]{1,0:T(8,128)(2,1)S(1)} %get-tuple-element.62), channel_id=1, source_target_pairs={{0,16},{4,20},{8,24},{12,28},{1,17},{5,21},{9,25},{13,29},{2,18},{... | collective-permute-start | bytes 417800 | tf_op jit(solution)/shard_map/ppermute | solution.py:229
  44.0 8.1 %collective-permute-start.5 = (bf16[672,128]{1,0:T(8,128)(2,1)S(1)}, bf16[672,128]{1,0:T(8,128)(2,1)S(1)}, u32[]{:S(2)}, u32[]{:S(2)}) collective-permute-start(bf16[672,128]{1,0:T(8,128)(2,1)S(1)} %get-tuple-element.49), channel_id=1, source_target_pairs={{0,16},{4,20},{8,24},{12,28},{1,17},{5,21},{9,25},{13,29},{2,18},{... | collective-permute-start | bytes 516104 | tf_op jit(solution)/shard_map/ppermute | solution.py:229
  47.6 13.2 %collective-permute-start.12 = (bf16[64,512]{1,0:T(8,128)(2,1)S(1)}, bf16[64,512]{1,0:T(8,128)(2,1)S(1)}, u32[]{:S(2)}, u32[]{:S(2)}) collective-permute-start(bf16[64,512]{1,0:T(8,128)(2,1)S(1)} %get-tuple-element.64), channel_id=1, source_target_pairs={{0,1},{1,2},{2,3},{3,0},{4,5},{5,6},{6,7},{7,4},{8,9},{9,10},{10,1... | collective-permute-start | bytes 196616 | tf_op jit(solution)/shard_map/ppermute | solution.py:371
  52.2 10.1 %copy-start = (f32[4608]{0:T(1024)S(1)}, f32[4608]{0:T(1024)}, u32[]{:S(2)}) copy-start(f32[4608]{0:T(1024)} %param.15) | copy-start | bytes 55300
  53.1 14.5 %collective-permute-start.6 = (bf16[64,640]{1,0:T(8,128)(2,1)S(1)}, bf16[64,640]{1,0:T(8,128)(2,1)S(1)}, u32[]{:S(2)}, u32[]{:S(2)}) collective-permute-start(bf16[64,640]{1,0:T(8,128)(2,1)S(1)} %get-tuple-element.51), channel_id=1, source_target_pairs={{0,1},{1,2},{2,3},{3,0},{4,5},{5,6},{6,7},{7,4},{8,9},{9,10},{10,1... | collective-permute-start | bytes 245768 | tf_op jit(solution)/shard_map/ppermute | solution.py:371
  55.9 11.6 %collective-permute-start.7 = (bf16[64,640]{1,0:T(8,128)(2,1)S(1)}, bf16[64,640]{1,0:T(8,128)(2,1)S(1)}, u32[]{:S(2)}, u32[]{:S(2)}) collective-permute-start(bf16[64,640]{1,0:T(8,128)(2,1)S(1)} %get-tuple-element.52), channel_id=1, source_target_pairs={{0,2},{1,3},{2,0},{3,1},{4,6},{5,7},{6,4},{7,5},{8,10},{9,11},{10,... | collective-permute-start | bytes 245768 | tf_op jit(solution)/shard_map/ppermute | solution.py:371
  57.9 9.7 %collective-permute-start.8 = (bf16[64,640]{1,0:T(8,128)(2,1)S(1)}, bf16[64,640]{1,0:T(8,128)(2,1)S(1)}, u32[]{:S(2)}, u32[]{:S(2)}) collective-permute-start(bf16[64,640]{1,0:T(8,128)(2,1)S(1)} %get-tuple-element.53), channel_id=1, source_target_pairs={{0,3},{1,0},{2,1},{3,2},{4,7},{5,4},{6,5},{7,6},{8,11},{9,8},{10,9... | collective-permute-start | bytes 245768 | tf_op jit(solution)/shard_map/ppermute | solution.py:371
  60.8 6.8 %collective-permute-start.13 = (bf16[64,512]{1,0:T(8,128)(2,1)S(1)}, bf16[64,512]{1,0:T(8,128)(2,1)S(1)}, u32[]{:S(2)}, u32[]{:S(2)}) collective-permute-start(bf16[64,512]{1,0:T(8,128)(2,1)S(1)} %get-tuple-element.65), channel_id=1, source_target_pairs={{0,2},{1,3},{2,0},{3,1},{4,6},{5,7},{6,4},{7,5},{8,10},{9,11},{10,... | collective-permute-start | bytes 196616 | tf_op jit(solution)/shard_map/ppermute | solution.py:371
  60.8 6.8 %collective-permute-start.14 = (bf16[64,512]{1,0:T(8,128)(2,1)S(1)}, bf16[64,512]{1,0:T(8,128)(2,1)S(1)}, u32[]{:S(2)}, u32[]{:S(2)}) collective-permute-start(bf16[64,512]{1,0:T(8,128)(2,1)S(1)} %get-tuple-element.66), channel_id=1, source_target_pairs={{0,3},{1,0},{2,1},{3,2},{4,7},{5,4},{6,5},{7,6},{8,11},{9,8},{10,9... | collective-permute-start | bytes 196616 | tf_op jit(solution)/shard_map/ppermute | solution.py:371

commit v4 on v3

--- a/solution.py
+++ b/solution.py
@@ -66,12 +66,9 @@
         self.seg = self.rows * self.n
         bits = (lax.axis_size("ctx") - 1).bit_length()
         self.steps = [(at, 1) for at in range(bits)]
-        first = -(-self.local // PARTS)
-        self.parts = []
-        at = 0
-        while at < self.local:
-            self.parts.append((at, min(first, self.local - at)))
-            at += first
+        first = max(1, self.local // PARTS)
+        self.parts = [(at, min(first, self.local - at)) for at in range(0, first * PARTS, first) if at < self.local]
+        self.parts[-1] = (self.parts[-1][0], self.local - self.parts[-1][0])
 
 
 def project(z, names, part, lengths, low_rank, bases, edit_up, columns, log_decay, decays, after=(), whole=False, places=None):
@@ -217,17 +214,11 @@
     return lax.rem(lax.axis_index("ctx") // (1 << shift), 1 << width)
 
 
-def exchange(step, last, send):
+def exchange(step, send):
     shift, width = step
-    size, mask = lax.axis_size("ctx"), (1 << width) - 1
-
-    def needed(source, m):
-        mine = (source >> shift) & mask
-        return not last or mine < mine ^ m
-
+    size = lax.axis_size("ctx")
     return [
-        lax.ppermute(send, "ctx", [(i, i ^ (m << shift)) for i in range(size) if needed(i, m)])
-        for m in range(1, mask + 1)
+        lax.ppermute(send, "ctx", [(i, i ^ (m << shift)) for i in range(size)]) for m in range(1, 1 << width)
     ]
 
 
@@ -340,15 +331,27 @@
     return call(kernel, [((rows, count * dh), BF16)] * n, args, scratch=scratch)
 
 
+def squares(z, blocks):
+    def kernel(*refs):
+        total = jnp.zeros((z.rows, 1), F32)
+        for ref in refs[:-1]:
+            flat = ref[...].astype(F32)
+            total = total + jnp.sum(flat * flat, axis=1, keepdims=True)
+        refs[-1][...] = jnp.broadcast_to(total, (z.rows, LANES))
+
+    return call(kernel, [((z.rows, LANES), F32)], blocks)[0]
+
+
 def normalize(z, lengths, gain, blocks):
     n, rows, dh = z.n, z.rows, z.dh
-
-    def kernel(len_ref, gain_ref, *refs):
+    early = squares(z, [block for part in blocks[:-1] for block in part])
+
+    def kernel(len_ref, gain_ref, early_ref, *refs):
         out = refs[-1]
         me = lax.axis_index("inner")
         live = live_mask(len_ref, rows)
-        total = jnp.zeros((rows, 1), F32)
-        for ref in refs[:-1]:
+        total = early_ref[:, :1]
+        for ref in refs[-1 - n : -1]:
             flat = ref[...].astype(F32)
             total = total + jnp.sum(flat * flat, axis=1, keepdims=True)
         inv = lax.rsqrt(total / z.width + 1e-06)
@@ -359,8 +362,7 @@
                 scaled = refs[p * n + k][...].astype(F32) * inv * gain_ref[:, cols]
                 out[:, cols] = jnp.where(live, scaled, 0.0).astype(BF16)
 
-    flat_blocks = [block for part in blocks for block in part]
-    args = [lengths, gain, *flat_blocks]
+    args = [lengths, gain, early, *(block for part in blocks for block in part)]
     specs = [SMEM] + [pl.BlockSpec(memory_space=pltpu.VMEM)] * (len(args) - 1)
     return call(kernel, [((rows, z.width), BF16)], args, specs)[0]
 
@@ -386,7 +388,7 @@
             kv[k] = block
     kv = shift_blocks(z, kv)
     qs = project(z, "q", every, lengths, low_rank, (q_base,), edit_up, (0,), log_decay, False, whole=True)
-    qs = gate(qs, (kv[2],))
+    qs = gate(qs, (kv[first],))
     qs = [lax.all_to_all(qs[0], "inner", split_axis=0, concat_axis=0, tiled=True)]
     outs = []
     decays = None
@@ -396,10 +398,10 @@
         carried, sums = None, decays[1]
         for step in z.steps[:-1]:
             final = step is z.steps[-2]
-            got = exchange(step, False, send)
+            got = exchange(step, send)
             *total, carried, send, sums = join(z, step, part, total, got, sums, carried, final)
             total = total[0] if total else None
-        got = exchange(z.steps[-1], True, send)
+        got = exchange(z.steps[-1], send)
         outs.append(shift_blocks(z, attend(z, part, kv, qs, *decays, carried, got, sums)))
     return normalize(z, lengths, norm_gain[None, :], outs)
 

time: 69.2 us -> 65.3 us (0.944)
  starting transfers between devices: 34.5 us -> 31.4 us
  waiting for transfers between devices: 22.8 us -> 22 us
    ppermute x6, starting transfers between devices: 9.29 us -> 7.1 us  [exchange(): lax.ppermute(send, 'ctx', [(i, i ^ m << shift) for i in range(size)])]
    ppermute x9, waiting for transfers between devices: 17.6 us -> 16.3 us  [shift_blocks(): lax.ppermute(blocks[k], 'inner', [(i, (i + k) % n) for i in range(n)])]
    ppermute x9, starting transfers between devices: 21.8 us -> 20.8 us  [shift_blocks(): lax.ppermute(blocks[k], 'inner', [(i, (i + k) % n) for i in range(n)])]
    pallas_call x12 -> x13, Pallas kernels: 10.6 us -> 10.8 us  [call(): pl.pallas_call(kernel, out_shape=[jax.ShapeDtypeStruct(*shape) for shape...]
  transfers between devices with their start and end apart: 16 -> 16, of which waited for: 4 -> 8; matrix products, arithmetic and copies ran while one was open for 0% -> 0% of each run, Pallas kernels for 12% -> 12%
where the time goes in v4:
time: 65.3 us; the launch traced here: 65 us
  starting transfers between devices  31.4 us (48%)
  waiting for transfers between devices  22 us (34%)
  Pallas kernels  10.8 us (17%)
  between operations  0.79 us (1%)
    ppermute x9, starting transfers between devices, shift_blocks(): lax.ppermute(blocks[k], 'inner', [(i, (i + k) % n) for i in range(n)])  20.8 us
    ppermute x9, waiting for transfers between devices, shift_blocks(): lax.ppermute(blocks[k], 'inner', [(i, (i + k) % n) for i in range(n)])  16.3 us
    pallas_call x13, Pallas kernels, call(): pl.pallas_call(kernel, out_shape=[jax.ShapeDtypeStruct(*shape) for shape...  10.8 us
    ppermute x6, starting transfers between devices, exchange(): lax.ppermute(send, 'ctx', [(i, i ^ m << shift) for i in range(size)])  7.1 us
    ppermute x6, waiting for transfers between devices, exchange(): lax.ppermute(send, 'ctx', [(i, i ^ m << shift) for i in range(size)])  5.1 us
    all_to_all x1, starting transfers between devices, shards(): lax.all_to_all(qs[0], 'inner', split_axis=0, concat_axis=0, tiled=True)  3.48 us
  transfers between devices with their start and end apart: 16, of which 8 were waited for; matrix products, arithmetic and copies ran while one was open for 0% of the time, Pallas kernels for 12%

profile of v4, /device:TPU:0, one launch (start us, length us, event | category | flops | bytes accessed | tf_op | source)
XLA Modules:
  0.0 65.0 jit_solution(10561833384056431079)
XLA Ops:
  0.7 1.5 %shard_map.83 = bf16[1168,128]{1,0:T(8,128)(2,1)S(1)} custom-call(s32[1]{0:T(128)S(6)} %copy.11.len_ref, bf16[32,64]{1,0:T(8,128)(2,1)} %bitcast.5, bf16[64,4608]{1,0:T(8,128)(2,1)} %refs_0_.4, bf16[64,4608]{1,0:T(8,128)(2,1)} %refs_1_.4, bf16[32,13824]{1,0:T(8,128)(2,1)} %refs_1_.5, bf16[36,64]{1,0:T(8,128)(2,1)} %bitcast.2), custom_call_target="tpu_custom_call" | custom-call | flops 1000000000 | bytes 1 | tf_op jit(solution)/shard_map/pallas_call | solution.py:31
  2.1 4.1 %collective-permute-start.1 = (bf16[1168,128]{1,0:T(8,128)(2,1)S(1)}, bf16[1168,128]{1,0:T(8,128)(2,1)S(1)}, u32[]{:S(2)}, u32[]{:S(2)}) collective-permute-start(bf16[1168,128]{1,0:T(8,128)(2,1)S(1)} %shard_map.83), channel_id=1, source_target_pairs={{0,2},{1,3},{2,0},{3,1},{4,6},{5,7},{6,4},{7,5},{8,10},{9,11},{10,... | collective-permute-start | bytes 897032 | tf_op jit(solution)/shard_map/ppermute | solution.py:373
  6.2 1.9 %shard_map.82 = (bf16[1168,128]{1,0:T(8,128)(2,1)S(1)}, bf16[1168,128]{1,0:T(8,128)(2,1)S(1)}, bf16[1168,128]{1,0:T(8,128)(2,1)S(1)}) custom-call(s32[1]{0:T(128)S(6)} %copy.11.len_ref, bf16[32,64]{1,0:T(8,128)(2,1)} %bitcast.6, bf16[64,4608]{1,0:T(8,128)(2,1)} %refs_0_.4, bf16[64,4608]{1,0:T(8,128)(2,1)} %refs_1_.4, bf16[32,13824]{1,0:T(8,128)(2,1)} %refs_1_.5, ...), custom_call_target="tpu_custom_call" | custom-call | flops 1000000000 | bytes 1 | tf_op jit(solution)/shard_map/pallas_call | solution.py:31
  8.2 1.6 %collective-permute-start = (bf16[1168,128]{1,0:T(8,128)(2,1)S(1)}, bf16[1168,128]{1,0:T(8,128)(2,1)S(1)}, u32[]{:S(2)}, u32[]{:S(2)}) collective-permute-start(bf16[1168,128]{1,0:T(8,128)(2,1)S(1)} %get-tuple-element.37), channel_id=1, source_target_pairs={{0,1},{1,2},{2,3},{3,0},{4,5},{5,6},{6,7},{7,4},{8,9},{9,10},{10,1... | collective-permute-start | bytes 897032 | tf_op jit(solution)/shard_map/ppermute | solution.py:373
  9.8 2.2 %collective-permute-start.2 = (bf16[1168,128]{1,0:T(8,128)(2,1)S(1)}, bf16[1168,128]{1,0:T(8,128)(2,1)S(1)}, u32[]{:S(2)}, u32[]{:S(2)}) collective-permute-start(bf16[1168,128]{1,0:T(8,128)(2,1)S(1)} %get-tuple-element.38), channel_id=1, source_target_pairs={{0,3},{1,0},{2,1},{3,2},{4,7},{5,4},{6,5},{7,6},{8,11},{9,8},{10,9... | collective-permute-start | bytes 897032 | tf_op jit(solution)/shard_map/ppermute | solution.py:373
  12.0 2.6 %shard_map.84.refs_0_ = bf16[4,576,128]{2,1,0:T(8,128)(2,1)} custom-call(s32[1]{0:T(128)S(6)} %copy.11.len_ref, bf16[32,64]{1,0:T(8,128)(2,1)} %bitcast.7, bf16[64,4608]{1,0:T(8,128)(2,1)} %refs_0_.5, bf16[32,13824]{1,0:T(8,128)(2,1)} %refs_1_.5, bf16[36,64]{1,0:T(8,128)(2,1)} %bitcast.4), custom_call_target="tpu_custom_call" | custom-call | flops 1000000000 | bytes 1 | tf_op jit(solution)/shard_map/pallas_call | solution.py:31
  14.6 12.4 %collective-permute-done.1.refs_1_.refs_2_ = bf16[1168,128]{1,0:T(8,128)(2,1)S(1)} collective-permute-done((bf16[1168,128]{1,0:T(8,128)(2,1)S(1)}, bf16[1168,128]{1,0:T(8,128)(2,1)S(1)}, u32[]{:S(2)}, u32[]{:S(2)}) %collective-permute-start.1) | collective-permute-done | bytes 299040 | tf_op jit(solution)/shard_map/ppermute | solution.py:373
  27.0 3.5 %all-to-all-start = ((bf16[4,576,128]{2,1,0:T(8,128)(2,1)}), bf16[4,576,128]{2,1,0:T(8,128)(2,1)S(1)}, u32[]{:S(2)}, u32[]{:S(2)}) async-start(bf16[4,576,128]{2,1,0:T(8,128)(2,1)} %shard_map.85), calls=%async_computation | async-start | bytes 1179648 | tf_op jit(solution)/shard_map/all_to_all | solution.py:392
  30.5 0.7 %shard_map.86 = (f32[512,128]{1,0:T(8,128)S(1)}, bf16[544,128]{1,0:T(8,128)(2,1)S(1)}, f32[256,128]{1,0:T(8,128)S(1)}, f32[16,256]{1,0:T(8,128)S(1)}) custom-call(bf16[1168,128]{1,0:T(8,128)(2,1)S(1)} %get-tuple-element.36.refs_0_, bf16[1168,128]{1,0:T(8,128)(2,1)S(1)} %collective-permute-done.refs_1_, ...), custom_call_target="tpu_custom_call" | custom-call | flops 1000000000 | bytes 1 | tf_op jit(solution)/shard_map/pallas_call | solution.py:31
  32.8 1.9 %collective-permute-start.4 = (bf16[544,128]{1,0:T(8,128)(2,1)S(1)}, bf16[544,128]{1,0:T(8,128)(2,1)S(1)}, u32[]{:S(2)}, u32[]{:S(2)}) collective-permute-start(bf16[544,128]{1,0:T(8,128)(2,1)S(1)} %get-tuple-element.45), channel_id=1, source_target_pairs={{0,8},{4,12},{8,0},{12,4},{16,24},{20,28},{24,16},{28,20},{1,9},{5... | collective-permute-start | bytes 417800 | tf_op jit(solution)/shard_map/ppermute | solution.py:221
  34.8 0.8 %collective-permute-start.10 = (bf16[672,128]{1,0:T(8,128)(2,1)S(1)}, bf16[672,128]{1,0:T(8,128)(2,1)S(1)}, u32[]{:S(2)}, u32[]{:S(2)}) collective-permute-start(bf16[672,128]{1,0:T(8,128)(2,1)S(1)} %get-tuple-element.58), channel_id=1, source_target_pairs={{0,8},{4,12},{8,0},{12,4},{16,24},{20,28},{24,16},{28,20},{1,9},{5... | collective-permute-start | bytes 516104 | tf_op jit(solution)/shard_map/ppermute | solution.py:221
  35.6 3.8 %collective-permute-done.4.refs_2_ = bf16[544,128]{1,0:T(8,128)(2,1)S(1)} collective-permute-done((bf16[544,128]{1,0:T(8,128)(2,1)S(1)}, bf16[544,128]{1,0:T(8,128)(2,1)S(1)}, u32[]{:S(2)}, u32[]{:S(2)}) %collective-permute-start.4) | collective-permute-done | bytes 139296 | tf_op jit(solution)/shard_map/ppermute | solution.py:221
  39.5 1.9 %collective-permute-start.5 = (bf16[544,128]{1,0:T(8,128)(2,1)S(1)}, bf16[544,128]{1,0:T(8,128)(2,1)S(1)}, u32[]{:S(2)}, u32[]{:S(2)}) collective-permute-start(bf16[544,128]{1,0:T(8,128)(2,1)S(1)} %get-tuple-element.49), channel_id=1, source_target_pairs={{0,16},{4,20},{8,24},{12,28},{16,0},{20,4},{24,8},{28,12},{1,17},{... | collective-permute-start | bytes 417800 | tf_op jit(solution)/shard_map/ppermute | solution.py:221
  41.4 1.0 %collective-permute-done.10.refs_2_ = bf16[672,128]{1,0:T(8,128)(2,1)S(1)} collective-permute-done((bf16[672,128]{1,0:T(8,128)(2,1)S(1)}, bf16[672,128]{1,0:T(8,128)(2,1)S(1)}, u32[]{:S(2)}, u32[]{:S(2)}) %collective-permute-start.10) | collective-permute-done | bytes 172064 | tf_op jit(solution)/shard_map/ppermute | solution.py:221
  42.5 1.8 %collective-permute-start.11 = (bf16[672,128]{1,0:T(8,128)(2,1)S(1)}, bf16[672,128]{1,0:T(8,128)(2,1)S(1)}, u32[]{:S(2)}, u32[]{:S(2)}) collective-permute-start(bf16[672,128]{1,0:T(8,128)(2,1)S(1)} %get-tuple-element.62), channel_id=1, source_target_pairs={{0,16},{4,20},{8,24},{12,28},{16,0},{20,4},{24,8},{28,12},{1,17},{... | collective-permute-start | bytes 516104 | tf_op jit(solution)/shard_map/ppermute | solution.py:221
  45.3 0.8 %shard_map.89 = (bf16[64,512]{1,0:T(8,128)(2,1)S(1)}, bf16[64,512]{1,0:T(8,128)(2,1)S(1)}, bf16[64,512]{1,0:T(8,128)(2,1)S(1)}, bf16[64,512]{1,0:T(8,128)(2,1)S(1)}) custom-call(bf16[1168,128]{1,0:T(8,128)(2,1)S(1)} %get-tuple-element.36.refs_0_, bf16[1168,128]{1,0:T(8,128)(2,1)S(1)} %collective-permute-done.refs_1_, ...), custom_call_target="tpu_custom_call" | custom-call | flops 1000000000 | bytes 1 | tf_op jit(solution)/shard_map/pallas_call | solution.py:31
  46.0 3.8 %collective-permute-start.6 = (bf16[64,512]{1,0:T(8,128)(2,1)S(1)}, bf16[64,512]{1,0:T(8,128)(2,1)S(1)}, u32[]{:S(2)}, u32[]{:S(2)}) collective-permute-start(bf16[64,512]{1,0:T(8,128)(2,1)S(1)} %get-tuple-element.51), channel_id=1, source_target_pairs={{0,1},{1,2},{2,3},{3,0},{4,5},{5,6},{6,7},{7,4},{8,9},{9,10},{10,1... | collective-permute-start | bytes 196616 | tf_op jit(solution)/shard_map/ppermute | solution.py:373
  49.8 2.3 %collective-permute-start.7 = (bf16[64,512]{1,0:T(8,128)(2,1)S(1)}, bf16[64,512]{1,0:T(8,128)(2,1)S(1)}, u32[]{:S(2)}, u32[]{:S(2)}) collective-permute-start(bf16[64,512]{1,0:T(8,128)(2,1)S(1)} %get-tuple-element.52), channel_id=1, source_target_pairs={{0,2},{1,3},{2,0},{3,1},{4,6},{5,7},{6,4},{7,5},{8,10},{9,11},{10,... | collective-permute-start | bytes 196616 | tf_op jit(solution)/shard_map/ppermute | solution.py:373
  52.1 2.8 %collective-permute-start.8 = (bf16[64,512]{1,0:T(8,128)(2,1)S(1)}, bf16[64,512]{1,0:T(8,128)(2,1)S(1)}, u32[]{:S(2)}, u32[]{:S(2)}) collective-permute-start(bf16[64,512]{1,0:T(8,128)(2,1)S(1)} %get-tuple-element.53), channel_id=1, source_target_pairs={{0,3},{1,0},{2,1},{3,2},{4,7},{5,4},{6,5},{7,6},{8,11},{9,8},{10,9... | collective-permute-start | bytes 196616 | tf_op jit(solution)/shard_map/ppermute | solution.py:373
  55.0 0.9 %shard_map.94 = (bf16[64,640]{1,0:T(8,128)(2,1)S(1)}, bf16[64,640]{1,0:T(8,128)(2,1)S(1)}, bf16[64,640]{1,0:T(8,128)(2,1)S(1)}, bf16[64,640]{1,0:T(8,128)(2,1)S(1)}) custom-call(bf16[1168,128]{1,0:T(8,128)(2,1)S(1)} %get-tuple-element.36.refs_0_, bf16[1168,128]{1,0:T(8,128)(2,1)S(1)} %collective-permute-done.refs_1_, ...), custom_call_target="tpu_custom_call" | custom-call | flops 1000000000 | bytes 1 | tf_op jit(solution)/shard_map/pallas_call | solution.py:31
  56.5 3.3 %collective-permute-start.14 = (bf16[64,640]{1,0:T(8,128)(2,1)S(1)}, bf16[64,640]{1,0:T(8,128)(2,1)S(1)}, u32[]{:S(2)}, u32[]{:S(2)}) collective-permute-start(bf16[64,640]{1,0:T(8,128)(2,1)S(1)} %get-tuple-element.66), channel_id=1, source_target_pairs={{0,3},{1,0},{2,1},{3,2},{4,7},{5,4},{6,5},{7,6},{8,11},{9,8},{10,9... | collective-permute-start | bytes 245768 | tf_op jit(solution)/shard_map/ppermute | solution.py:373
  59.9 2.4 %collective-permute-done.12.refs_5_ = bf16[64,640]{1,0:T(8,128)(2,1)S(1)} collective-permute-done((bf16[64,640]{1,0:T(8,128)(2,1)S(1)}, bf16[64,640]{1,0:T(8,128)(2,1)S(1)}, u32[]{:S(2)}, u32[]{:S(2)}) %collective-permute-start.12) | collective-permute-done | bytes 81952 | tf_op jit(solution)/shard_map/ppermute | solution.py:373
  62.3 1.4 %collective-permute-done.13.refs_6_ = bf16[64,640]{1,0:T(8,128)(2,1)S(1)} collective-permute-done((bf16[64,640]{1,0:T(8,128)(2,1)S(1)}, bf16[64,640]{1,0:T(8,128)(2,1)S(1)}, u32[]{:S(2)}, u32[]{:S(2)}) %collective-permute-start.13) | collective-permute-done | bytes 81952 | tf_op jit(solution)/shard_map/ppermute | solution.py:373
  63.8 1.2 %shard_map.95 = bf16[64,4608]{1,0:T(8,128)(2,1)} custom-call(s32[1]{0:T(128)S(6)} %copy.11.len_ref, f32[1,4608]{1,0:T(1,128)S(1)} %broadcast_in_dim.3.gain_ref, f32[64,128]{1,0:T(8,128)S(1)} %shard_map.90.early_ref, bf16[64,512]{1,0:T(8,128)(2,1)S(1)} %get-tuple-element.50.refs_0_, bf16[64,512]{1,0:T(8,128)(2,1)S(1)} %collective-permute-done.6.refs_1_, ...), custom_call_target="tpu_custom_call" | custom-call | flops 1000000000 | bytes 1 | tf_op jit(solution)/shard_map/pallas_call | solution.py:31
  (25 shorter events, 3.5 us)
Async XLA Ops:
  2.1 24.9 %collective-permute-start.1 = (bf16[1168,128]{1,0:T(8,128)(2,1)S(1)}, bf16[1168,128]{1,0:T(8,128)(2,1)S(1)}, u32[]{:S(2)}, u32[]{:S(2)}) collective-permute-start(bf16[1168,128]{1,0:T(8,128)(2,1)S(1)} %shard_map.83), channel_id=1, source_target_pairs={{0,2},{1,3},{2,0},{3,1},{4,6},{5,7},{6,4},{7,5},{8,10},{9,11},{10,... | collective-permute-start | bytes 897032 | tf_op jit(solution)/shard_map/ppermute | solution.py:373
  8.2 22.4 %collective-permute-start = (bf16[1168,128]{1,0:T(8,128)(2,1)S(1)}, bf16[1168,128]{1,0:T(8,128)(2,1)S(1)}, u32[]{:S(2)}, u32[]{:S(2)}) collective-permute-start(bf16[1168,128]{1,0:T(8,128)(2,1)S(1)} %get-tuple-element.37), channel_id=1, source_target_pairs={{0,1},{1,2},{2,3},{3,0},{4,5},{5,6},{6,7},{7,4},{8,9},{9,10},{10,1... | collective-permute-start | bytes 897032 | tf_op jit(solution)/shard_map/ppermute | solution.py:373
  9.8 20.7 %collective-permute-start.2 = (bf16[1168,128]{1,0:T(8,128)(2,1)S(1)}, bf16[1168,128]{1,0:T(8,128)(2,1)S(1)}, u32[]{:S(2)}, u32[]{:S(2)}) collective-permute-start(bf16[1168,128]{1,0:T(8,128)(2,1)S(1)} %get-tuple-element.38), channel_id=1, source_target_pairs={{0,3},{1,0},{2,1},{3,2},{4,7},{5,4},{6,5},{7,6},{8,11},{9,8},{10,9... | collective-permute-start | bytes 897032 | tf_op jit(solution)/shard_map/ppermute | solution.py:373
  27.0 18.2 %all-to-all-start = ((bf16[4,576,128]{2,1,0:T(8,128)(2,1)}), bf16[4,576,128]{2,1,0:T(8,128)(2,1)S(1)}, u32[]{:S(2)}, u32[]{:S(2)}) async-start(bf16[4,576,128]{2,1,0:T(8,128)(2,1)} %shard_map.85), calls=%async_computation | async-start | bytes 1179648 | tf_op jit(solution)/shard_map/all_to_all | solution.py:392
  31.3 1.4 %collective-permute-start.3 = (bf16[544,128]{1,0:T(8,128)(2,1)S(1)}, bf16[544,128]{1,0:T(8,128)(2,1)S(1)}, u32[]{:S(2)}, u32[]{:S(2)}) collective-permute-start(bf16[544,128]{1,0:T(8,128)(2,1)S(1)} %get-tuple-element.42), channel_id=1, source_target_pairs={{0,4},{4,0},{8,12},{12,8},{16,20},{20,16},{24,28},{28,24},{1,5},{5... | collective-permute-start | bytes 417800 | tf_op jit(solution)/shard_map/ppermute | solution.py:221
  32.0 2.7 %collective-permute-start.9 = (bf16[672,128]{1,0:T(8,128)(2,1)S(1)}, bf16[672,128]{1,0:T(8,128)(2,1)S(1)}, u32[]{:S(2)}, u32[]{:S(2)}) collective-permute-start(bf16[672,128]{1,0:T(8,128)(2,1)S(1)} %get-tuple-element.55), channel_id=1, source_target_pairs={{0,4},{4,0},{8,12},{12,8},{16,20},{20,16},{24,28},{28,24},{1,5},{5... | collective-permute-start | bytes 516104 | tf_op jit(solution)/shard_map/ppermute | solution.py:221
  32.8 6.6 %collective-permute-start.4 = (bf16[544,128]{1,0:T(8,128)(2,1)S(1)}, bf16[544,128]{1,0:T(8,128)(2,1)S(1)}, u32[]{:S(2)}, u32[]{:S(2)}) collective-permute-start(bf16[544,128]{1,0:T(8,128)(2,1)S(1)} %get-tuple-element.45), channel_id=1, source_target_pairs={{0,8},{4,12},{8,0},{12,4},{16,24},{20,28},{24,16},{28,20},{1,9},{5... | collective-permute-start | bytes 417800 | tf_op jit(solution)/shard_map/ppermute | solution.py:221
  34.8 7.5 %collective-permute-start.10 = (bf16[672,128]{1,0:T(8,128)(2,1)S(1)}, bf16[672,128]{1,0:T(8,128)(2,1)S(1)}, u32[]{:S(2)}, u32[]{:S(2)}) collective-permute-start(bf16[672,128]{1,0:T(8,128)(2,1)S(1)} %get-tuple-element.58), channel_id=1, source_target_pairs={{0,8},{4,12},{8,0},{12,4},{16,24},{20,28},{24,16},{28,20},{1,9},{5... | collective-permute-start | bytes 516104 | tf_op jit(solution)/shard_map/ppermute | solution.py:221
  39.5 5.1 %collective-permute-start.5 = (bf16[544,128]{1,0:T(8,128)(2,1)S(1)}, bf16[544,128]{1,0:T(8,128)(2,1)S(1)}, u32[]{:S(2)}, u32[]{:S(2)}) collective-permute-start(bf16[544,128]{1,0:T(8,128)(2,1)S(1)} %get-tuple-element.49), channel_id=1, source_target_pairs={{0,16},{4,20},{8,24},{12,28},{16,0},{20,4},{24,8},{28,12},{1,17},{... | collective-permute-start | bytes 417800 | tf_op jit(solution)/shard_map/ppermute | solution.py:221
  42.4 2.0 %copy-start = (f32[4608]{0:T(1024)S(1)}, f32[4608]{0:T(1024)}, u32[]{:S(2)}) copy-start(f32[4608]{0:T(1024)} %param.15) | copy-start | bytes 55300
  42.5 12.5 %collective-permute-start.11 = (bf16[672,128]{1,0:T(8,128)(2,1)S(1)}, bf16[672,128]{1,0:T(8,128)(2,1)S(1)}, u32[]{:S(2)}, u32[]{:S(2)}) collective-permute-start(bf16[672,128]{1,0:T(8,128)(2,1)S(1)} %get-tuple-element.62), channel_id=1, source_target_pairs={{0,16},{4,20},{8,24},{12,28},{16,0},{20,4},{24,8},{28,12},{1,17},{... | collective-permute-start | bytes 516104 | tf_op jit(solution)/shard_map/ppermute | solution.py:221
  46.0 10.5 %collective-permute-start.6 = (bf16[64,512]{1,0:T(8,128)(2,1)S(1)}, bf16[64,512]{1,0:T(8,128)(2,1)S(1)}, u32[]{:S(2)}, u32[]{:S(2)}) collective-permute-start(bf16[64,512]{1,0:T(8,128)(2,1)S(1)} %get-tuple-element.51), channel_id=1, source_target_pairs={{0,1},{1,2},{2,3},{3,0},{4,5},{5,6},{6,7},{7,4},{8,9},{9,10},{10,1... | collective-permute-start | bytes 196616 | tf_op jit(solution)/shard_map/ppermute | solution.py:373
  49.8 10.0 %collective-permute-start.7 = (bf16[64,512]{1,0:T(8,128)(2,1)S(1)}, bf16[64,512]{1,0:T(8,128)(2,1)S(1)}, u32[]{:S(2)}, u32[]{:S(2)}) collective-permute-start(bf16[64,512]{1,0:T(8,128)(2,1)S(1)} %get-tuple-element.52), channel_id=1, source_target_pairs={{0,2},{1,3},{2,0},{3,1},{4,6},{5,7},{6,4},{7,5},{8,10},{9,11},{10,... | collective-permute-start | bytes 196616 | tf_op jit(solution)/shard_map/ppermute | solution.py:373
  52.1 7.6 %collective-permute-start.8 = (bf16[64,512]{1,0:T(8,128)(2,1)S(1)}, bf16[64,512]{1,0:T(8,128)(2,1)S(1)}, u32[]{:S(2)}, u32[]{:S(2)}) collective-permute-start(bf16[64,512]{1,0:T(8,128)(2,1)S(1)} %get-tuple-element.53), channel_id=1, source_target_pairs={{0,3},{1,0},{2,1},{3,2},{4,7},{5,4},{6,5},{7,6},{8,11},{9,8},{10,9... | collective-permute-start | bytes 196616 | tf_op jit(solution)/shard_map/ppermute | solution.py:373
  55.9 6.4 %collective-permute-start.12 = (bf16[64,640]{1,0:T(8,128)(2,1)S(1)}, bf16[64,640]{1,0:T(8,128)(2,1)S(1)}, u32[]{:S(2)}, u32[]{:S(2)}) collective-permute-start(bf16[64,640]{1,0:T(8,128)(2,1)S(1)} %get-tuple-element.64), channel_id=1, source_target_pairs={{0,1},{1,2},{2,3},{3,0},{4,5},{5,6},{6,7},{7,4},{8,9},{9,10},{10,1... | collective-permute-start | bytes 245768 | tf_op jit(solution)/shard_map/ppermute | solution.py:373
  55.9 7.8 %collective-permute-start.13 = (bf16[64,640]{1,0:T(8,128)(2,1)S(1)}, bf16[64,640]{1,0:T(8,128)(2,1)S(1)}, u32[]{:S(2)}, u32[]{:S(2)}) collective-permute-start(bf16[64,640]{1,0:T(8,128)(2,1)S(1)} %get-tuple-element.65), channel_id=1, source_target_pairs={{0,2},{1,3},{2,0},{3,1},{4,6},{5,7},{6,4},{7,5},{8,10},{9,11},{10,... | collective-permute-start | bytes 245768 | tf_op jit(solution)/shard_map/ppermute | solution.py:373
  56.5 7.3 %collective-permute-start.14 = (bf16[64,640]{1,0:T(8,128)(2,1)S(1)}, bf16[64,640]{1,0:T(8,128)(2,1)S(1)}, u32[]{:S(2)}, u32[]{:S(2)}) collective-permute-start(bf16[64,640]{1,0:T(8,128)(2,1)S(1)} %get-tuple-element.66), channel_id=1, source_target_pairs={{0,3},{1,0},{2,1},{3,2},{4,7},{5,4},{6,5},{7,6},{8,11},{9,8},{10,9... | collective-permute-start | bytes 245768 | tf_op jit(solution)/shard_map/ppermute | solution.py:373

commit v5 on v4

--- a/solution.py
+++ b/solution.py
@@ -9,7 +9,7 @@
 LANES = 128
 PAD = 16
 PARTS = 2
-PARAMS = pltpu.CompilerParams(vmem_limit_bytes=48 * 1024 * 1024)
+PARAMS = pltpu.CompilerParams(vmem_limit_bytes=32 * 1024 * 1024)
 COST = pl.CostEstimate(flops=1000000000, bytes_accessed=1, transcendentals=0)
 SMEM = pl.BlockSpec(memory_space=pltpu.SMEM)
 
@@ -18,7 +18,7 @@
     return lax.dot_general(a, b, ((dims[:1], dims[1:]), ((), ())), preferred_element_type=F32)
 
 
-def call(kernel, shapes, args, specs=None, scratch=(), after=()):
+def call(kernel, shapes, args, specs=None, scratch=(), after=(), out=pltpu.VMEM):
     whole = [pl.BlockSpec(memory_space=pltpu.VMEM)] * len(args) if specs is None else specs
     if after:
         inner, used = kernel, len(args)
@@ -32,7 +32,7 @@
         kernel,
         out_shape=[jax.ShapeDtypeStruct(*shape) for shape in shapes],
         in_specs=whole,
-        out_specs=[pl.BlockSpec(memory_space=pltpu.VMEM)] * len(shapes),
+        out_specs=[pl.BlockSpec(memory_space=out)] * len(shapes),
         scratch_shapes=list(scratch),
         compiler_params=PARAMS,
         cost_estimate=COST,
@@ -80,13 +80,14 @@
     height = kinds * count * rows + (PAD if decays else 0)
 
     def kernel(len_ref, lr_ref, *refs):
-        base_refs, up_ref, ld_from = refs[:kinds], refs[kinds], refs[kinds + 1]
+        base_refs, up_ref = refs[:kinds], refs[kinds]
+        ld_ref = refs[kinds + 1] if decays else None
         me = lax.axis_index("inner")
         if whole:
-            outs = [refs[-6].at[lax.rem(me + k, n)] for k in places]
+            outs = [refs[-5].at[lax.rem(me + k, n)] for k in places]
         else:
-            outs = refs[-len(places) - 5 : -5]
-        base_buf, up_buf, low_buf, ld_ref, sems = refs[-5:]
+            outs = refs[-len(places) - 4 : -4]
+        base_buf, up_buf, low_buf, sems = refs[-4:]
 
         def copies(i):
             at = (lax.rem(me + places[i], n) * z.local + h0) * dh
@@ -97,18 +98,13 @@
                 yield pltpu.make_async_copy(base_refs[kind].at[:, cols], base_buf.at[slot], sems.at[0, slot])
                 yield pltpu.make_async_copy(up_ref.at[:, up_cols], up_buf.at[slot], sems.at[1, slot])
 
-        small = [
-            pltpu.make_async_copy(lr_ref, low_buf, sems.at[0, n * kinds]),
-            pltpu.make_async_copy(ld_from, ld_ref, sems.at[1, n * kinds]),
-        ]
-        for copy in small:
-            copy.start()
+        small = pltpu.make_async_copy(lr_ref, low_buf, sems.at[0, n * kinds])
+        small.start()
         for i in range(len(places)):
             for copy in copies(i):
                 copy.start()
         live = live_mask(len_ref, rows)
-        for copy in small:
-            copy.wait()
+        small.wait()
         low = low_buf[...].T
         for i, k in enumerate(places):
             for copy in copies(i):
@@ -132,13 +128,15 @@
                 )
                 outs[i][height - PAD : height, :] = wide.astype(BF16)
 
-    args = [lengths, *(pltpu.with_memory_space_constraint(a, pltpu.HBM) for a in (low_rank, *bases, edit_up, log_decay))]
-    specs = [SMEM, *([pl.BlockSpec(memory_space=pltpu.HBM)] * (kinds + 3))]
+    args = [lengths, *(pltpu.with_memory_space_constraint(a, pltpu.HBM) for a in (low_rank, *bases, edit_up))]
+    specs = [SMEM, *([pl.BlockSpec(memory_space=pltpu.HBM)] * (kinds + 2))]
+    if decays:
+        args.append(log_decay)
+        specs.append(pl.BlockSpec(memory_space=pltpu.VMEM))
     scratch = [
         pltpu.VMEM((n * kinds, rows, count * dh), BF16),
         pltpu.VMEM((n * kinds, rank, count * dh), BF16),
         pltpu.VMEM(low_rank.shape, BF16),
-        pltpu.VMEM(log_decay.shape, BF16),
         pltpu.SemaphoreType.DMA((2, n * kinds + 1)),
     ]
     shapes = [((n, height, dh), BF16)] if whole else [((height, dh), BF16)] * len(places)
@@ -331,13 +329,17 @@
     return call(kernel, [((rows, count * dh), BF16)] * n, args, scratch=scratch)
 
 
+def lane_squares(total, refs):
+    for ref in refs:
+        for at in range(0, ref.shape[1], LANES):
+            flat = ref[:, at : at + LANES].astype(F32)
+            total = total + flat * flat
+    return total
+
+
 def squares(z, blocks):
     def kernel(*refs):
-        total = jnp.zeros((z.rows, 1), F32)
-        for ref in refs[:-1]:
-            flat = ref[...].astype(F32)
-            total = total + jnp.sum(flat * flat, axis=1, keepdims=True)
-        refs[-1][...] = jnp.broadcast_to(total, (z.rows, LANES))
+        refs[-1][...] = lane_squares(jnp.zeros((z.rows, LANES), F32), refs[:-1])
 
     return call(kernel, [((z.rows, LANES), F32)], blocks)[0]
 
@@ -347,24 +349,28 @@
     early = squares(z, [block for part in blocks[:-1] for block in part])
 
     def kernel(len_ref, gain_ref, early_ref, *refs):
-        out = refs[-1]
+        *refs, far, out, sems = refs
         me = lax.axis_index("inner")
         live = live_mask(len_ref, rows)
-        total = early_ref[:, :1]
-        for ref in refs[-1 - n : -1]:
-            flat = ref[...].astype(F32)
-            total = total + jnp.sum(flat * flat, axis=1, keepdims=True)
+        total = jnp.sum(lane_squares(early_ref[...], refs[-n:]), axis=1, keepdims=True)
         inv = lax.rsqrt(total / z.width + 1e-06)
-        for p, (h0, count) in enumerate(z.parts):
-            for k in range(n):
-                group = lax.rem(me + (n - k), n)
-                cols = pl.ds(pl.multiple_of((group * z.local + h0) * dh, LANES), count * dh)
+        copies = []
+        for k in range(n):
+            first = lax.rem(me + (n - k), n) * z.local
+            for p, (h0, count) in enumerate(z.parts):
+                cols = pl.ds(pl.multiple_of((first + h0) * dh, LANES), count * dh)
                 scaled = refs[p * n + k][...].astype(F32) * inv * gain_ref[:, cols]
                 out[:, cols] = jnp.where(live, scaled, 0.0).astype(BF16)
+            cols = pl.ds(pl.multiple_of(first * dh, LANES), z.local * dh)
+            copies.append(pltpu.make_async_copy(out.at[:, cols], far.at[:, cols], sems.at[k]))
+            copies[-1].start()
+        for copy in copies:
+            copy.wait()
 
     args = [lengths, gain, early, *(block for part in blocks for block in part)]
     specs = [SMEM] + [pl.BlockSpec(memory_space=pltpu.VMEM)] * (len(args) - 1)
-    return call(kernel, [((rows, z.width), BF16)], args, specs)[0]
+    scratch = [pltpu.VMEM((rows, z.width), BF16), pltpu.SemaphoreType.DMA((n,))]
+    return call(kernel, [((rows, z.width), BF16)], args, specs, scratch, out=pltpu.HBM)[0]
 
 
 def shift_blocks(z, blocks):

time: 65.3 us -> 65.9 us (level)
  local copies, waits for them, and re-layouts: 0.02 us -> 0.71 us
    unnamed x2 -> x4, local copies, waits for them, and re-layouts: 0.01 us -> 0.7 us
where the time goes in v5:
time: 65.9 us; the launch traced here: 65.5 us
  starting transfers between devices  31.4 us (48%)
  waiting for transfers between devices  22.1 us (34%)
  Pallas kernels  10.5 us (16%)
  between operations  0.8 us (1%)
  local copies, waits for them, and re-layouts  0.71 us (1%)
    ppermute x9, starting transfers between devices, shift_blocks(): lax.ppermute(blocks[k], 'inner', [(i, (i + k) % n) for i in range(n)])  20.8 us
    ppermute x9, waiting for transfers between devices, shift_blocks(): lax.ppermute(blocks[k], 'inner', [(i, (i + k) % n) for i in range(n)])  16.4 us
    pallas_call x13, Pallas kernels, call(): pl.pallas_call(kernel, out_shape=[jax.ShapeDtypeStruct(*shape) for shape...  10.5 us
    ppermute x6, starting transfers between devices, exchange(): lax.ppermute(send, 'ctx', [(i, i ^ m << shift) for i in range(size)])  7.1 us
    ppermute x6, waiting for transfers between devices, exchange(): lax.ppermute(send, 'ctx', [(i, i ^ m << shift) for i in range(size)])  5.1 us
    all_to_all x1, starting transfers between devices, shards(): lax.all_to_all(qs[0], 'inner', split_axis=0, concat_axis=0, tiled=True)  3.48 us
  transfers between devices with their start and end apart: 16, of which 8 were waited for; matrix products, arithmetic and copies ran while one was open for 0% of the time, Pallas kernels for 12%

profile of v5, /device:TPU:0, one launch (start us, length us, event | category | flops | bytes accessed | tf_op | source)
XLA Modules:
  0.0 65.5 jit_solution(16407165782507141360)
XLA Ops:
  1.4 1.5 %shard_map.83 = bf16[1168,128]{1,0:T(8,128)(2,1)S(1)} custom-call(s32[1]{0:T(128)S(6)} %copy.11.len_ref, bf16[32,64]{1,0:T(8,128)(2,1)} %bitcast.4, bf16[64,4608]{1,0:T(8,128)(2,1)} %refs_0_.4, bf16[64,4608]{1,0:T(8,128)(2,1)} %refs_1_.4, bf16[32,13824]{1,0:T(8,128)(2,1)} %refs_1_.5, bf16[36,64]{1,0:T(8,128)(2,1)S(1)} %bitcast.2), custom_call_target="tpu_custom_call" | custom-call | flops 1000000000 | bytes 1 | tf_op jit(solution)/shard_map/pallas_call | solution.py:31
  2.8 4.1 %collective-permute-start.1 = (bf16[1168,128]{1,0:T(8,128)(2,1)S(1)}, bf16[1168,128]{1,0:T(8,128)(2,1)S(1)}, u32[]{:S(2)}, u32[]{:S(2)}) collective-permute-start(bf16[1168,128]{1,0:T(8,128)(2,1)S(1)} %shard_map.83), channel_id=1, source_target_pairs={{0,2},{1,3},{2,0},{3,1},{4,6},{5,7},{6,4},{7,5},{8,10},{9,11},{10,... | collective-permute-start | bytes 897032 | tf_op jit(solution)/shard_map/ppermute | solution.py:379
  6.9 1.9 %shard_map.82 = (bf16[1168,128]{1,0:T(8,128)(2,1)S(1)}, bf16[1168,128]{1,0:T(8,128)(2,1)S(1)}, bf16[1168,128]{1,0:T(8,128)(2,1)S(1)}) custom-call(s32[1]{0:T(128)S(6)} %copy.11.len_ref, bf16[32,64]{1,0:T(8,128)(2,1)} %bitcast.5, bf16[64,4608]{1,0:T(8,128)(2,1)} %refs_0_.4, bf16[64,4608]{1,0:T(8,128)(2,1)} %refs_1_.4, bf16[32,13824]{1,0:T(8,128)(2,1)} %refs_1_.5, ...), custom_call_target="tpu_custom_call" | custom-call | flops 1000000000 | bytes 1 | tf_op jit(solution)/shard_map/pallas_call | solution.py:31
  8.8 1.6 %collective-permute-start = (bf16[1168,128]{1,0:T(8,128)(2,1)S(1)}, bf16[1168,128]{1,0:T(8,128)(2,1)S(1)}, u32[]{:S(2)}, u32[]{:S(2)}) collective-permute-start(bf16[1168,128]{1,0:T(8,128)(2,1)S(1)} %get-tuple-element.37), channel_id=1, source_target_pairs={{0,1},{1,2},{2,3},{3,0},{4,5},{5,6},{6,7},{7,4},{8,9},{9,10},{10,1... | collective-permute-start | bytes 897032 | tf_op jit(solution)/shard_map/ppermute | solution.py:379
  10.5 2.3 %collective-permute-start.2 = (bf16[1168,128]{1,0:T(8,128)(2,1)S(1)}, bf16[1168,128]{1,0:T(8,128)(2,1)S(1)}, u32[]{:S(2)}, u32[]{:S(2)}) collective-permute-start(bf16[1168,128]{1,0:T(8,128)(2,1)S(1)} %get-tuple-element.38), channel_id=1, source_target_pairs={{0,3},{1,0},{2,1},{3,2},{4,7},{5,4},{6,5},{7,6},{8,11},{9,8},{10,9... | collective-permute-start | bytes 897032 | tf_op jit(solution)/shard_map/ppermute | solution.py:379
  12.7 2.6 %shard_map.84.refs_0_ = bf16[4,576,128]{2,1,0:T(8,128)(2,1)} custom-call(s32[1]{0:T(128)S(6)} %copy.11.len_ref, bf16[32,64]{1,0:T(8,128)(2,1)} %bitcast.6, bf16[64,4608]{1,0:T(8,128)(2,1)} %refs_0_.5, bf16[32,13824]{1,0:T(8,128)(2,1)} %refs_1_.5), custom_call_target="tpu_custom_call" | custom-call | flops 1000000000 | bytes 1 | tf_op jit(solution)/shard_map/pallas_call | solution.py:31
  15.3 12.4 %collective-permute-done.1.refs_1_.refs_2_ = bf16[1168,128]{1,0:T(8,128)(2,1)S(1)} collective-permute-done((bf16[1168,128]{1,0:T(8,128)(2,1)S(1)}, bf16[1168,128]{1,0:T(8,128)(2,1)S(1)}, u32[]{:S(2)}, u32[]{:S(2)}) %collective-permute-start.1) | collective-permute-done | bytes 299040 | tf_op jit(solution)/shard_map/ppermute | solution.py:379
  27.7 3.5 %all-to-all-start = ((bf16[4,576,128]{2,1,0:T(8,128)(2,1)}), bf16[4,576,128]{2,1,0:T(8,128)(2,1)S(1)}, u32[]{:S(2)}, u32[]{:S(2)}) async-start(bf16[4,576,128]{2,1,0:T(8,128)(2,1)} %shard_map.85), calls=%async_computation | async-start | bytes 1179648 | tf_op jit(solution)/shard_map/all_to_all | solution.py:398
  31.2 0.7 %shard_map.86 = (f32[512,128]{1,0:T(8,128)S(1)}, bf16[544,128]{1,0:T(8,128)(2,1)S(1)}, f32[256,128]{1,0:T(8,128)S(1)}, f32[16,256]{1,0:T(8,128)S(1)}) custom-call(bf16[1168,128]{1,0:T(8,128)(2,1)S(1)} %get-tuple-element.36.refs_0_, bf16[1168,128]{1,0:T(8,128)(2,1)S(1)} %collective-permute-done.refs_1_, ...), custom_call_target="tpu_custom_call" | custom-call | flops 1000000000 | bytes 1 | tf_op jit(solution)/shard_map/pallas_call | solution.py:31
  33.5 1.9 %collective-permute-start.4 = (bf16[544,128]{1,0:T(8,128)(2,1)S(1)}, bf16[544,128]{1,0:T(8,128)(2,1)S(1)}, u32[]{:S(2)}, u32[]{:S(2)}) collective-permute-start(bf16[544,128]{1,0:T(8,128)(2,1)S(1)} %get-tuple-element.45), channel_id=1, source_target_pairs={{0,8},{4,12},{8,0},{12,4},{16,24},{20,28},{24,16},{28,20},{1,9},{5... | collective-permute-start | bytes 417800 | tf_op jit(solution)/shard_map/ppermute | solution.py:219
  35.5 0.8 %collective-permute-start.10 = (bf16[672,128]{1,0:T(8,128)(2,1)S(1)}, bf16[672,128]{1,0:T(8,128)(2,1)S(1)}, u32[]{:S(2)}, u32[]{:S(2)}) collective-permute-start(bf16[672,128]{1,0:T(8,128)(2,1)S(1)} %get-tuple-element.58), channel_id=1, source_target_pairs={{0,8},{4,12},{8,0},{12,4},{16,24},{20,28},{24,16},{28,20},{1,9},{5... | collective-permute-start | bytes 516104 | tf_op jit(solution)/shard_map/ppermute | solution.py:219
  36.3 3.8 %collective-permute-done.4.refs_2_ = bf16[544,128]{1,0:T(8,128)(2,1)S(1)} collective-permute-done((bf16[544,128]{1,0:T(8,128)(2,1)S(1)}, bf16[544,128]{1,0:T(8,128)(2,1)S(1)}, u32[]{:S(2)}, u32[]{:S(2)}) %collective-permute-start.4) | collective-permute-done | bytes 139296 | tf_op jit(solution)/shard_map/ppermute | solution.py:219
  40.2 1.9 %collective-permute-start.5 = (bf16[544,128]{1,0:T(8,128)(2,1)S(1)}, bf16[544,128]{1,0:T(8,128)(2,1)S(1)}, u32[]{:S(2)}, u32[]{:S(2)}) collective-permute-start(bf16[544,128]{1,0:T(8,128)(2,1)S(1)} %get-tuple-element.49), channel_id=1, source_target_pairs={{0,16},{4,20},{8,24},{12,28},{16,0},{20,4},{24,8},{28,12},{1,17},{... | collective-permute-start | bytes 417800 | tf_op jit(solution)/shard_map/ppermute | solution.py:219
  42.1 1.0 %collective-permute-done.10.refs_2_ = bf16[672,128]{1,0:T(8,128)(2,1)S(1)} collective-permute-done((bf16[672,128]{1,0:T(8,128)(2,1)S(1)}, bf16[672,128]{1,0:T(8,128)(2,1)S(1)}, u32[]{:S(2)}, u32[]{:S(2)}) %collective-permute-start.10) | collective-permute-done | bytes 172064 | tf_op jit(solution)/shard_map/ppermute | solution.py:219
  43.2 1.8 %collective-permute-start.11 = (bf16[672,128]{1,0:T(8,128)(2,1)S(1)}, bf16[672,128]{1,0:T(8,128)(2,1)S(1)}, u32[]{:S(2)}, u32[]{:S(2)}) collective-permute-start(bf16[672,128]{1,0:T(8,128)(2,1)S(1)} %get-tuple-element.62), channel_id=1, source_target_pairs={{0,16},{4,20},{8,24},{12,28},{16,0},{20,4},{24,8},{28,12},{1,17},{... | collective-permute-start | bytes 516104 | tf_op jit(solution)/shard_map/ppermute | solution.py:219
  46.0 0.8 %shard_map.89 = (bf16[64,512]{1,0:T(8,128)(2,1)S(1)}, bf16[64,512]{1,0:T(8,128)(2,1)S(1)}, bf16[64,512]{1,0:T(8,128)(2,1)S(1)}, bf16[64,512]{1,0:T(8,128)(2,1)S(1)}) custom-call(bf16[1168,128]{1,0:T(8,128)(2,1)S(1)} %get-tuple-element.36.refs_0_, bf16[1168,128]{1,0:T(8,128)(2,1)S(1)} %collective-permute-done.refs_1_, ...), custom_call_target="tpu_custom_call" | custom-call | flops 1000000000 | bytes 1 | tf_op jit(solution)/shard_map/pallas_call | solution.py:31
  46.7 3.8 %collective-permute-start.6 = (bf16[64,512]{1,0:T(8,128)(2,1)S(1)}, bf16[64,512]{1,0:T(8,128)(2,1)S(1)}, u32[]{:S(2)}, u32[]{:S(2)}) collective-permute-start(bf16[64,512]{1,0:T(8,128)(2,1)S(1)} %get-tuple-element.51), channel_id=1, source_target_pairs={{0,1},{1,2},{2,3},{3,0},{4,5},{5,6},{6,7},{7,4},{8,9},{9,10},{10,1... | collective-permute-start | bytes 196616 | tf_op jit(solution)/shard_map/ppermute | solution.py:379
  50.5 2.3 %collective-permute-start.7 = (bf16[64,512]{1,0:T(8,128)(2,1)S(1)}, bf16[64,512]{1,0:T(8,128)(2,1)S(1)}, u32[]{:S(2)}, u32[]{:S(2)}) collective-permute-start(bf16[64,512]{1,0:T(8,128)(2,1)S(1)} %get-tuple-element.52), channel_id=1, source_target_pairs={{0,2},{1,3},{2,0},{3,1},{4,6},{5,7},{6,4},{7,5},{8,10},{9,11},{10,... | collective-permute-start | bytes 196616 | tf_op jit(solution)/shard_map/ppermute | solution.py:379
  52.8 2.8 %collective-permute-start.8 = (bf16[64,512]{1,0:T(8,128)(2,1)S(1)}, bf16[64,512]{1,0:T(8,128)(2,1)S(1)}, u32[]{:S(2)}, u32[]{:S(2)}) collective-permute-start(bf16[64,512]{1,0:T(8,128)(2,1)S(1)} %get-tuple-element.53), channel_id=1, source_target_pairs={{0,3},{1,0},{2,1},{3,2},{4,7},{5,4},{6,5},{7,6},{8,11},{9,8},{10,9... | collective-permute-start | bytes 196616 | tf_op jit(solution)/shard_map/ppermute | solution.py:379
  55.7 0.9 %shard_map.94 = (bf16[64,640]{1,0:T(8,128)(2,1)S(1)}, bf16[64,640]{1,0:T(8,128)(2,1)S(1)}, bf16[64,640]{1,0:T(8,128)(2,1)S(1)}, bf16[64,640]{1,0:T(8,128)(2,1)S(1)}) custom-call(bf16[1168,128]{1,0:T(8,128)(2,1)S(1)} %get-tuple-element.36.refs_0_, bf16[1168,128]{1,0:T(8,128)(2,1)S(1)} %collective-permute-done.refs_1_, ...), custom_call_target="tpu_custom_call" | custom-call | flops 1000000000 | bytes 1 | tf_op jit(solution)/shard_map/pallas_call | solution.py:31
  57.2 3.3 %collective-permute-start.14 = (bf16[64,640]{1,0:T(8,128)(2,1)S(1)}, bf16[64,640]{1,0:T(8,128)(2,1)S(1)}, u32[]{:S(2)}, u32[]{:S(2)}) collective-permute-start(bf16[64,640]{1,0:T(8,128)(2,1)S(1)} %get-tuple-element.66), channel_id=1, source_target_pairs={{0,3},{1,0},{2,1},{3,2},{4,7},{5,4},{6,5},{7,6},{8,11},{9,8},{10,9... | collective-permute-start | bytes 245768 | tf_op jit(solution)/shard_map/ppermute | solution.py:379
  60.5 2.5 %collective-permute-done.12.refs_5_ = bf16[64,640]{1,0:T(8,128)(2,1)S(1)} collective-permute-done((bf16[64,640]{1,0:T(8,128)(2,1)S(1)}, bf16[64,640]{1,0:T(8,128)(2,1)S(1)}, u32[]{:S(2)}, u32[]{:S(2)}) %collective-permute-start.12) | collective-permute-done | bytes 81952 | tf_op jit(solution)/shard_map/ppermute | solution.py:379
  63.0 1.4 %collective-permute-done.13.refs_6_ = bf16[64,640]{1,0:T(8,128)(2,1)S(1)} collective-permute-done((bf16[64,640]{1,0:T(8,128)(2,1)S(1)}, bf16[64,640]{1,0:T(8,128)(2,1)S(1)}, u32[]{:S(2)}, u32[]{:S(2)}) %collective-permute-start.13) | collective-permute-done | bytes 81952 | tf_op jit(solution)/shard_map/ppermute | solution.py:379
  64.4 1.0 %shard_map.95 = bf16[64,4608]{1,0:T(8,128)(2,1)} custom-call(s32[1]{0:T(128)S(6)} %copy.11.len_ref, f32[1,4608]{1,0:T(1,128)S(1)} %broadcast_in_dim.3.gain_ref, f32[64,128]{1,0:T(8,128)S(1)} %shard_map.90.early_ref, bf16[64,512]{1,0:T(8,128)(2,1)S(1)} %get-tuple-element.50.refs_0_, bf16[64,512]{1,0:T(8,128)(2,1)S(1)} %collective-permute-done.6.refs_1_, ...), custom_call_target="tpu_custom_call" | custom-call | flops 1000000000 | bytes 1 | tf_op jit(solution)/shard_map/pallas_call | solution.py:31
  (27 shorter events, 4.2 us)
Async XLA Ops:
  0.7 0.7 %copy-start = (bf16[64,36]{0,1:T(8,128)(2,1)S(1)}, bf16[64,36]{0,1:T(8,128)(2,1)}, u32[]{:S(2)}) copy-start(bf16[64,36]{0,1:T(8,128)(2,1)} %param.13) | copy-start | bytes 13828
  2.8 24.9 %collective-permute-start.1 = (bf16[1168,128]{1,0:T(8,128)(2,1)S(1)}, bf16[1168,128]{1,0:T(8,128)(2,1)S(1)}, u32[]{:S(2)}, u32[]{:S(2)}) collective-permute-start(bf16[1168,128]{1,0:T(8,128)(2,1)S(1)} %shard_map.83), channel_id=1, source_target_pairs={{0,2},{1,3},{2,0},{3,1},{4,6},{5,7},{6,4},{7,5},{8,10},{9,11},{10,... | collective-permute-start | bytes 897032 | tf_op jit(solution)/shard_map/ppermute | solution.py:379
  8.8 22.4 %collective-permute-start = (bf16[1168,128]{1,0:T(8,128)(2,1)S(1)}, bf16[1168,128]{1,0:T(8,128)(2,1)S(1)}, u32[]{:S(2)}, u32[]{:S(2)}) collective-permute-start(bf16[1168,128]{1,0:T(8,128)(2,1)S(1)} %get-tuple-element.37), channel_id=1, source_target_pairs={{0,1},{1,2},{2,3},{3,0},{4,5},{5,6},{6,7},{7,4},{8,9},{9,10},{10,1... | collective-permute-start | bytes 897032 | tf_op jit(solution)/shard_map/ppermute | solution.py:379
  10.5 20.7 %collective-permute-start.2 = (bf16[1168,128]{1,0:T(8,128)(2,1)S(1)}, bf16[1168,128]{1,0:T(8,128)(2,1)S(1)}, u32[]{:S(2)}, u32[]{:S(2)}) collective-permute-start(bf16[1168,128]{1,0:T(8,128)(2,1)S(1)} %get-tuple-element.38), channel_id=1, source_target_pairs={{0,3},{1,0},{2,1},{3,2},{4,7},{5,4},{6,5},{7,6},{8,11},{9,8},{10,9... | collective-permute-start | bytes 897032 | tf_op jit(solution)/shard_map/ppermute | solution.py:379
  27.7 18.2 %all-to-all-start = ((bf16[4,576,128]{2,1,0:T(8,128)(2,1)}), bf16[4,576,128]{2,1,0:T(8,128)(2,1)S(1)}, u32[]{:S(2)}, u32[]{:S(2)}) async-start(bf16[4,576,128]{2,1,0:T(8,128)(2,1)} %shard_map.85), calls=%async_computation | async-start | bytes 1179648 | tf_op jit(solution)/shard_map/all_to_all | solution.py:398
  32.0 1.4 %collective-permute-start.3 = (bf16[544,128]{1,0:T(8,128)(2,1)S(1)}, bf16[544,128]{1,0:T(8,128)(2,1)S(1)}, u32[]{:S(2)}, u32[]{:S(2)}) collective-permute-start(bf16[544,128]{1,0:T(8,128)(2,1)S(1)} %get-tuple-element.42), channel_id=1, source_target_pairs={{0,4},{4,0},{8,12},{12,8},{16,20},{20,16},{24,28},{28,24},{1,5},{5... | collective-permute-start | bytes 417800 | tf_op jit(solution)/shard_map/ppermute | solution.py:219
  32.7 2.7 %collective-permute-start.9 = (bf16[672,128]{1,0:T(8,128)(2,1)S(1)}, bf16[672,128]{1,0:T(8,128)(2,1)S(1)}, u32[]{:S(2)}, u32[]{:S(2)}) collective-permute-start(bf16[672,128]{1,0:T(8,128)(2,1)S(1)} %get-tuple-element.55), channel_id=1, source_target_pairs={{0,4},{4,0},{8,12},{12,8},{16,20},{20,16},{24,28},{28,24},{1,5},{5... | collective-permute-start | bytes 516104 | tf_op jit(solution)/shard_map/ppermute | solution.py:219
  33.5 6.6 %collective-permute-start.4 = (bf16[544,128]{1,0:T(8,128)(2,1)S(1)}, bf16[544,128]{1,0:T(8,128)(2,1)S(1)}, u32[]{:S(2)}, u32[]{:S(2)}) collective-permute-start(bf16[544,128]{1,0:T(8,128)(2,1)S(1)} %get-tuple-element.45), channel_id=1, source_target_pairs={{0,8},{4,12},{8,0},{12,4},{16,24},{20,28},{24,16},{28,20},{1,9},{5... | collective-permute-start | bytes 417800 | tf_op jit(solution)/shard_map/ppermute | solution.py:219
  35.5 7.5 %collective-permute-start.10 = (bf16[672,128]{1,0:T(8,128)(2,1)S(1)}, bf16[672,128]{1,0:T(8,128)(2,1)S(1)}, u32[]{:S(2)}, u32[]{:S(2)}) collective-permute-start(bf16[672,128]{1,0:T(8,128)(2,1)S(1)} %get-tuple-element.58), channel_id=1, source_target_pairs={{0,8},{4,12},{8,0},{12,4},{16,24},{20,28},{24,16},{28,20},{1,9},{5... | collective-permute-start | bytes 516104 | tf_op jit(solution)/shard_map/ppermute | solution.py:219
  40.2 5.1 %collective-permute-start.5 = (bf16[544,128]{1,0:T(8,128)(2,1)S(1)}, bf16[544,128]{1,0:T(8,128)(2,1)S(1)}, u32[]{:S(2)}, u32[]{:S(2)}) collective-permute-start(bf16[544,128]{1,0:T(8,128)(2,1)S(1)} %get-tuple-element.49), channel_id=1, source_target_pairs={{0,16},{4,20},{8,24},{12,28},{16,0},{20,4},{24,8},{28,12},{1,17},{... | collective-permute-start | bytes 417800 | tf_op jit(solution)/shard_map/ppermute | solution.py:219
  43.1 2.0 %copy-start.1 = (f32[4608]{0:T(1024)S(1)}, f32[4608]{0:T(1024)}, u32[]{:S(2)}) copy-start(f32[4608]{0:T(1024)} %param.15) | copy-start | bytes 55300
  43.2 12.5 %collective-permute-start.11 = (bf16[672,128]{1,0:T(8,128)(2,1)S(1)}, bf16[672,128]{1,0:T(8,128)(2,1)S(1)}, u32[]{:S(2)}, u32[]{:S(2)}) collective-permute-start(bf16[672,128]{1,0:T(8,128)(2,1)S(1)} %get-tuple-element.62), channel_id=1, source_target_pairs={{0,16},{4,20},{8,24},{12,28},{16,0},{20,4},{24,8},{28,12},{1,17},{... | collective-permute-start | bytes 516104 | tf_op jit(solution)/shard_map/ppermute | solution.py:219
  46.7 10.5 %collective-permute-start.6 = (bf16[64,512]{1,0:T(8,128)(2,1)S(1)}, bf16[64,512]{1,0:T(8,128)(2,1)S(1)}, u32[]{:S(2)}, u32[]{:S(2)}) collective-permute-start(bf16[64,512]{1,0:T(8,128)(2,1)S(1)} %get-tuple-element.51), channel_id=1, source_target_pairs={{0,1},{1,2},{2,3},{3,0},{4,5},{5,6},{6,7},{7,4},{8,9},{9,10},{10,1... | collective-permute-start | bytes 196616 | tf_op jit(solution)/shard_map/ppermute | solution.py:379
  50.5 10.0 %collective-permute-start.7 = (bf16[64,512]{1,0:T(8,128)(2,1)S(1)}, bf16[64,512]{1,0:T(8,128)(2,1)S(1)}, u32[]{:S(2)}, u32[]{:S(2)}) collective-permute-start(bf16[64,512]{1,0:T(8,128)(2,1)S(1)} %get-tuple-element.52), channel_id=1, source_target_pairs={{0,2},{1,3},{2,0},{3,1},{4,6},{5,7},{6,4},{7,5},{8,10},{9,11},{10,... | collective-permute-start | bytes 196616 | tf_op jit(solution)/shard_map/ppermute | solution.py:379
  52.8 7.6 %collective-permute-start.8 = (bf16[64,512]{1,0:T(8,128)(2,1)S(1)}, bf16[64,512]{1,0:T(8,128)(2,1)S(1)}, u32[]{:S(2)}, u32[]{:S(2)}) collective-permute-start(bf16[64,512]{1,0:T(8,128)(2,1)S(1)} %get-tuple-element.53), channel_id=1, source_target_pairs={{0,3},{1,0},{2,1},{3,2},{4,7},{5,4},{6,5},{7,6},{8,11},{9,8},{10,9... | collective-permute-start | bytes 196616 | tf_op jit(solution)/shard_map/ppermute | solution.py:379
  56.6 6.4 %collective-permute-start.12 = (bf16[64,640]{1,0:T(8,128)(2,1)S(1)}, bf16[64,640]{1,0:T(8,128)(2,1)S(1)}, u32[]{:S(2)}, u32[]{:S(2)}) collective-permute-start(bf16[64,640]{1,0:T(8,128)(2,1)S(1)} %get-tuple-element.64), channel_id=1, source_target_pairs={{0,1},{1,2},{2,3},{3,0},{4,5},{5,6},{6,7},{7,4},{8,9},{9,10},{10,1... | collective-permute-start | bytes 245768 | tf_op jit(solution)/shard_map/ppermute | solution.py:379
  56.6 7.8 %collective-permute-start.13 = (bf16[64,640]{1,0:T(8,128)(2,1)S(1)}, bf16[64,640]{1,0:T(8,128)(2,1)S(1)}, u32[]{:S(2)}, u32[]{:S(2)}) collective-permute-start(bf16[64,640]{1,0:T(8,128)(2,1)S(1)} %get-tuple-element.65), channel_id=1, source_target_pairs={{0,2},{1,3},{2,0},{3,1},{4,6},{5,7},{6,4},{7,5},{8,10},{9,11},{10,... | collective-permute-start | bytes 245768 | tf_op jit(solution)/shard_map/ppermute | solution.py:379
  57.2 7.3 %collective-permute-start.14 = (bf16[64,640]{1,0:T(8,128)(2,1)S(1)}, bf16[64,640]{1,0:T(8,128)(2,1)S(1)}, u32[]{:S(2)}, u32[]{:S(2)}) collective-permute-start(bf16[64,640]{1,0:T(8,128)(2,1)S(1)} %get-tuple-element.66), channel_id=1, source_target_pairs={{0,3},{1,0},{2,1},{3,2},{4,7},{5,4},{6,5},{7,6},{8,11},{9,8},{10,9... | collective-permute-start | bytes 245768 | tf_op jit(solution)/shard_map/ppermute | solution.py:379

commit v6 on v5

--- a/solution.py
+++ b/solution.py
@@ -182,9 +182,11 @@
         scatter_heads(z, kv_refs, vs, z.local + h0, count)
         col = col_ref[...]
         scale = jnp.exp(col[seg - 1 : seg, :] - col)
-        for h in range(count):
-            scaled = (ks[h].astype(F32) * scale[:, h0 + h : h0 + h + 1]).astype(BF16)
-            value = dot(scaled, vs[h], (0, 0))
+        scaled = [
+            (ks[h].astype(F32) * scale[:, h0 + h : h0 + h + 1]).astype(BF16) for h in range(count)
+        ]
+        values = [dot(scaled[h], vs[h], (0, 0)) for h in range(count)]
+        for h, value in enumerate(values):
             state[h * dh : (h + 1) * dh, :] = value
             send[h * dh : (h + 1) * dh, :] = value.astype(BF16)
         put_sums(send, count * dh, jnp.broadcast_to(row_ref[:, seg - 1 : seg], (PAD, LANES)))
@@ -307,18 +309,22 @@
         t = lax.broadcasted_iota(jnp.int32, (seg, seg), 0)
         s = lax.broadcasted_iota(jnp.int32, (seg, seg), 1)
         causal = s <= t
+        scores = [dot(qs[h], ks[h], (1, 1)) for h in range(count)]
+        inter = []
         for h in range(count):
             at = slice(h * dh, (h + 1) * dh)
             former = carried_ref[at, :]
             for ref, weight in zip(got_refs, before):
                 former = former + ref[at, :].astype(F32) * weight[h0 + h : h0 + h + 1, :]
-            q = qs[h]
-            d_col = col_ref[:, h0 + h : h0 + h + 1]
-            scores = dot(q, ks[h], (1, 1))
-            gap = jnp.where(causal, d_col - row_ref[h0 + h : h0 + h + 1, :], 0.0)
-            weights = jnp.where(causal, scores * jnp.exp(gap), 0.0).astype(BF16)
-            out = dot(weights, vs[h], (1, 0)) + jnp.exp(d_col) * dot(q, former.astype(BF16), (1, 0))
-            mixed[:, at] = out.astype(BF16)
+            inter.append(dot(qs[h], former.astype(BF16), (1, 0)))
+        weights = []
+        for h in range(count):
+            gap = jnp.where(causal, col_ref[:, h0 + h : h0 + h + 1] - row_ref[h0 + h : h0 + h + 1, :], 0.0)
+            weights.append(jnp.where(causal, scores[h] * jnp.exp(gap), 0.0).astype(BF16))
+        totals = [dot(weights[h], vs[h], (1, 0)) for h in range(count)]
+        for h in range(count):
+            out = totals[h] + jnp.exp(col_ref[:, h0 + h : h0 + h + 1]) * inter[h]
+            mixed[:, h * dh : (h + 1) * dh] = out.astype(BF16)
         me = lax.axis_index("inner")
         for k in range(n):
             chunk = lax.rem(me + k, n)

time: 65.9 us -> 65.6 us (level)
  no operation moved by 1% of the time
where the time goes in v6:
time: 65.6 us; the launch traced here: 65.2 us
  starting transfers between devices  31.3 us (48%)
  waiting for transfers between devices  22.3 us (34%)
  Pallas kernels  10.1 us (15%)
  between operations  0.8 us (1%)
  local copies, waits for them, and re-layouts  0.71 us (1%)
    ppermute x9, starting transfers between devices, shift_blocks(): lax.ppermute(blocks[k], 'inner', [(i, (i + k) % n) for i in range(n)])  20.8 us
    ppermute x9, waiting for transfers between devices, shift_blocks(): lax.ppermute(blocks[k], 'inner', [(i, (i + k) % n) for i in range(n)])  16.4 us
    pallas_call x13, Pallas kernels, call(): pl.pallas_call(kernel, out_shape=[jax.ShapeDtypeStruct(*shape) for shape...  10.1 us
    ppermute x6, starting transfers between devices, exchange(): lax.ppermute(send, 'ctx', [(i, i ^ m << shift) for i in range(size)])  7.02 us
    ppermute x6, waiting for transfers between devices, exchange(): lax.ppermute(send, 'ctx', [(i, i ^ m << shift) for i in range(size)])  5.26 us
    all_to_all x1, starting transfers between devices, shards(): lax.all_to_all(qs[0], 'inner', split_axis=0, concat_axis=0, tiled=True)  3.48 us
  transfers between devices with their start and end apart: 16, of which 8 were waited for; matrix products, arithmetic and copies ran while one was open for 0% of the time, Pallas kernels for 12%

profile of v6, /device:TPU:0, one launch (start us, length us, event | category | flops | bytes accessed | tf_op | source)
XLA Modules:
  0.0 65.2 jit_solution(14716475281411188124)
XLA Ops:
  0.7 0.7 %copy-done = bf16[64,36]{0,1:T(8,128)(2,1)S(1)} copy-done((bf16[64,36]{0,1:T(8,128)(2,1)S(1)}, bf16[64,36]{0,1:T(8,128)(2,1)}, u32[]{:S(2)}) %copy-start) | copy-done | bytes 4632
  1.4 1.5 %shard_map.83 = bf16[1168,128]{1,0:T(8,128)(2,1)S(1)} custom-call(s32[1]{0:T(128)S(6)} %copy.11.len_ref, bf16[32,64]{1,0:T(8,128)(2,1)} %bitcast.4, bf16[64,4608]{1,0:T(8,128)(2,1)} %refs_0_.4, bf16[64,4608]{1,0:T(8,128)(2,1)} %refs_1_.4, bf16[32,13824]{1,0:T(8,128)(2,1)} %refs_1_.5, bf16[36,64]{1,0:T(8,128)(2,1)S(1)} %bitcast.2), custom_call_target="tpu_custom_call" | custom-call | flops 1000000000 | bytes 1 | tf_op jit(solution)/shard_map/pallas_call | solution.py:31
  2.8 4.1 %collective-permute-start.1 = (bf16[1168,128]{1,0:T(8,128)(2,1)S(1)}, bf16[1168,128]{1,0:T(8,128)(2,1)S(1)}, u32[]{:S(2)}, u32[]{:S(2)}) collective-permute-start(bf16[1168,128]{1,0:T(8,128)(2,1)S(1)} %shard_map.83), channel_id=1, source_target_pairs={{0,2},{1,3},{2,0},{3,1},{4,6},{5,7},{6,4},{7,5},{8,10},{9,11},{10,... | collective-permute-start | bytes 897032 | tf_op jit(solution)/shard_map/ppermute | solution.py:385
  6.9 1.9 %shard_map.82 = (bf16[1168,128]{1,0:T(8,128)(2,1)S(1)}, bf16[1168,128]{1,0:T(8,128)(2,1)S(1)}, bf16[1168,128]{1,0:T(8,128)(2,1)S(1)}) custom-call(s32[1]{0:T(128)S(6)} %copy.11.len_ref, bf16[32,64]{1,0:T(8,128)(2,1)} %bitcast.5, bf16[64,4608]{1,0:T(8,128)(2,1)} %refs_0_.4, bf16[64,4608]{1,0:T(8,128)(2,1)} %refs_1_.4, bf16[32,13824]{1,0:T(8,128)(2,1)} %refs_1_.5, ...), custom_call_target="tpu_custom_call" | custom-call | flops 1000000000 | bytes 1 | tf_op jit(solution)/shard_map/pallas_call | solution.py:31
  8.8 1.6 %collective-permute-start = (bf16[1168,128]{1,0:T(8,128)(2,1)S(1)}, bf16[1168,128]{1,0:T(8,128)(2,1)S(1)}, u32[]{:S(2)}, u32[]{:S(2)}) collective-permute-start(bf16[1168,128]{1,0:T(8,128)(2,1)S(1)} %get-tuple-element.37), channel_id=1, source_target_pairs={{0,1},{1,2},{2,3},{3,0},{4,5},{5,6},{6,7},{7,4},{8,9},{9,10},{10,1... | collective-permute-start | bytes 897032 | tf_op jit(solution)/shard_map/ppermute | solution.py:385
  10.5 2.3 %collective-permute-start.2 = (bf16[1168,128]{1,0:T(8,128)(2,1)S(1)}, bf16[1168,128]{1,0:T(8,128)(2,1)S(1)}, u32[]{:S(2)}, u32[]{:S(2)}) collective-permute-start(bf16[1168,128]{1,0:T(8,128)(2,1)S(1)} %get-tuple-element.38), channel_id=1, source_target_pairs={{0,3},{1,0},{2,1},{3,2},{4,7},{5,4},{6,5},{7,6},{8,11},{9,8},{10,9... | collective-permute-start | bytes 897032 | tf_op jit(solution)/shard_map/ppermute | solution.py:385
  12.7 2.6 %shard_map.84.refs_0_ = bf16[4,576,128]{2,1,0:T(8,128)(2,1)} custom-call(s32[1]{0:T(128)S(6)} %copy.11.len_ref, bf16[32,64]{1,0:T(8,128)(2,1)} %bitcast.6, bf16[64,4608]{1,0:T(8,128)(2,1)} %refs_0_.5, bf16[32,13824]{1,0:T(8,128)(2,1)} %refs_1_.5), custom_call_target="tpu_custom_call" | custom-call | flops 1000000000 | bytes 1 | tf_op jit(solution)/shard_map/pallas_call | solution.py:31
  15.3 12.4 %collective-permute-done.1.refs_1_.refs_2_ = bf16[1168,128]{1,0:T(8,128)(2,1)S(1)} collective-permute-done((bf16[1168,128]{1,0:T(8,128)(2,1)S(1)}, bf16[1168,128]{1,0:T(8,128)(2,1)S(1)}, u32[]{:S(2)}, u32[]{:S(2)}) %collective-permute-start.1) | collective-permute-done | bytes 299040 | tf_op jit(solution)/shard_map/ppermute | solution.py:385
  27.7 3.5 %all-to-all-start = ((bf16[4,576,128]{2,1,0:T(8,128)(2,1)}), bf16[4,576,128]{2,1,0:T(8,128)(2,1)S(1)}, u32[]{:S(2)}, u32[]{:S(2)}) async-start(bf16[4,576,128]{2,1,0:T(8,128)(2,1)} %shard_map.85), calls=%async_computation | async-start | bytes 1179648 | tf_op jit(solution)/shard_map/all_to_all | solution.py:404
  31.2 0.7 %shard_map.86 = (f32[512,128]{1,0:T(8,128)S(1)}, bf16[544,128]{1,0:T(8,128)(2,1)S(1)}, f32[256,128]{1,0:T(8,128)S(1)}, f32[16,256]{1,0:T(8,128)S(1)}) custom-call(bf16[1168,128]{1,0:T(8,128)(2,1)S(1)} %get-tuple-element.36.refs_0_, bf16[1168,128]{1,0:T(8,128)(2,1)S(1)} %collective-permute-done.refs_1_, ...), custom_call_target="tpu_custom_call" | custom-call | flops 1000000000 | bytes 1 | tf_op jit(solution)/shard_map/pallas_call | solution.py:31
  33.5 1.9 %collective-permute-start.4 = (bf16[544,128]{1,0:T(8,128)(2,1)S(1)}, bf16[544,128]{1,0:T(8,128)(2,1)S(1)}, u32[]{:S(2)}, u32[]{:S(2)}) collective-permute-start(bf16[544,128]{1,0:T(8,128)(2,1)S(1)} %get-tuple-element.45), channel_id=1, source_target_pairs={{0,8},{4,12},{8,0},{12,4},{16,24},{20,28},{24,16},{28,20},{1,9},{5... | collective-permute-start | bytes 417800 | tf_op jit(solution)/shard_map/ppermute | solution.py:221
  35.5 0.7 %collective-permute-start.10 = (bf16[672,128]{1,0:T(8,128)(2,1)S(1)}, bf16[672,128]{1,0:T(8,128)(2,1)S(1)}, u32[]{:S(2)}, u32[]{:S(2)}) collective-permute-start(bf16[672,128]{1,0:T(8,128)(2,1)S(1)} %get-tuple-element.58), channel_id=1, source_target_pairs={{0,8},{4,12},{8,0},{12,4},{16,24},{20,28},{24,16},{28,20},{1,9},{5... | collective-permute-start | bytes 516104 | tf_op jit(solution)/shard_map/ppermute | solution.py:221
  36.2 3.8 %collective-permute-done.4.refs_2_ = bf16[544,128]{1,0:T(8,128)(2,1)S(1)} collective-permute-done((bf16[544,128]{1,0:T(8,128)(2,1)S(1)}, bf16[544,128]{1,0:T(8,128)(2,1)S(1)}, u32[]{:S(2)}, u32[]{:S(2)}) %collective-permute-start.4) | collective-permute-done | bytes 139296 | tf_op jit(solution)/shard_map/ppermute | solution.py:221
  40.1 1.9 %collective-permute-start.5 = (bf16[544,128]{1,0:T(8,128)(2,1)S(1)}, bf16[544,128]{1,0:T(8,128)(2,1)S(1)}, u32[]{:S(2)}, u32[]{:S(2)}) collective-permute-start(bf16[544,128]{1,0:T(8,128)(2,1)S(1)} %get-tuple-element.49), channel_id=1, source_target_pairs={{0,16},{4,20},{8,24},{12,28},{16,0},{20,4},{24,8},{28,12},{1,17},{... | collective-permute-start | bytes 417800 | tf_op jit(solution)/shard_map/ppermute | solution.py:221
  42.1 1.0 %collective-permute-done.10.refs_2_ = bf16[672,128]{1,0:T(8,128)(2,1)S(1)} collective-permute-done((bf16[672,128]{1,0:T(8,128)(2,1)S(1)}, bf16[672,128]{1,0:T(8,128)(2,1)S(1)}, u32[]{:S(2)}, u32[]{:S(2)}) %collective-permute-start.10) | collective-permute-done | bytes 172064 | tf_op jit(solution)/shard_map/ppermute | solution.py:221
  43.2 1.8 %collective-permute-start.11 = (bf16[672,128]{1,0:T(8,128)(2,1)S(1)}, bf16[672,128]{1,0:T(8,128)(2,1)S(1)}, u32[]{:S(2)}, u32[]{:S(2)}) collective-permute-start(bf16[672,128]{1,0:T(8,128)(2,1)S(1)} %get-tuple-element.62), channel_id=1, source_target_pairs={{0,16},{4,20},{8,24},{12,28},{16,0},{20,4},{24,8},{28,12},{1,17},{... | collective-permute-start | bytes 516104 | tf_op jit(solution)/shard_map/ppermute | solution.py:221
  46.6 3.7 %collective-permute-start.6 = (bf16[64,512]{1,0:T(8,128)(2,1)S(1)}, bf16[64,512]{1,0:T(8,128)(2,1)S(1)}, u32[]{:S(2)}, u32[]{:S(2)}) collective-permute-start(bf16[64,512]{1,0:T(8,128)(2,1)S(1)} %get-tuple-element.51), channel_id=1, source_target_pairs={{0,1},{1,2},{2,3},{3,0},{4,5},{5,6},{6,7},{7,4},{8,9},{9,10},{10,1... | collective-permute-start | bytes 196616 | tf_op jit(solution)/shard_map/ppermute | solution.py:385
  50.3 2.3 %collective-permute-start.7 = (bf16[64,512]{1,0:T(8,128)(2,1)S(1)}, bf16[64,512]{1,0:T(8,128)(2,1)S(1)}, u32[]{:S(2)}, u32[]{:S(2)}) collective-permute-start(bf16[64,512]{1,0:T(8,128)(2,1)S(1)} %get-tuple-element.52), channel_id=1, source_target_pairs={{0,2},{1,3},{2,0},{3,1},{4,6},{5,7},{6,4},{7,5},{8,10},{9,11},{10,... | collective-permute-start | bytes 196616 | tf_op jit(solution)/shard_map/ppermute | solution.py:385
  52.7 2.8 %collective-permute-start.8 = (bf16[64,512]{1,0:T(8,128)(2,1)S(1)}, bf16[64,512]{1,0:T(8,128)(2,1)S(1)}, u32[]{:S(2)}, u32[]{:S(2)}) collective-permute-start(bf16[64,512]{1,0:T(8,128)(2,1)S(1)} %get-tuple-element.53), channel_id=1, source_target_pairs={{0,3},{1,0},{2,1},{3,2},{4,7},{5,4},{6,5},{7,6},{8,11},{9,8},{10,9... | collective-permute-start | bytes 196616 | tf_op jit(solution)/shard_map/ppermute | solution.py:385
  55.5 0.8 %shard_map.94 = (bf16[64,640]{1,0:T(8,128)(2,1)S(1)}, bf16[64,640]{1,0:T(8,128)(2,1)S(1)}, bf16[64,640]{1,0:T(8,128)(2,1)S(1)}, bf16[64,640]{1,0:T(8,128)(2,1)S(1)}) custom-call(bf16[1168,128]{1,0:T(8,128)(2,1)S(1)} %get-tuple-element.36.refs_0_, bf16[1168,128]{1,0:T(8,128)(2,1)S(1)} %collective-permute-done.refs_1_, ...), custom_call_target="tpu_custom_call" | custom-call | flops 1000000000 | bytes 1 | tf_op jit(solution)/shard_map/pallas_call | solution.py:31
  56.9 3.3 %collective-permute-start.14 = (bf16[64,640]{1,0:T(8,128)(2,1)S(1)}, bf16[64,640]{1,0:T(8,128)(2,1)S(1)}, u32[]{:S(2)}, u32[]{:S(2)}) collective-permute-start(bf16[64,640]{1,0:T(8,128)(2,1)S(1)} %get-tuple-element.66), channel_id=1, source_target_pairs={{0,3},{1,0},{2,1},{3,2},{4,7},{5,4},{6,5},{7,6},{8,11},{9,8},{10,9... | collective-permute-start | bytes 245768 | tf_op jit(solution)/shard_map/ppermute | solution.py:385
  60.2 2.5 %collective-permute-done.12.refs_5_ = bf16[64,640]{1,0:T(8,128)(2,1)S(1)} collective-permute-done((bf16[64,640]{1,0:T(8,128)(2,1)S(1)}, bf16[64,640]{1,0:T(8,128)(2,1)S(1)}, u32[]{:S(2)}, u32[]{:S(2)}) %collective-permute-start.12) | collective-permute-done | bytes 81952 | tf_op jit(solution)/shard_map/ppermute | solution.py:385
  62.7 1.4 %collective-permute-done.13.refs_6_ = bf16[64,640]{1,0:T(8,128)(2,1)S(1)} collective-permute-done((bf16[64,640]{1,0:T(8,128)(2,1)S(1)}, bf16[64,640]{1,0:T(8,128)(2,1)S(1)}, u32[]{:S(2)}, u32[]{:S(2)}) %collective-permute-start.13) | collective-permute-done | bytes 81952 | tf_op jit(solution)/shard_map/ppermute | solution.py:385
  64.2 1.0 %shard_map.95 = bf16[64,4608]{1,0:T(8,128)(2,1)} custom-call(s32[1]{0:T(128)S(6)} %copy.11.len_ref, f32[1,4608]{1,0:T(1,128)S(1)} %broadcast_in_dim.3.gain_ref, f32[64,128]{1,0:T(8,128)S(1)} %shard_map.90.early_ref, bf16[64,512]{1,0:T(8,128)(2,1)S(1)} %get-tuple-element.50.refs_0_, bf16[64,512]{1,0:T(8,128)(2,1)S(1)} %collective-permute-done.6.refs_1_, ...), custom_call_target="tpu_custom_call" | custom-call | flops 1000000000 | bytes 1 | tf_op jit(solution)/shard_map/pallas_call | solution.py:31
  (27 shorter events, 4.1 us)
Async XLA Ops:
  0.7 0.7 %copy-start = (bf16[64,36]{0,1:T(8,128)(2,1)S(1)}, bf16[64,36]{0,1:T(8,128)(2,1)}, u32[]{:S(2)}) copy-start(bf16[64,36]{0,1:T(8,128)(2,1)} %param.13) | copy-start | bytes 13828
  2.8 24.9 %collective-permute-start.1 = (bf16[1168,128]{1,0:T(8,128)(2,1)S(1)}, bf16[1168,128]{1,0:T(8,128)(2,1)S(1)}, u32[]{:S(2)}, u32[]{:S(2)}) collective-permute-start(bf16[1168,128]{1,0:T(8,128)(2,1)S(1)} %shard_map.83), channel_id=1, source_target_pairs={{0,2},{1,3},{2,0},{3,1},{4,6},{5,7},{6,4},{7,5},{8,10},{9,11},{10,... | collective-permute-start | bytes 897032 | tf_op jit(solution)/shard_map/ppermute | solution.py:385
  8.8 22.4 %collective-permute-start = (bf16[1168,128]{1,0:T(8,128)(2,1)S(1)}, bf16[1168,128]{1,0:T(8,128)(2,1)S(1)}, u32[]{:S(2)}, u32[]{:S(2)}) collective-permute-start(bf16[1168,128]{1,0:T(8,128)(2,1)S(1)} %get-tuple-element.37), channel_id=1, source_target_pairs={{0,1},{1,2},{2,3},{3,0},{4,5},{5,6},{6,7},{7,4},{8,9},{9,10},{10,1... | collective-permute-start | bytes 897032 | tf_op jit(solution)/shard_map/ppermute | solution.py:385
  10.5 20.7 %collective-permute-start.2 = (bf16[1168,128]{1,0:T(8,128)(2,1)S(1)}, bf16[1168,128]{1,0:T(8,128)(2,1)S(1)}, u32[]{:S(2)}, u32[]{:S(2)}) collective-permute-start(bf16[1168,128]{1,0:T(8,128)(2,1)S(1)} %get-tuple-element.38), channel_id=1, source_target_pairs={{0,3},{1,0},{2,1},{3,2},{4,7},{5,4},{6,5},{7,6},{8,11},{9,8},{10,9... | collective-permute-start | bytes 897032 | tf_op jit(solution)/shard_map/ppermute | solution.py:385
  27.7 18.2 %all-to-all-start = ((bf16[4,576,128]{2,1,0:T(8,128)(2,1)}), bf16[4,576,128]{2,1,0:T(8,128)(2,1)S(1)}, u32[]{:S(2)}, u32[]{:S(2)}) async-start(bf16[4,576,128]{2,1,0:T(8,128)(2,1)} %shard_map.85), calls=%async_computation | async-start | bytes 1179648 | tf_op jit(solution)/shard_map/all_to_all | solution.py:404
  31.9 1.4 %collective-permute-start.3 = (bf16[544,128]{1,0:T(8,128)(2,1)S(1)}, bf16[544,128]{1,0:T(8,128)(2,1)S(1)}, u32[]{:S(2)}, u32[]{:S(2)}) collective-permute-start(bf16[544,128]{1,0:T(8,128)(2,1)S(1)} %get-tuple-element.42), channel_id=1, source_target_pairs={{0,4},{4,0},{8,12},{12,8},{16,20},{20,16},{24,28},{28,24},{1,5},{5... | collective-permute-start | bytes 417800 | tf_op jit(solution)/shard_map/ppermute | solution.py:221
  32.6 2.8 %collective-permute-start.9 = (bf16[672,128]{1,0:T(8,128)(2,1)S(1)}, bf16[672,128]{1,0:T(8,128)(2,1)S(1)}, u32[]{:S(2)}, u32[]{:S(2)}) collective-permute-start(bf16[672,128]{1,0:T(8,128)(2,1)S(1)} %get-tuple-element.55), channel_id=1, source_target_pairs={{0,4},{4,0},{8,12},{12,8},{16,20},{20,16},{24,28},{28,24},{1,5},{5... | collective-permute-start | bytes 516104 | tf_op jit(solution)/shard_map/ppermute | solution.py:221
  33.5 6.6 %collective-permute-start.4 = (bf16[544,128]{1,0:T(8,128)(2,1)S(1)}, bf16[544,128]{1,0:T(8,128)(2,1)S(1)}, u32[]{:S(2)}, u32[]{:S(2)}) collective-permute-start(bf16[544,128]{1,0:T(8,128)(2,1)S(1)} %get-tuple-element.45), channel_id=1, source_target_pairs={{0,8},{4,12},{8,0},{12,4},{16,24},{20,28},{24,16},{28,20},{1,9},{5... | collective-permute-start | bytes 417800 | tf_op jit(solution)/shard_map/ppermute | solution.py:221
  35.5 7.5 %collective-permute-start.10 = (bf16[672,128]{1,0:T(8,128)(2,1)S(1)}, bf16[672,128]{1,0:T(8,128)(2,1)S(1)}, u32[]{:S(2)}, u32[]{:S(2)}) collective-permute-start(bf16[672,128]{1,0:T(8,128)(2,1)S(1)} %get-tuple-element.58), channel_id=1, source_target_pairs={{0,8},{4,12},{8,0},{12,4},{16,24},{20,28},{24,16},{28,20},{1,9},{5... | collective-permute-start | bytes 516104 | tf_op jit(solution)/shard_map/ppermute | solution.py:221
  40.1 5.1 %collective-permute-start.5 = (bf16[544,128]{1,0:T(8,128)(2,1)S(1)}, bf16[544,128]{1,0:T(8,128)(2,1)S(1)}, u32[]{:S(2)}, u32[]{:S(2)}) collective-permute-start(bf16[544,128]{1,0:T(8,128)(2,1)S(1)} %get-tuple-element.49), channel_id=1, source_target_pairs={{0,16},{4,20},{8,24},{12,28},{16,0},{20,4},{24,8},{28,12},{1,17},{... | collective-permute-start | bytes 417800 | tf_op jit(solution)/shard_map/ppermute | solution.py:221
  43.0 2.0 %copy-start.1 = (f32[4608]{0:T(1024)S(1)}, f32[4608]{0:T(1024)}, u32[]{:S(2)}) copy-start(f32[4608]{0:T(1024)} %param.15) | copy-start | bytes 55300
  43.2 12.3 %collective-permute-start.11 = (bf16[672,128]{1,0:T(8,128)(2,1)S(1)}, bf16[672,128]{1,0:T(8,128)(2,1)S(1)}, u32[]{:S(2)}, u32[]{:S(2)}) collective-permute-start(bf16[672,128]{1,0:T(8,128)(2,1)S(1)} %get-tuple-element.62), channel_id=1, source_target_pairs={{0,16},{4,20},{8,24},{12,28},{16,0},{20,4},{24,8},{28,12},{1,17},{... | collective-permute-start | bytes 516104 | tf_op jit(solution)/shard_map/ppermute | solution.py:221
  46.6 10.3 %collective-permute-start.6 = (bf16[64,512]{1,0:T(8,128)(2,1)S(1)}, bf16[64,512]{1,0:T(8,128)(2,1)S(1)}, u32[]{:S(2)}, u32[]{:S(2)}) collective-permute-start(bf16[64,512]{1,0:T(8,128)(2,1)S(1)} %get-tuple-element.51), channel_id=1, source_target_pairs={{0,1},{1,2},{2,3},{3,0},{4,5},{5,6},{6,7},{7,4},{8,9},{9,10},{10,1... | collective-permute-start | bytes 196616 | tf_op jit(solution)/shard_map/ppermute | solution.py:385
  50.3 9.8 %collective-permute-start.7 = (bf16[64,512]{1,0:T(8,128)(2,1)S(1)}, bf16[64,512]{1,0:T(8,128)(2,1)S(1)}, u32[]{:S(2)}, u32[]{:S(2)}) collective-permute-start(bf16[64,512]{1,0:T(8,128)(2,1)S(1)} %get-tuple-element.52), channel_id=1, source_target_pairs={{0,2},{1,3},{2,0},{3,1},{4,6},{5,7},{6,4},{7,5},{8,10},{9,11},{10,... | collective-permute-start | bytes 196616 | tf_op jit(solution)/shard_map/ppermute | solution.py:385
  52.7 7.5 %collective-permute-start.8 = (bf16[64,512]{1,0:T(8,128)(2,1)S(1)}, bf16[64,512]{1,0:T(8,128)(2,1)S(1)}, u32[]{:S(2)}, u32[]{:S(2)}) collective-permute-start(bf16[64,512]{1,0:T(8,128)(2,1)S(1)} %get-tuple-element.53), channel_id=1, source_target_pairs={{0,3},{1,0},{2,1},{3,2},{4,7},{5,4},{6,5},{7,6},{8,11},{9,8},{10,9... | collective-permute-start | bytes 196616 | tf_op jit(solution)/shard_map/ppermute | solution.py:385
  56.3 6.4 %collective-permute-start.12 = (bf16[64,640]{1,0:T(8,128)(2,1)S(1)}, bf16[64,640]{1,0:T(8,128)(2,1)S(1)}, u32[]{:S(2)}, u32[]{:S(2)}) collective-permute-start(bf16[64,640]{1,0:T(8,128)(2,1)S(1)} %get-tuple-element.64), channel_id=1, source_target_pairs={{0,1},{1,2},{2,3},{3,0},{4,5},{5,6},{6,7},{7,4},{8,9},{9,10},{10,1... | collective-permute-start | bytes 245768 | tf_op jit(solution)/shard_map/ppermute | solution.py:385
  56.4 7.8 %collective-permute-start.13 = (bf16[64,640]{1,0:T(8,128)(2,1)S(1)}, bf16[64,640]{1,0:T(8,128)(2,1)S(1)}, u32[]{:S(2)}, u32[]{:S(2)}) collective-permute-start(bf16[64,640]{1,0:T(8,128)(2,1)S(1)} %get-tuple-element.65), channel_id=1, source_target_pairs={{0,2},{1,3},{2,0},{3,1},{4,6},{5,7},{6,4},{7,5},{8,10},{9,11},{10,... | collective-permute-start | bytes 245768 | tf_op jit(solution)/shard_map/ppermute | solution.py:385
  56.9 7.3 %collective-permute-start.14 = (bf16[64,640]{1,0:T(8,128)(2,1)S(1)}, bf16[64,640]{1,0:T(8,128)(2,1)S(1)}, u32[]{:S(2)}, u32[]{:S(2)}) collective-permute-start(bf16[64,640]{1,0:T(8,128)(2,1)S(1)} %get-tuple-element.66), channel_id=1, source_target_pairs={{0,3},{1,0},{2,1},{3,2},{4,7},{5,4},{6,5},{7,6},{8,11},{9,8},{10,9... | collective-permute-start | bytes 245768 | tf_op jit(solution)/shard_map/ppermute | solution.py:385
